TPU v7x, 32 devices: a whole 2x2x4 slice. The times are simulated.
32 devices in a mesh: expert: 8 (over z, y), dp: 4 (over x, core).
Axes of the slice: x: 2, y: 2, z: 4, core: 2. Of those that a mesh axis runs over, the one named last changes fastest.
Arguments:
- tokens: bfloat16 [4096, 3584], P(('expert', 'dp')), may hold values from -6 to 6
- out_grad: bfloat16 [4096, 3584], P(('expert', 'dp')), may hold values from -2 to 2
- expert_ids: int32 [4096, 8], P(('expert', 'dp')), may hold values from 0 to 63, as said below
- route_weights: bfloat16 [4096, 8], P(('expert', 'dp')), may hold values from 0.099609375 to 1
- w_gate: bfloat16 [8, 3584, 1024], P('expert', None, 'dp'), may hold values from -0.09375 to 0.09375
- w_up: bfloat16 [8, 3584, 1024], P('expert', None, 'dp'), may hold values from -0.09375 to 0.09375
- w_down: bfloat16 [8, 1024, 3584], P('expert', 'dp'), may hold values from -0.1875 to 0.1875
Outputs:
- grad_tokens: bfloat16 [4096, 3584], P(('expert', 'dp'))
- grad_route: bfloat16 [4096, 8], P(('expert', 'dp'))
- grad_gate: bfloat16 [8, 3584, 1024], P('expert', None, 'dp')
- grad_upproj: bfloat16 [8, 3584, 1024], P('expert', None, 'dp')
- grad_down: bfloat16 [8, 1024, 3584], P('expert', 'dp')
Inputs may be any that keep to these rules, and one draw needn't show every extreme that they name: `expert_ids`: each token's 8 ids are distinct. Ids below 8 are the window's experts. Within the 128 tokens of one device no id below 8 appears more than 20 times.
All inputs are finite; a program needn't handle non-finite values.
Results may differ from a plain program's by a relative error of at most 0.015.
Values may be sent and summed in bfloat16 or wider, within the bound.
No kernel may reach another device: no remote copies, remote signals or barrier semaphores. Data moves between devices by JAX's collectives and lax.ppermute only.
A program may use at most 128 MiB of HBM per device.

v0:
```python
import jax
import jax.numpy as jnp
from jax import lax
from jax.sharding import PartitionSpec as P


def build_slots(expert_ids, expert_count, capacity):
    flat_ids = expert_ids.reshape(-1)
    onehot = (flat_ids[:, None] == jnp.arange(expert_count, dtype=jnp.int32)[None, :]).astype(
        jnp.int32
    )
    ranking = jnp.sum((jnp.cumsum(onehot, axis=0) - 1) * onehot, axis=1)
    target = jnp.where(
        flat_ids < expert_count, flat_ids * capacity + ranking, expert_count * capacity
    )
    source = jnp.arange(flat_ids.shape[0], dtype=jnp.int32)
    return jnp.full((expert_count * capacity,), -1, jnp.int32).at[target].set(source, mode="drop")


def repeat_groups(values, group_count):
    lead = values.shape[0]
    widened = jnp.broadcast_to(values[:, None], (lead, group_count) + values.shape[1:])
    return widened.reshape((lead * group_count,) + values.shape[1:])


def backward_rows(x_rows, dy_rows, weight_rows, gate_w, up_w, down_w):
    gate_value = jnp.dot(x_rows, gate_w, preferred_element_type=jnp.float32)
    up_value = jnp.dot(x_rows, up_w, preferred_element_type=jnp.float32)
    sigmoid_gate = jax.nn.sigmoid(gate_value)
    hidden = (gate_value * sigmoid_gate * up_value).astype(jnp.bfloat16)
    back_proj = lax.dot_general(
        dy_rows, down_w, (((1,), (1,)), ((), ())), preferred_element_type=jnp.float32
    )
    hidden_f = hidden.astype(jnp.float32)
    route_part = jnp.sum(hidden_f * back_proj, axis=1)
    weight = weight_rows.astype(jnp.float32)[:, None]
    scaled = weight * back_proj
    d_gate = (scaled * up_value * sigmoid_gate * (1.0 + gate_value * (1.0 - sigmoid_gate))).astype(
        jnp.bfloat16
    )
    d_up = (scaled * gate_value * sigmoid_gate).astype(jnp.bfloat16)
    weighted = (weight * hidden_f).astype(jnp.bfloat16)
    contract_rows = (((0,), (0,)), ((), ()))
    grad_g = lax.dot_general(
        x_rows, d_gate, contract_rows, preferred_element_type=jnp.float32
    ).astype(jnp.bfloat16)
    grad_u = lax.dot_general(
        x_rows, d_up, contract_rows, preferred_element_type=jnp.float32
    ).astype(jnp.bfloat16)
    grad_d = lax.dot_general(
        weighted, dy_rows, contract_rows, preferred_element_type=jnp.float32
    ).astype(jnp.bfloat16)
    contract_hidden = (((1,), (1,)), ((), ()))
    partial_value = lax.dot_general(
        d_gate, gate_w, contract_hidden, preferred_element_type=jnp.float32
    )
    partial_value = partial_value + lax.dot_general(
        d_up, up_w, contract_hidden, preferred_element_type=jnp.float32
    )
    return (partial_value, route_part, grad_g, grad_u, grad_d)


def shards(tokens, out_grad, expert_ids, route_weights, w_gate, w_up, w_down):
    expert_count = lax.axis_size("expert")
    group_count = lax.axis_size("dp")
    token_rows, width = tokens.shape
    route_count = expert_ids.shape[1]
    capacity = 5 * token_rows // (4 * expert_count)
    slot_table = build_slots(expert_ids, expert_count, capacity)
    occupied = slot_table >= 0
    clamped = jnp.where(occupied, slot_table, 0)
    owner_token = clamped // route_count
    zero_row = jnp.zeros((), jnp.bfloat16)
    x_send = jnp.where(occupied[:, None], tokens[owner_token], zero_row).reshape(
        expert_count, capacity, width
    )
    dy_send = jnp.where(occupied[:, None], out_grad[owner_token], zero_row).reshape(
        expert_count, capacity, width
    )
    w_send = jnp.where(occupied, route_weights.reshape(-1)[clamped], zero_row).reshape(
        expert_count, capacity
    )
    x_all, dy_all, w_all = (
        lax.all_to_all(
            repeat_groups(x_send, group_count),
            ("expert", "dp"),
            split_axis=0,
            concat_axis=0,
            tiled=True,
        ),
        lax.all_to_all(
            repeat_groups(dy_send, group_count),
            ("expert", "dp"),
            split_axis=0,
            concat_axis=0,
            tiled=True,
        ),
        lax.all_to_all(
            repeat_groups(w_send, group_count),
            ("expert", "dp"),
            split_axis=0,
            concat_axis=0,
            tiled=True,
        ),
    )
    partial_value, route_part, grad_g, grad_u, grad_d = backward_rows(
        x_all.reshape(-1, width),
        dy_all.reshape(-1, width),
        w_all.reshape(-1),
        w_gate[0],
        w_up[0],
        w_down[0],
    )
    part_rows = partial_value.astype(jnp.bfloat16).reshape(
        expert_count * group_count, capacity, width
    )
    part_route = route_part.astype(jnp.bfloat16).reshape(expert_count * group_count, capacity)
    got_rows, got_route = (
        lax.all_to_all(part_rows, ("expert", "dp"), split_axis=0, concat_axis=0, tiled=True),
        lax.all_to_all(part_route, ("expert", "dp"), split_axis=0, concat_axis=0, tiled=True),
    )
    return_rows = jnp.sum(
        got_rows.reshape(expert_count, group_count, capacity, width).astype(jnp.float32), axis=1
    ).astype(jnp.bfloat16)
    return_route = jnp.sum(
        got_route.reshape(expert_count, group_count, capacity).astype(jnp.float32), axis=1
    ).astype(jnp.bfloat16)
    picker = (
        (owner_token[None, :] == jnp.arange(token_rows, dtype=jnp.int32)[:, None])
        & occupied[None, :]
    ).astype(jnp.bfloat16)
    grad_tokens = jnp.dot(
        picker, return_rows.reshape(-1, width), preferred_element_type=jnp.float32
    ).astype(jnp.bfloat16)
    route_match = (
        slot_table[None, :] == jnp.arange(token_rows * route_count, dtype=jnp.int32)[:, None]
    )
    route_values = return_route.reshape(-1).astype(jnp.float32)
    grad_route = jnp.sum(jnp.where(route_match, route_values[None, :], 0.0), axis=1)
    grad_route = grad_route.reshape(token_rows, route_count).astype(jnp.bfloat16)
    return (grad_tokens, grad_route, grad_g[None], grad_u[None], grad_d[None])


def solution(mesh):
    in_specs = (
        P(("expert", "dp"), None),
        P(("expert", "dp"), None),
        P(("expert", "dp"), None),
        P(("expert", "dp"), None),
        P("expert", None, "dp"),
        P("expert", None, "dp"),
        P("expert", "dp", None),
    )
    out_specs = (
        P(("expert", "dp"), None),
        P(("expert", "dp"), None),
        P("expert", None, "dp"),
        P("expert", None, "dp"),
        P("expert", "dp", None),
    )
    return jax.shard_map(shards, mesh=mesh, in_specs=in_specs, out_specs=out_specs, check_vma=False)
```

profile of v0, /device:TPU:0, one launch (start us, length us, event | category | flops | bytes accessed | tf_op | source)
XLA Modules:
  0.0 457.6 jit_solution(1207629875926636465)
XLA Ops:
  7.4 4.3 scatter_custom_fusion
  14.1 7.3 %all-to-all-start = ((bf16[32,1,20]{2,1,0:T(2,128)(2,1)}), bf16[32,1,20]{2,1,0:T(2,128)(2,1)S(1)}, u32[]{:S(2)}, u32[]{:S(2)}) async-start(bf16[32,1,20]{2,1,0:T(2,128)(2,1)} %copy.38), calls=%async_computation | async-start | bytes 32768 | tf_op jit(solution)/shard_map/all_to_all | solution.py:98
  21.5 2.3 gather_fusion.2
  23.8 2.3 gather.17
  30.6 3.1 broadcast_select_fusion.1
  35.5 128.9 %all_to_all.30 = bf16[32,20,3584]{2,1,0:T(8,128)(2,1)} all-to-all(bf16[32,20,3584]{2,1,0:T(8,128)(2,1)S(1)} %bitcast.57), channel_id=1, replica_groups=mesh['expert'=8,'dp'=4] {'expert','dp'}, dimensions={0} | all-to-all | bytes 9175040 | tf_op jit(solution)/shard_map/all_to_all | solution.py:84
  164.3 2.8 broadcast_in_dim.97
  167.1 3.6 all-to-all-start.1
  170.9 7.3 %reshape.171 = bf16[640,3584]{1,0:T(8,128)(2,1)} reshape(bf16[32,20,3584]{2,1,0:T(8,128)(2,1)} %all_to_all.30) | data formatting | bytes 9175040 | tf_op jit(solution)/shard_map/reshape | solution.py:107
  178.1 4.9 %fusion.5 = f32[640,256]{0,1:T(8,128)} fusion(bf16[640,3584]{1,0:T(8,128)(2,1)} %reshape.171, bf16[1,3584,256]{2,1,0:T(8,128)(2,1)S(1)} %copy-done), kind=kOutput, calls=%fused_computation.15 | convolution fusion | flops 1174405120 | bytes 7077888 | tf_op jit(solution)/shard_map/dot_general | solution.py:27
  183.0 2.6 fusion.8
  185.6 107.6 %all-to-all-done.1 = bf16[32,20,3584]{2,1,0:T(8,128)(2,1)} async-done(((bf16[32,20,3584]{2,1,0:T(8,128)(2,1)}), bf16[32,20,3584]{2,1,0:T(8,128)(2,1)}, u32[]{:S(2)}, u32[]{:S(2)}) %all-to-all-start.1) | async-done | bytes 4587552 | tf_op jit(solution)/shard_map/all_to_all | solution.py:91
  293.2 7.3 %reshape.169 = bf16[640,3584]{1,0:T(8,128)(2,1)} reshape(bf16[32,20,3584]{2,1,0:T(8,128)(2,1)} %all-to-all-done.1) | data formatting | bytes 9175040 | tf_op jit(solution)/shard_map/reshape | solution.py:108
  300.5 4.9 %fusion.12 = (bf16[640]{0:T(1024)(128)(2,1)S(1)}, bf16[640,256]{0,1:T(8,128)(2,1)S(1)}, bf16[640,256]{0,1:T(8,128)(2,1)S(1)}, bf16[640,256]{0,1:T(8,128)(2,1)S(1)}) fusion(f32[640,256]{0,1:T(8,128)} %fusion.8, f32[640,256]{0,1:T(8,128)} %fusion.5, f32[640]{0:T(1024)S(1)} %reshape.176, bf16[640,3584]{1,0:T(8,128)(2,1)} %reshape.169, ...), kind=kOutput, calls=%fused_computation.26 | convolution fusion | flops 1177681280 | bytes 8720128 | tf_op jit(solution)/shard_map/dot_general | solution.py:31
  306.2 3.6 all-to-all-start.4
  311.3 3.5 add_convert_fusion
  314.8 7.2 %reshape.172 = bf16[32,20,3584]{2,1,0:T(8,128)(2,1)} reshape(bf16[640,3584]{1,0:T(8,128)(2,1)} %add_convert_fusion) | data formatting | bytes 9175040 | tf_op jit(solution)/shard_map/reshape | solution.py:114
  322.1 5.8 %all-to-all-start.3 = ((bf16[32,20,3584]{2,1,0:T(8,128)(2,1)}), bf16[32,20,3584]{2,1,0:T(8,128)(2,1)}, u32[]{:S(2)}, u32[]{:S(2)}) async-start(bf16[32,20,3584]{2,1,0:T(8,128)(2,1)} %reshape.172), calls=%async_computation.3 | async-start | bytes 11010048 | tf_op jit(solution)/shard_map/all_to_all | solution.py:119
  327.9 5.3 %fusion = bf16[1,3584,256]{2,1,0:T(8,128)(2,1)} fusion(bf16[640,3584]{1,0:T(8,128)(2,1)} %reshape.171, bf16[640,256]{0,1:T(8,128)(2,1)S(1)} %get-tuple-element.29), kind=kOutput, calls=%fused_computation.9 | convolution fusion | flops 1175322624 | bytes 6750208 | tf_op jit(solution)/shard_map/dot_general | solution.py:44
  333.2 5.2 %fusion.1 = bf16[1,3584,256]{2,1,0:T(8,128)(2,1)} fusion(bf16[640,3584]{1,0:T(8,128)(2,1)} %reshape.171, bf16[640,256]{0,1:T(8,128)(2,1)S(1)} %get-tuple-element.30), kind=kOutput, calls=%fused_computation.10 | convolution fusion | flops 1175322624 | bytes 6750208 | tf_op jit(solution)/shard_map/dot_general | solution.py:47
  338.4 2.8 fusion.2
  342.3 108.1 %all-to-all-done.3 = bf16[32,20,3584]{2,1,0:T(8,128)(2,1)} async-done(((bf16[32,20,3584]{2,1,0:T(8,128)(2,1)}), bf16[32,20,3584]{2,1,0:T(8,128)(2,1)}, u32[]{:S(2)}, u32[]{:S(2)}) %all-to-all-start.3) | async-done | bytes 4587552 | tf_op jit(solution)/shard_map/all_to_all | solution.py:119
  450.4 3.4 bitcast_reduce_fusion
  455.0 2.6 convolution_convert_fusion.3
  (61 shorter events, 20.0 us)
Async XLA Ops:
  0.6 177.5 %copy-start = (bf16[1,3584,256]{2,1,0:T(8,128)(2,1)S(1)}, bf16[1,3584,256]{2,1,0:T(8,128)(2,1)}, u32[]{:S(2)}) copy-start(bf16[1,3584,256]{2,1,0:T(8,128)(2,1)} %param.11) | copy-start | bytes 5505028
  0.6 20.8 %copy-start.1 = (bf16[128,3584]{1,0:T(8,128)(2,1)S(1)}, bf16[128,3584]{1,0:T(8,128)(2,1)}, u32[]{:S(2)}) copy-start(bf16[128,3584]{1,0:T(8,128)(2,1)} %param.7) | copy-start | bytes 2752516
  14.1 19.6 %all-to-all-start = ((bf16[32,1,20]{2,1,0:T(2,128)(2,1)}), bf16[32,1,20]{2,1,0:T(2,128)(2,1)S(1)}, u32[]{:S(2)}, u32[]{:S(2)}) async-start(bf16[32,1,20]{2,1,0:T(2,128)(2,1)} %copy.38), calls=%async_computation | async-start | bytes 32768 | tf_op jit(solution)/shard_map/all_to_all | solution.py:98
  23.7 2.3 copy-start.2
  167.1 126.1 %all-to-all-start.1 = ((bf16[32,20,3584]{2,1,0:T(8,128)(2,1)}), bf16[32,20,3584]{2,1,0:T(8,128)(2,1)}, u32[]{:S(2)}, u32[]{:S(2)}) async-start(bf16[32,20,3584]{2,1,0:T(8,128)(2,1)} %bitcast.56), calls=%async_computation.1 | async-start | bytes 11010048 | tf_op jit(solution)/shard_map/all_to_all | solution.py:91
  178.1 4.9 %copy-start.3 = (bf16[640,3584]{1,0:T(8,128)(2,1)S(1)}, bf16[640,3584]{1,0:T(8,128)(2,1)}, u32[]{:S(2)}) copy-start(bf16[640,3584]{1,0:T(8,128)(2,1)} %reshape.171) | copy-start | bytes 13762564
  178.1 4.9 %copy-start.4 = (bf16[1,3584,256]{2,1,0:T(8,128)(2,1)S(1)}, bf16[1,3584,256]{2,1,0:T(8,128)(2,1)}, u32[]{:S(2)}) copy-start(bf16[1,3584,256]{2,1,0:T(8,128)(2,1)} %param.12) | copy-start | bytes 5505028
  306.2 15.9 %all-to-all-start.4 = ((bf16[32,1,20]{2,1,0:T(2,128)(2,1)}), bf16[32,1,20]{2,1,0:T(2,128)(2,1)S(1)}, u32[]{:S(2)}, u32[]{:S(2)}) async-start(bf16[32,1,20]{2,1,0:T(2,128)(2,1)} %convert_element_type.101), calls=%async_computation.4 | async-start | bytes 32768 | tf_op jit(solution)/shard_map/all_to_all | solution.py:120
  309.8 1.5 copy-start.5
  322.1 128.3 %all-to-all-start.3 = ((bf16[32,20,3584]{2,1,0:T(8,128)(2,1)}), bf16[32,20,3584]{2,1,0:T(8,128)(2,1)}, u32[]{:S(2)}, u32[]{:S(2)}) async-start(bf16[32,20,3584]{2,1,0:T(8,128)(2,1)} %reshape.172), calls=%async_computation.3 | async-start | bytes 11010048 | tf_op jit(solution)/shard_map/all_to_all | solution.py:119
  327.8 10.6 %slice-start = ((s8[4587520]{0:T(1024)(128)(4,1)}), s8[4194304]{0:T(1024)(128)(4,1)S(1)}, s32[]{:S(2)}) async-start(s8[4587520]{0:T(1024)(128)(4,1)} %bitcast.58), calls=%async_computation.5 | async-start | bytes 8388608
  333.2 5.2 %slice-start.1 = ((s8[4587520]{0:T(1024)(128)(4,1)}), s8[393216]{0:T(1024)(128)(4,1)S(1)}, s32[]{:S(2)}) async-start(s8[4587520]{0:T(1024)(128)(4,1)} %bitcast.58), calls=%async_computation.6 | async-start | bytes 786432
where the time goes:
time: 459 us; the launch traced here: 458 us
  waiting for transfers between devices  216 us (47%)
  blocking collectives  129 us (28%)
  local copies, waits for them, and re-layouts  47.6 us (10%)
  matrix products  33.3 us (7%)
  starting transfers between devices  20.3 us (4%)
  other arithmetic  10.9 us (2%)
    all_to_all x1, blocking collectives, shards(): lax.all_to_all(repeat_groups(x_send, group_count), ('expert', 'dp'), spli...  129 us
    all_to_all x1, waiting for transfers between devices, shards(): lax.all_to_all(part_rows, ('expert', 'dp'), split_axis=0, concat_axis=0,...  108 us
    all_to_all x1, waiting for transfers between devices, shards(): lax.all_to_all(repeat_groups(dy_send, group_count), ('expert', 'dp'), spl...  108 us
  transfers between devices with their start and end apart: 4, of which 2 were waited for; matrix products, arithmetic and copies ran while one was open for 12% of the time, Pallas kernels for 0%

commit v1 on v0

v1 whole, which is shorter than its diff:
```python
import functools

import jax
import jax.numpy as jnp
from jax import lax
from jax.experimental import pallas as pl
from jax.experimental.pallas import tpu as pltpu
from jax.sharding import PartitionSpec as P

AXES = ("expert", "dp")
VMEM_LIMIT = 56 * 1024 * 1024
EXTRA = 128


def vmem():
    return pl.BlockSpec(memory_space=pltpu.VMEM)


def smem():
    return pl.BlockSpec(memory_space=pltpu.SMEM)


def params():
    return pltpu.CompilerParams(vmem_limit_bytes=VMEM_LIMIT)


def cost(flops, size):
    return pl.CostEstimate(flops=int(flops), bytes_accessed=int(size), transcendentals=0)


def chunks(total, step):
    return [(start, min(step, total - start)) for start in range(0, total, step)]


def routed(me, ids, lanes):
    target = lax.broadcasted_iota(jnp.int32, (1, lanes), 1) ^ me
    return [ids[:, k : k + 1] == target for k in range(ids.shape[1])]


def pick_kernel(expert_count, capacity, me_ref, ids_ref, weight_ref, tok_ref, grad_ref, *outs):
    rows, width = tok_ref.shape
    lanes = 128
    me = me_ref[0]
    ids = ids_ref[...]
    weights = weight_ref[...].astype(jnp.float32)
    hits = routed(me, ids, lanes)
    lane = lax.broadcasted_iota(jnp.int32, (rows, lanes), 1)
    has = jnp.zeros((rows, lanes), jnp.float32)
    weight = jnp.zeros((rows, lanes), jnp.float32)
    for k, hit in enumerate(hits):
        hit = hit & (lane < expert_count)
        has = jnp.where(hit, 1.0, has)
        weight = jnp.where(hit, weights[:, k : k + 1], weight)
    has_t = has.T
    weight_t = weight.T
    before = lax.broadcasted_iota(jnp.int32, (rows, rows), 0) < lax.broadcasted_iota(
        jnp.int32, (rows, rows), 1
    )
    rank_t = jnp.dot(
        has_t.astype(jnp.bfloat16),
        before.astype(jnp.float32).astype(jnp.bfloat16),
        preferred_element_type=jnp.float32,
    )
    slot_t = jnp.where(has_t > 0.0, rank_t, -1.0).astype(jnp.int32)
    index = lax.broadcasted_iota(jnp.int32, (2 * capacity, rows), 0)
    for s in range(expert_count):
        slot = slot_t[s : s + 1, :]
        pick_x = jnp.where((slot >= 0) & (slot == index), 1.0, 0.0).astype(jnp.bfloat16)
        pick_dy = jnp.where(
            (slot >= 0) & (slot + capacity == index), weight_t[s : s + 1, :], 0.0
        ).astype(jnp.bfloat16)
        pick_x = jnp.where(index < capacity, pick_x.astype(jnp.float32), 0.0).astype(jnp.bfloat16)
        for start, size in chunks(width, 896):
            part = slice(start, start + size)
            picked = jnp.dot(pick_x, tok_ref[:, part], preferred_element_type=jnp.float32)
            picked += jnp.dot(pick_dy, grad_ref[:, part], preferred_element_type=jnp.float32)
            outs[s][:, part] = picked.astype(jnp.bfloat16)


def pick_rows(me, ids, weights, tokens, out_grad, expert_count, capacity):
    rows, width = tokens.shape
    block = jax.ShapeDtypeStruct((2 * capacity, width), jnp.bfloat16)
    return pl.pallas_call(
        functools.partial(pick_kernel, expert_count, capacity),
        out_shape=[block] * expert_count,
        in_specs=[smem(), vmem(), vmem(), vmem(), vmem()],
        out_specs=[vmem()] * expert_count,
        compiler_params=params(),
        cost_estimate=cost(1e9, 4e6),
        name="pick_rows",
    )(me, ids, weights, tokens, out_grad)


def compact_kernel(capacity, count, *refs):
    blocks, out_ref = refs[:count], refs[count]
    for i, ref in enumerate(blocks):
        value = ref[...].astype(jnp.float32)
        place = slice(i * capacity, (i + 1) * capacity)
        out_ref[0, place, :] = value[:capacity].astype(jnp.bfloat16)
        out_ref[1, place, :] = value[capacity:].astype(jnp.bfloat16)


def compact(blocks, capacity):
    width = blocks[0].shape[1]
    count = len(blocks)
    return pl.pallas_call(
        functools.partial(compact_kernel, capacity, count),
        out_shape=jax.ShapeDtypeStruct((2, count * capacity, width), jnp.bfloat16),
        in_specs=[vmem()] * count,
        out_specs=vmem(),
        compiler_params=params(),
        cost_estimate=cost(1e6, 8 * count * capacity * width),
        name="compact",
    )(*blocks)


def expert_kernel(
    tiles, own, other, gate_ref, up_ref, down_ref, keep_ref, send_ref, units_ref, gate_w, up_w, total
):
    step = pl.program_id(0)
    rows = own.shape[1]
    hidden_units = gate_ref.shape[1]
    tile = gate_ref.shape[0]

    @pl.when(step == 0)
    def _():
        total[...] = jnp.zeros_like(total)

    @pl.when(step < tiles)
    def _():
        gate_w[step] = gate_ref[...]
        up_w[step] = up_ref[...]
        x = jnp.concatenate([own[0], other[0]], axis=0)
        dy = jnp.concatenate([own[1], other[1]], axis=0)
        total[0] += jnp.dot(x, gate_ref[...], preferred_element_type=jnp.float32)
        total[1] += jnp.dot(x, up_ref[...], preferred_element_type=jnp.float32)
        total[2] += lax.dot_general(
            dy, down_ref[...], (((1,), (1,)), ((), ())), preferred_element_type=jnp.float32
        )

    @pl.when(step == tiles - 1)
    def _():
        gate_value = total[0]
        up_value = total[1]
        back = total[2]
        sigmoid = jax.nn.sigmoid(gate_value)
        silu = gate_value * sigmoid
        hidden = (silu * up_value).astype(jnp.bfloat16)
        d_gate = back * up_value * sigmoid * (1.0 + gate_value * (1.0 - sigmoid))
        units_ref[:, 0:hidden_units] = d_gate.astype(jnp.bfloat16)
        units_ref[:, hidden_units : 2 * hidden_units] = (back * silu).astype(jnp.bfloat16)
        units_ref[:, 2 * hidden_units :] = hidden
        route = jnp.sum(hidden.astype(jnp.float32) * back, axis=1, keepdims=True)
        total[2, :, 0:EXTRA] = jnp.broadcast_to(route, (2 * rows, EXTRA))

    @pl.when((step >= tiles) & (step < 2 * tiles))
    def _():
        at = step - tiles
        contract = (((1,), (1,)), ((), ()))
        part = lax.dot_general(
            units_ref[:, 0:hidden_units], gate_w[at], contract, preferred_element_type=jnp.float32
        )
        part += lax.dot_general(
            units_ref[:, hidden_units : 2 * hidden_units],
            up_w[at],
            contract,
            preferred_element_type=jnp.float32,
        )
        part = part.astype(jnp.bfloat16)
        start = pl.multiple_of(at * tile, 128)
        keep_ref[:, pl.ds(start, tile)] = part[:rows]
        send_ref[:, pl.ds(start, tile)] = part[rows:]

    @pl.when(step == 2 * tiles - 1)
    def _():
        route = total[2, :, 0:EXTRA].astype(jnp.bfloat16)
        width = tiles * tile
        keep_ref[:, width:] = route[:rows]
        send_ref[:, width:] = route[rows:]


def run_expert(own, other, gate, up, down):
    _, rows, width = own.shape
    units = gate.shape[1]
    tile = width // 4 if width % 512 == 0 else width
    tiles = width // tile
    last = tiles - 1
    out = jax.ShapeDtypeStruct((rows, width + EXTRA), jnp.bfloat16)
    return pl.pallas_call(
        functools.partial(expert_kernel, tiles),
        grid=(2 * tiles,),
        out_shape=[out, out, jax.ShapeDtypeStruct((2 * rows, 3 * units), jnp.bfloat16)],
        in_specs=[
            pl.BlockSpec((2, rows, tile), lambda i: (0, 0, jnp.minimum(i, last))),
            pl.BlockSpec((2, rows, tile), lambda i: (0, 0, jnp.minimum(i, last))),
            pl.BlockSpec((tile, units), lambda i: (jnp.minimum(i, last), 0)),
            pl.BlockSpec((tile, units), lambda i: (jnp.minimum(i, last), 0)),
            pl.BlockSpec((units, tile), lambda i: (0, jnp.minimum(i, last))),
        ],
        out_specs=[
            pl.BlockSpec((rows, width + EXTRA), lambda i: (0, 0)),
            pl.BlockSpec((rows, width + EXTRA), lambda i: (0, 0)),
            pl.BlockSpec((2 * rows, 3 * units), lambda i: (0, 0)),
        ],
        scratch_shapes=[
            pltpu.VMEM((tiles, tile, units), jnp.bfloat16),
            pltpu.VMEM((tiles, tile, units), jnp.bfloat16),
            pltpu.VMEM((3, 2 * rows, units), jnp.float32),
        ],
        compiler_params=params(),
        cost_estimate=cost(20 * rows * width * units, 6 * width * units + 12 * rows * width),
        name="run_expert",
    )(own, other, gate, up, down)


def half_kernel(keep_ref, recv_ref, out_ref):
    rows = out_ref.shape[0]
    out_ref[...] = (
        keep_ref[rows:, :].astype(jnp.float32) + recv_ref[rows:, :].astype(jnp.float32)
    ).astype(jnp.bfloat16)


def add_half(keep, recv):
    rows, width = keep.shape
    return pl.pallas_call(
        half_kernel,
        out_shape=jax.ShapeDtypeStruct((rows // 2, width), jnp.bfloat16),
        in_specs=[vmem(), vmem()],
        out_specs=vmem(),
        compiler_params=params(),
        cost_estimate=cost(rows * width, 5 * rows * width),
        name="add_half",
    )(keep, recv)


def finish_kernel(capacity, keep_ref, recv_ref, far_ref, *outs):
    rows = far_ref.shape[0]
    half = (far_ref.shape[1] - EXTRA) // 2

    def summed(part):
        return (
            keep_ref[:rows, part].astype(jnp.float32)
            + recv_ref[:rows, part].astype(jnp.float32)
            + far_ref[:, part].astype(jnp.float32)
        )

    for h in range(2):
        for start, size in chunks(half, 896):
            value = summed(slice(h * half + start, h * half + start + size))
            for i, out in enumerate(outs):
                out[h * capacity : (h + 1) * capacity, start : start + size] = value[
                    i * capacity : (i + 1) * capacity
                ].astype(jnp.bfloat16)
    value = summed(slice(2 * half, 2 * half + EXTRA))
    for i, out in enumerate(outs):
        block = value[i * capacity : (i + 1) * capacity].astype(jnp.bfloat16)
        out[0:capacity, half:] = block
        out[capacity:, half:] = block


def finish(keep, recv, far, capacity):
    rows, width = far.shape
    count = rows // capacity
    half = (width - EXTRA) // 2
    block = jax.ShapeDtypeStruct((2 * capacity, half + EXTRA), jnp.bfloat16)
    return pl.pallas_call(
        functools.partial(finish_kernel, capacity),
        out_shape=[block] * count,
        in_specs=[vmem()] * 3,
        out_specs=[vmem()] * count,
        compiler_params=params(),
        cost_estimate=cost(3 * rows * width, 10 * rows * width),
        name="finish",
    )(keep, recv, far)


def weight_kernel(group_rows, *refs):
    count = len(group_rows)
    inputs, units = refs[: 2 * count], refs[2 * count : 3 * count]
    gate_ref, up_ref, down_ref, all_units, x_rows, dy_rows = refs[3 * count :]
    hidden_units = gate_ref.shape[1]

    @pl.when(pl.program_id(0) == 0)
    def _():
        at = 0
        for rows, ref in zip(group_rows, units):
            all_units[at : at + 2 * rows, :] = ref[...]
            at += 2 * rows

    at = 0
    for g, rows in enumerate(group_rows):
        for ref in (inputs[2 * g], inputs[2 * g + 1]):
            x_rows[at : at + rows, :] = ref[0]
            dy_rows[at : at + rows, :] = ref[1]
            at += rows
    contract = (((0,), (0,)), ((), ()))
    grads = lax.dot_general(
        x_rows[...],
        all_units[:, 0 : 2 * hidden_units],
        contract,
        preferred_element_type=jnp.float32,
    )
    gate_ref[...] = grads[:, :hidden_units].astype(jnp.bfloat16)
    up_ref[...] = grads[:, hidden_units:].astype(jnp.bfloat16)
    down_ref[...] = lax.dot_general(
        all_units[:, 2 * hidden_units :],
        dy_rows[...],
        contract,
        preferred_element_type=jnp.float32,
    ).astype(jnp.bfloat16)


def weight_grads(inputs, units):
    width = inputs[0].shape[2]
    hidden_units = units[0].shape[1] // 3
    group_rows = [u.shape[0] // 2 for u in units]
    total = 2 * sum(group_rows)
    tile = 512 if width % 512 == 0 else width
    return pl.pallas_call(
        functools.partial(weight_kernel, group_rows),
        grid=(width // tile,),
        out_shape=[
            jax.ShapeDtypeStruct((width, hidden_units), jnp.bfloat16),
            jax.ShapeDtypeStruct((width, hidden_units), jnp.bfloat16),
            jax.ShapeDtypeStruct((hidden_units, width), jnp.bfloat16),
        ],
        in_specs=[pl.BlockSpec((2, a.shape[1], tile), lambda i: (0, 0, i)) for a in inputs]
        + [pl.BlockSpec(u.shape, lambda i: (0, 0)) for u in units],
        out_specs=[
            pl.BlockSpec((tile, hidden_units), lambda i: (i, 0)),
            pl.BlockSpec((tile, hidden_units), lambda i: (i, 0)),
            pl.BlockSpec((hidden_units, tile), lambda i: (0, i)),
        ],
        scratch_shapes=[
            pltpu.VMEM((total, 3 * hidden_units), jnp.bfloat16),
            pltpu.VMEM((total, tile), jnp.bfloat16),
            pltpu.VMEM((total, tile), jnp.bfloat16),
        ],
        compiler_params=params(),
        cost_estimate=cost(
            6 * total * width * hidden_units, 4 * total * width + 6 * width * hidden_units
        ),
        name="weight_grads",
    )(*inputs, *units)


def combine_kernel(expert_count, capacity, me_ref, ids_ref, weight_ref, *refs):
    blocks = refs[:expert_count]
    tok_ref, route_ref, total = refs[expert_count:]
    rows, routes = ids_ref.shape
    half = blocks[0].shape[1] - EXTRA
    lanes = 128
    me = me_ref[0]
    ids = ids_ref[...]
    lane = lax.broadcasted_iota(jnp.int32, (rows, lanes), 1)
    has = jnp.zeros((rows, lanes), jnp.float32)
    hits = [hit & (lane < expert_count) for hit in routed(me, ids, lanes)]
    for hit in hits:
        has = jnp.where(hit, 1.0, has)
    before = lax.broadcasted_iota(jnp.int32, (rows, rows), 1) < lax.broadcasted_iota(
        jnp.int32, (rows, rows), 0
    )
    rank = jnp.dot(
        before.astype(jnp.float32).astype(jnp.bfloat16),
        has.astype(jnp.bfloat16),
        preferred_element_type=jnp.float32,
    )
    slot = jnp.where(has > 0.0, rank, -1.0).astype(jnp.int32)
    index = lax.broadcasted_iota(jnp.int32, (rows, 2 * capacity), 1)
    picks = []
    for s in range(expert_count):
        column = slot[:, s : s + 1]
        low = jnp.where((column >= 0) & (column == index), 1.0, 0.0)
        high = jnp.where((column >= 0) & (column + capacity == index), 1.0, 0.0)
        low = jnp.where(index < capacity, low, 0.0)
        picks.append(jnp.concatenate([low, high], axis=0).astype(jnp.bfloat16))
    for start, size in chunks(half, 896):
        part = jnp.zeros((2 * rows, size), jnp.float32)
        for s in range(expert_count):
            part += jnp.dot(
                picks[s], blocks[s][:, start : start + size], preferred_element_type=jnp.float32
            )
        tok_ref[:, start : start + size] = part[:rows].astype(jnp.bfloat16)
        tok_ref[:, half + start : half + start + size] = part[rows:].astype(jnp.bfloat16)
    values = jnp.zeros((rows, lanes), jnp.float32)
    for s in range(expert_count):
        found = jnp.dot(picks[s], blocks[s][:, half:], preferred_element_type=jnp.float32)
        values = jnp.where(lane == s, found[:rows], values)
    total[...] = jnp.zeros_like(total)
    out = jnp.zeros((rows, lanes), jnp.float32)
    for k, hit in enumerate(hits):
        picked = jnp.sum(jnp.where(hit, values, 0.0), axis=1, keepdims=True)
        out = jnp.where(lane == k, picked, out)
    total[...] = out
    route_ref[...] = (
        total[:, 0:routes] / weight_ref[...].astype(jnp.float32)
    ).astype(jnp.bfloat16)


def combine(me, ids, weights, blocks, capacity):
    rows, routes = ids.shape
    half = blocks[0].shape[1] - EXTRA
    return pl.pallas_call(
        functools.partial(combine_kernel, len(blocks), capacity),
        out_shape=[
            jax.ShapeDtypeStruct((rows, 2 * half), jnp.bfloat16),
            jax.ShapeDtypeStruct((rows, routes), jnp.bfloat16),
        ],
        in_specs=[smem()] + [vmem()] * (2 + len(blocks)),
        out_specs=[vmem(), vmem()],
        scratch_shapes=[pltpu.VMEM((rows, 128), jnp.float32)],
        compiler_params=params(),
        cost_estimate=cost(1e9, 3e6),
        name="combine",
    )(me, ids, weights, *blocks)


def source_groups(expert_count):
    half, three = expert_count // 2, 3 * expert_count // 4
    return [
        list(range(half)),
        list(range(three, expert_count)),
        list(range(half, three)),
    ]


def shards(tokens, out_grad, expert_ids, route_weights, w_gate, w_up, w_down):
    expert_count = lax.axis_size("expert")
    group_count = lax.axis_size("dp")
    device_count = expert_count * group_count
    capacity = 5 * tokens.shape[0] // (4 * expert_count)
    if (2 * capacity) % 8:
        capacity = -(-capacity // 8) * 8
    me = lax.axis_index("expert").astype(jnp.int32).reshape(1)

    def swap(value, distance):
        return lax.ppermute(value, AXES, [(i, i ^ distance) for i in range(device_count)])

    blocks = pick_rows(
        me, expert_ids, route_weights, tokens, out_grad, expert_count, capacity
    )
    got, crossed = {}, {}
    for s in reversed(range(expert_count)):
        got[s] = swap(blocks[s], s * group_count) if s else blocks[0]
    inputs, units, back = [], [], {}
    for group in source_groups(expert_count):
        for s in group:
            crossed[s] = swap(got[s], 2)
        own = compact([got[s] for s in group] + [crossed[s] for s in group], capacity)
        other = swap(own, 1)
        keep, send, group_units = run_expert(own, other, w_gate[0], w_up[0], w_down[0])
        inputs += [own, other]
        units.append(group_units)
        recv = swap(send, 1)
        far = swap(add_half(keep, recv), 2)
        for s, block in zip(group, finish(keep, recv, far, capacity)):
            back[s] = swap(block, s * group_count) if s else block
    grad_gate, grad_up, grad_down = weight_grads(inputs, units)
    grad_tokens, grad_route = combine(
        me, expert_ids, route_weights, [back[s] for s in range(expert_count)], capacity
    )
    return (grad_tokens, grad_route, grad_gate[None], grad_up[None], grad_down[None])


def solution(mesh):
    rows = P(AXES, None)
    columns = P("expert", None, "dp")
    return jax.shard_map(
        shards,
        mesh=mesh,
        in_specs=(rows, rows, rows, rows, columns, columns, P("expert", "dp", None)),
        out_specs=(rows, rows, columns, columns, P("expert", "dp", None)),
        check_vma=False,
    )
```

time: 459 us -> 211 us (0.46)
  blocking collectives: 129 us -> 0 us
  waiting for transfers between devices: 216 us -> 88.1 us
  Pallas kernels: 0 us -> 67.9 us
  matrix products: 33.3 us -> 0 us
  local copies, waits for them, and re-layouts: 47.6 us -> 15.6 us
  starting transfers between devices: 20.3 us -> 37.3 us
  other arithmetic: 10.9 us -> 0 us
    all_to_all x4 -> x0, waiting for transfers between devices: 216 us -> none  [the longest x1 108 us: shards(): lax.all_to_all(part_rows, ('expert', 'dp'), split_axis=0, concat_axis=0,...]
    all_to_all x1 -> x0, blocking collectives: 129 us -> none  [shards(): lax.all_to_all(repeat_groups(x_send, group_count), ('expert', 'dp'), spli...]
    ppermute x0 -> x31, waiting for transfers between devices: none -> 88.1 us  [swap(): lax.ppermute(value, AXES, [(i, i ^ distance) for i in range(device_count)])]
    pallas_call x0 -> x15, Pallas kernels: none -> 67.9 us  [the longest x3 26.1 us: run_expert(): pl.pallas_call(functools.partial(expert_kernel, tiles), grid=(2 * tiles,)...]
    ppermute x0 -> x31, starting transfers between devices: none -> 37.3 us  [swap(): lax.ppermute(value, AXES, [(i, i ^ distance) for i in range(device_count)])]
    dot_general x9 -> x0, matrix products: 33.3 us -> none  [the longest x1 5.33 us: backward_rows(): lax.dot_general(x_rows, d_gate, contract_rows, preferred_element_type=jnp...]
    reshape x5 -> x0, local copies, waits for them, and re-layouts: 23 us -> none  [the longest x1 7.27 us: shards(): dy_all.reshape(-1, width)]
    all_to_all x4 -> x0, starting transfers between devices: 20.3 us -> none  [the longest x1 7.3 us: shards(): lax.all_to_all(repeat_groups(w_send, group_count), ('expert', 'dp'), spli...]
  transfers between devices with their start and end apart: 4 -> 31, of which waited for: 2 -> 14; matrix products, arithmetic and copies ran while one was open for 12% -> 0% of each run, Pallas kernels for 0% -> 26%
where the time goes in v1:
time: 211 us; the launch traced here: 210 us
  waiting for transfers between devices  88.1 us (42%)
  Pallas kernels  67.9 us (32%)
  starting transfers between devices  37.3 us (18%)
  local copies, waits for them, and re-layouts  15.6 us (7%)
    ppermute x31, waiting for transfers between devices, swap(): lax.ppermute(value, AXES, [(i, i ^ distance) for i in range(device_count)])  88.1 us
    ppermute x31, starting transfers between devices, swap(): lax.ppermute(value, AXES, [(i, i ^ distance) for i in range(device_count)])  37.3 us
    pallas_call x3, Pallas kernels, run_expert(): pl.pallas_call(functools.partial(expert_kernel, tiles), grid=(2 * tiles,)...  26.1 us
    unnamed x73, local copies, waits for them, and re-layouts  15.6 us
    pallas_call x1, Pallas kernels, weight_grads(): pl.pallas_call(functools.partial(weight_kernel, group_rows), grid=(width...  10.1 us
    pallas_call x3, Pallas kernels, compact(): pl.pallas_call(functools.partial(compact_kernel, capacity, count), out_sh...  7.83 us
    pallas_call x3, Pallas kernels, finish(): pl.pallas_call(functools.partial(finish_kernel, capacity), out_shape=[blo...  7.18 us
    pallas_call x3, Pallas kernels, add_half(): pl.pallas_call(half_kernel, out_shape=jax.ShapeDtypeStruct((rows // 2, wi...  6.65 us
  transfers between devices with their start and end apart: 31, of which 14 were waited for; matrix products, arithmetic and copies ran while one was open for 0% of the time, Pallas kernels for 26%

profile of v1, /device:TPU:0, one launch (start us, length us, event | category | flops | bytes accessed | tf_op | source)
XLA Modules:
  0.0 209.9 jit_solution(17903925963884610771)
XLA Ops:
  3.4 5.0 %pick_rows.1 = (bf16[40,3584]{1,0:T(8,128)(2,1)}, bf16[40,3584]{1,0:T(8,128)(2,1)}, bf16[40,3584]{1,0:T(8,128)(2,1)}, bf16[40,3584]{1,0:T(8,128)(2,1)}, bf16[40,...) custom-call(s32[1]{0:T(128)} %bitcast.me_ref, ...), custom_call_target="tpu_custom_call" | custom-call | flops 1000000000 | bytes 4000000 | tf_op jit(solution)/shard_map/pick_rows/pallas_call | solution.py:83
  8.5 3.0 %collective-permute-start = (bf16[40,3584]{1,0:T(8,128)(2,1)}, bf16[40,3584]{1,0:T(8,128)(2,1)S(1)}, u32[]{:S(2)}, u32[]{:S(2)}) collective-permute-start(bf16[40,3584]{1,0:T(8,128)(2,1)} %get-tuple-element.36), channel_id=1, source_target_pairs={{0,4},{1,5},{2,6},{3,7},{4,0},{5,1},{6,2},{7,3},{8,12},{9,13},{10,... | collective-permute-start | bytes 860168 | tf_op jit(solution)/shard_map/ppermute | solution.py:437
  15.0 3.5 %collective-permute-done.refs_1_ = bf16[40,3584]{1,0:T(8,128)(2,1)S(1)} collective-permute-done((bf16[40,3584]{1,0:T(8,128)(2,1)}, bf16[40,3584]{1,0:T(8,128)(2,1)S(1)}, u32[]{:S(2)}, u32[]{:S(2)}) %collective-permute-start) | collective-permute-done | bytes 286752 | tf_op jit(solution)/shard_map/ppermute | solution.py:437
  22.9 3.0 %collective-permute-done.2.refs_3_ = bf16[40,3584]{1,0:T(8,128)(2,1)S(1)} collective-permute-done((bf16[40,3584]{1,0:T(8,128)(2,1)}, bf16[40,3584]{1,0:T(8,128)(2,1)S(1)}, u32[]{:S(2)}, u32[]{:S(2)}) %collective-permute-start.2) | collective-permute-done | bytes 286752 | tf_op jit(solution)/shard_map/ppermute | solution.py:437
  28.4 6.1 %collective-permute-done.5.refs_6_ = bf16[40,3584]{1,0:T(8,128)(2,1)S(1)} collective-permute-done((bf16[40,3584]{1,0:T(8,128)(2,1)S(1)}, bf16[40,3584]{1,0:T(8,128)(2,1)S(1)}, u32[]{:S(2)}, u32[]{:S(2)}) %collective-permute-start.5) | collective-permute-done | bytes 286752 | tf_op jit(solution)/shard_map/ppermute | solution.py:437
  34.5 5.2 %collective-permute-done.6.refs_7_ = bf16[40,3584]{1,0:T(8,128)(2,1)S(1)} collective-permute-done((bf16[40,3584]{1,0:T(8,128)(2,1)S(1)}, bf16[40,3584]{1,0:T(8,128)(2,1)S(1)}, u32[]{:S(2)}, u32[]{:S(2)}) %collective-permute-start.6) | collective-permute-done | bytes 286752 | tf_op jit(solution)/shard_map/ppermute | solution.py:437
  40.6 3.1 %compact.3.own.refs_0_ = bf16[2,160,3584]{2,1,0:T(8,128)(2,1)} custom-call(bf16[40,3584]{1,0:T(8,128)(2,1)} %get-tuple-element.35.refs_0_, bf16[40,3584]{1,0:T(8,128)(2,1)} %copy-done.11, bf16[40,3584]{1,0:T(8,128)(2,1)} %copy-done.13, bf16[40,3584]{1,0:T(8,128)(2,1)} %copy-done.14, bf16[40,3584]{1,0:T(8,128)(2,1)} %copy-done.15, ...), custom_call_target="tpu_custom_call" | custom-call | flops 1000000 | bytes 4587520 | tf_op jit(solution)/shard_map/compact/pallas_call | solution.py:106
  47.8 3.6 %collective-permute-start.22 = (bf16[40,3584]{1,0:T(8,128)(2,1)S(1)}, bf16[40,3584]{1,0:T(8,128)(2,1)S(1)}, u32[]{:S(2)}, u32[]{:S(2)}) collective-permute-start(bf16[40,3584]{1,0:T(8,128)(2,1)S(1)} %copy-done.25), channel_id=1, source_target_pairs={{0,24},{1,25},{2,26},{3,27},{4,28},{5,29},{6,30},{7,31},{8,16},{9,... | collective-permute-start | bytes 860168 | tf_op jit(solution)/shard_map/ppermute | solution.py:437
  51.4 27.4 %collective-permute-done.13.refs_0_ = bf16[40,3584]{1,0:T(8,128)(2,1)S(1)} collective-permute-done((bf16[40,3584]{1,0:T(8,128)(2,1)S(1)}, bf16[40,3584]{1,0:T(8,128)(2,1)S(1)}, u32[]{:S(2)}, u32[]{:S(2)}) %collective-permute-start.13) | collective-permute-done | bytes 286752 | tf_op jit(solution)/shard_map/ppermute | solution.py:437
  80.5 5.6 %collective-permute-done.14.refs_1_ = bf16[40,3584]{1,0:T(8,128)(2,1)S(1)} collective-permute-done((bf16[40,3584]{1,0:T(8,128)(2,1)S(1)}, bf16[40,3584]{1,0:T(8,128)(2,1)S(1)}, u32[]{:S(2)}, u32[]{:S(2)}) %collective-permute-start.14) | collective-permute-done | bytes 286752 | tf_op jit(solution)/shard_map/ppermute | solution.py:437
  89.6 6.2 %collective-permute-done.16.refs_3_ = bf16[40,3584]{1,0:T(8,128)(2,1)S(1)} collective-permute-done((bf16[40,3584]{1,0:T(8,128)(2,1)S(1)}, bf16[40,3584]{1,0:T(8,128)(2,1)S(1)}, u32[]{:S(2)}, u32[]{:S(2)}) %collective-permute-start.16) | collective-permute-done | bytes 286752 | tf_op jit(solution)/shard_map/ppermute | solution.py:437
  98.9 3.1 %collective-permute-done.24.refs_2_ = bf16[40,3584]{1,0:T(8,128)(2,1)S(1)} collective-permute-done((bf16[40,3584]{1,0:T(8,128)(2,1)S(1)}, bf16[40,3584]{1,0:T(8,128)(2,1)S(1)}, u32[]{:S(2)}, u32[]{:S(2)}) %collective-permute-start.24) | collective-permute-done | bytes 286752 | tf_op jit(solution)/shard_map/ppermute | solution.py:437
  102.0 4.3 %collective-permute-done.25.refs_3_ = bf16[40,3584]{1,0:T(8,128)(2,1)S(1)} collective-permute-done((bf16[40,3584]{1,0:T(8,128)(2,1)S(1)}, bf16[40,3584]{1,0:T(8,128)(2,1)S(1)}, u32[]{:S(2)}, u32[]{:S(2)}) %collective-permute-start.25) | collective-permute-done | bytes 286752 | tf_op jit(solution)/shard_map/ppermute | solution.py:437
  110.8 10.0 %run_expert.3 = (bf16[160,3712]{1,0:T(8,128)(2,1)}, bf16[160,3712]{1,0:T(8,128)(2,1)}, bf16[320,768]{1,0:T(8,128)(2,1)}) custom-call(bf16[2,160,3584]{2,1,0:T(8,128)(2,1)} %compact.3.own.refs_0_, bf16[2,160,3584]{2,1,0:T(8,128)(2,1)} %copy-done.23, bf16[3584,256]{1,0:T(8,128)(2,1)} %bitcast.7, bf16[3584,256]{1,0:T(8,128)(2,1)} %bitcast.10, ...), custom_call_target="tpu_custom_call" | custom-call | flops 2936012800 | bytes 12386304 | tf_op jit(solution)/shard_map/run_expert/pallas_call | solution.py:189
  122.3 8.0 %run_expert.4 = (bf16[80,3712]{1,0:T(8,128)(2,1)}, bf16[80,3712]{1,0:T(8,128)(2,1)}, bf16[160,768]{1,0:T(8,128)(2,1)}) custom-call(bf16[2,80,3584]{2,1,0:T(8,128)(2,1)} %compact.4.own.refs_4_, bf16[2,80,3584]{2,1,0:T(8,128)(2,1)} %copy-done.3, bf16[3584,256]{1,0:T(8,128)(2,1)} %bitcast.8, bf16[3584,256]{1,0:T(8,128)(2,1)} %bitcast.11, bf16[256,3584]{1,0:T(8,128)(2,1)} %bitcast.14), custom_call_target="tpu_custom_call" | custom-call | flops 1468006400 | bytes 8945664 | tf_op jit(solution)/shard_map/run_expert/pallas_call | solution.py:189
  131.4 8.1 %run_expert.5 = (bf16[80,3712]{1,0:T(8,128)(2,1)}, bf16[80,3712]{1,0:T(8,128)(2,1)}, bf16[160,768]{1,0:T(8,128)(2,1)}) custom-call(bf16[2,80,3584]{2,1,0:T(8,128)(2,1)} %compact.5.own.refs_2_, bf16[2,80,3584]{2,1,0:T(8,128)(2,1)} %copy-done.4, bf16[3584,256]{1,0:T(8,128)(2,1)} %bitcast.9, bf16[3584,256]{1,0:T(8,128)(2,1)} %bitcast.12, bf16[256,3584]{1,0:T(8,128)(2,1)} %bitcast.15), custom_call_target="tpu_custom_call" | custom-call | flops 1468006400 | bytes 8945664 | tf_op jit(solution)/shard_map/run_expert/pallas_call | solution.py:189
  152.9 13.6 %collective-permute-done.19.far_ref = bf16[40,3712]{1,0:T(8,128)(2,1)S(1)} collective-permute-done((bf16[40,3712]{1,0:T(8,128)(2,1)}, bf16[40,3712]{1,0:T(8,128)(2,1)S(1)}, u32[]{:S(2)}, u32[]{:S(2)}) %collective-permute-start.19) | collective-permute-done | bytes 296992 | tf_op jit(solution)/shard_map/ppermute | solution.py:437
  169.4 3.0 %collective-permute-start.20 = (bf16[40,1920]{1,0:T(8,128)(2,1)}, bf16[40,1920]{1,0:T(8,128)(2,1)S(1)}, u32[]{:S(2)}, u32[]{:S(2)}) collective-permute-start(bf16[40,1920]{1,0:T(8,128)(2,1)} %get-tuple-element.49), channel_id=1, source_target_pairs={{0,16},{1,17},{2,18},{3,19},{4,20},{5,21},{6,22},{7,23},{8,24},{9,... | collective-permute-start | bytes 460808 | tf_op jit(solution)/shard_map/ppermute | solution.py:437
  175.3 3.8 %collective-permute-start.29 = (bf16[40,1920]{1,0:T(8,128)(2,1)}, bf16[40,1920]{1,0:T(8,128)(2,1)S(1)}, u32[]{:S(2)}, u32[]{:S(2)}) collective-permute-start(bf16[40,1920]{1,0:T(8,128)(2,1)} %get-tuple-element.55), channel_id=1, source_target_pairs={{0,24},{1,25},{2,26},{3,27},{4,28},{5,29},{6,30},{7,31},{8,16},{9,... | collective-permute-start | bytes 460808 | tf_op jit(solution)/shard_map/ppermute | solution.py:437
  180.8 2.8 %finish.3 = (bf16[40,1920]{1,0:T(8,128)(2,1)}, bf16[40,1920]{1,0:T(8,128)(2,1)}, bf16[40,1920]{1,0:T(8,128)(2,1)}, bf16[40,1920]{1,0:T(8,128)(2,1)}) custom-call(bf16[160,3712]{1,0:T(8,128)(2,1)} %get-tuple-element.39.keep_ref, bf16[160,3712]{1,0:T(8,128)(2,1)} %copy-done, bf16[80,3712]{1,0:T(8,128)(2,1)} %copy-done.5), custom_call_target="tpu_custom_call" | custom-call | flops 890880 | bytes 2969600 | tf_op jit(solution)/shard_map/finish/pallas_call | solution.py:266
  184.2 5.0 %collective-permute-done.20.refs_4_ = bf16[40,1920]{1,0:T(8,128)(2,1)S(1)} collective-permute-done((bf16[40,1920]{1,0:T(8,128)(2,1)}, bf16[40,1920]{1,0:T(8,128)(2,1)S(1)}, u32[]{:S(2)}, u32[]{:S(2)}) %collective-permute-start.20) | collective-permute-done | bytes 153632 | tf_op jit(solution)/shard_map/ppermute | solution.py:437
  189.2 3.3 %collective-permute-done.21.refs_5_ = bf16[40,1920]{1,0:T(8,128)(2,1)S(1)} collective-permute-done((bf16[40,1920]{1,0:T(8,128)(2,1)}, bf16[40,1920]{1,0:T(8,128)(2,1)S(1)}, u32[]{:S(2)}, u32[]{:S(2)}) %collective-permute-start.21) | collective-permute-done | bytes 153632 | tf_op jit(solution)/shard_map/ppermute | solution.py:437
  192.4 10.1 %weight_grads.1 = (bf16[3584,256]{1,0:T(8,128)(2,1)}, bf16[3584,256]{1,0:T(8,128)(2,1)}, bf16[256,3584]{1,0:T(8,128)(2,1)}) custom-call(bf16[2,160,3584]{2,1,0:T(8,128)(2,1)} %compact.3.own.refs_0_, bf16[2,160,3584]{2,1,0:T(8,128)(2,1)} %copy-done.23, bf16[2,80,3584]{2,1,0:T(8,128)(2,1)} %compact.5.own.refs_2_, bf16[2,80,3584]{2,1,0:T(8,128)(2,1)} %copy-done.4, ...), custom_call_target="tpu_custom_call" | custom-call | flops 3523215360 | bytes 14680064 | tf_op jit(solution)/shard_map/weight_grads/pallas_call | solution.py:319
  203.4 5.1 %combine.1 = (bf16[128,3584]{1,0:T(8,128)(2,1)}, bf16[128,8]{1,0:T(8,128)(2,1)}) custom-call(s32[1]{0:T(128)} %bitcast.me_ref, s32[128,8]{1,0:T(8,128)} %copy.14.ids_ref, bf16[128,8]{1,0:T(8,128)(2,1)} %copy.15.weight_ref, bf16[40,1920]{1,0:T(8,128)(2,1)} %get-tuple-element.41.refs_0_, bf16[40,1920]{1,0:T(8,128)(2,1)} %copy-done.32, ...), custom_call_target="tpu_custom_call" | custom-call | flops 1000000000 | bytes 3000000 | tf_op jit(solution)/shard_map/combine/pallas_call | solution.py:403
  (126 shorter events, 57.1 us)
Async XLA Ops:
  13.0 12.8 %collective-permute-start.2 = (bf16[40,3584]{1,0:T(8,128)(2,1)}, bf16[40,3584]{1,0:T(8,128)(2,1)S(1)}, u32[]{:S(2)}, u32[]{:S(2)}) collective-permute-start(bf16[40,3584]{1,0:T(8,128)(2,1)} %get-tuple-element.38), channel_id=1, source_target_pairs={{0,12},{1,13},{2,14},{3,15},{4,8},{5,9},{6,10},{7,11},{8,4},{9,5},... | collective-permute-start | bytes 860168 | tf_op jit(solution)/shard_map/ppermute | solution.py:437
  13.1 14.5 %collective-permute-start.3 = (bf16[40,3584]{1,0:T(8,128)(2,1)}, bf16[40,3584]{1,0:T(8,128)(2,1)S(1)}, u32[]{:S(2)}, u32[]{:S(2)}) collective-permute-start(bf16[40,3584]{1,0:T(8,128)(2,1)} %get-tuple-element.35.refs_0_), channel_id=1, source_target_pairs={{0,2},{1,3},{2,0},{3,1},{4,6},{5,7},{6,4},{7,5},{8,10},{9,11},{10,... | collective-permute-start | bytes 860168 | tf_op jit(solution)/shard_map/ppermute | solution.py:437
  21.4 13.1 %collective-permute-start.5 = (bf16[40,3584]{1,0:T(8,128)(2,1)S(1)}, bf16[40,3584]{1,0:T(8,128)(2,1)S(1)}, u32[]{:S(2)}, u32[]{:S(2)}) collective-permute-start(bf16[40,3584]{1,0:T(8,128)(2,1)S(1)} %collective-permute-done.1.refs_2_), channel_id=1, source_target_pairs={{0,2},{1,3},{2,0},{3,1},{4,6},{5,7},{6,4},{7,5},{8,10},{9,11},{10,... | collective-permute-start | bytes 860168 | tf_op jit(solution)/shard_map/ppermute | solution.py:437
  25.9 13.9 %collective-permute-start.6 = (bf16[40,3584]{1,0:T(8,128)(2,1)S(1)}, bf16[40,3584]{1,0:T(8,128)(2,1)S(1)}, u32[]{:S(2)}, u32[]{:S(2)}) collective-permute-start(bf16[40,3584]{1,0:T(8,128)(2,1)S(1)} %collective-permute-done.2.refs_3_), channel_id=1, source_target_pairs={{0,2},{1,3},{2,0},{3,1},{4,6},{5,7},{6,4},{7,5},{8,10},{9,11},{10,... | collective-permute-start | bytes 860168 | tf_op jit(solution)/shard_map/ppermute | solution.py:437
  43.7 65.7 %collective-permute-start.7 = (bf16[2,160,3584]{2,1,0:T(8,128)(2,1)}, bf16[2,160,3584]{2,1,0:T(8,128)(2,1)S(1)}, u32[]{:S(2)}, u32[]{:S(2)}) collective-permute-start(bf16[2,160,3584]{2,1,0:T(8,128)(2,1)} %compact.3.own.refs_0_), channel_id=1, source_target_pairs={{0,1},{1,0},{2,3},{3,2},{4,5},{5,4},{6,7},{7,6},{8,9},{9,8},{10,11... | collective-permute-start | bytes 6881288 | tf_op jit(solution)/shard_map/ppermute | solution.py:437
  43.7 35.2 %collective-permute-start.13 = (bf16[40,3584]{1,0:T(8,128)(2,1)S(1)}, bf16[40,3584]{1,0:T(8,128)(2,1)S(1)}, u32[]{:S(2)}, u32[]{:S(2)}) collective-permute-start(bf16[40,3584]{1,0:T(8,128)(2,1)S(1)} %copy-done.27), channel_id=1, source_target_pairs={{0,16},{1,17},{2,18},{3,19},{4,20},{5,21},{6,22},{7,23},{8,24},{9,... | collective-permute-start | bytes 860168 | tf_op jit(solution)/shard_map/ppermute | solution.py:437
  46.5 39.6 %collective-permute-start.14 = (bf16[40,3584]{1,0:T(8,128)(2,1)S(1)}, bf16[40,3584]{1,0:T(8,128)(2,1)S(1)}, u32[]{:S(2)}, u32[]{:S(2)}) collective-permute-start(bf16[40,3584]{1,0:T(8,128)(2,1)S(1)} %copy-done.26), channel_id=1, source_target_pairs={{0,20},{1,21},{2,22},{3,23},{4,16},{5,17},{6,18},{7,19},{8,28},{9,... | collective-permute-start | bytes 860168 | tf_op jit(solution)/shard_map/ppermute | solution.py:437
  47.8 39.8 %collective-permute-start.22 = (bf16[40,3584]{1,0:T(8,128)(2,1)S(1)}, bf16[40,3584]{1,0:T(8,128)(2,1)S(1)}, u32[]{:S(2)}, u32[]{:S(2)}) collective-permute-start(bf16[40,3584]{1,0:T(8,128)(2,1)S(1)} %copy-done.25), channel_id=1, source_target_pairs={{0,24},{1,25},{2,26},{3,27},{4,28},{5,29},{6,30},{7,31},{8,16},{9,... | collective-permute-start | bytes 860168 | tf_op jit(solution)/shard_map/ppermute | solution.py:437
  51.4 36.8 %collective-permute-start.23 = (bf16[40,3584]{1,0:T(8,128)(2,1)S(1)}, bf16[40,3584]{1,0:T(8,128)(2,1)S(1)}, u32[]{:S(2)}, u32[]{:S(2)}) collective-permute-start(bf16[40,3584]{1,0:T(8,128)(2,1)S(1)} %copy-done.24), channel_id=1, source_target_pairs={{0,28},{1,29},{2,30},{3,31},{4,24},{5,25},{6,26},{7,27},{8,20},{9,... | collective-permute-start | bytes 860168 | tf_op jit(solution)/shard_map/ppermute | solution.py:437
  87.6 14.4 %collective-permute-start.24 = (bf16[40,3584]{1,0:T(8,128)(2,1)S(1)}, bf16[40,3584]{1,0:T(8,128)(2,1)S(1)}, u32[]{:S(2)}, u32[]{:S(2)}) collective-permute-start(bf16[40,3584]{1,0:T(8,128)(2,1)S(1)} %collective-permute-done.22.refs_0_), channel_id=1, source_target_pairs={{0,2},{1,3},{2,0},{3,1},{4,6},{5,7},{6,4},{7,5},{8,10},{9,11},{10,... | collective-permute-start | bytes 860168 | tf_op jit(solution)/shard_map/ppermute | solution.py:437
  88.1 18.2 %collective-permute-start.25 = (bf16[40,3584]{1,0:T(8,128)(2,1)S(1)}, bf16[40,3584]{1,0:T(8,128)(2,1)S(1)}, u32[]{:S(2)}, u32[]{:S(2)}) collective-permute-start(bf16[40,3584]{1,0:T(8,128)(2,1)S(1)} %collective-permute-done.23.refs_1_), channel_id=1, source_target_pairs={{0,2},{1,3},{2,0},{3,1},{4,6},{5,7},{6,4},{7,5},{8,10},{9,11},{10,... | collective-permute-start | bytes 860168 | tf_op jit(solution)/shard_map/ppermute | solution.py:437
  98.9 22.3 %collective-permute-start.17 = (bf16[2,80,3584]{2,1,0:T(8,128)(2,1)}, bf16[2,80,3584]{2,1,0:T(8,128)(2,1)S(1)}, u32[]{:S(2)}, u32[]{:S(2)}) collective-permute-start(bf16[2,80,3584]{2,1,0:T(8,128)(2,1)} %compact.4.own.refs_4_), channel_id=1, source_target_pairs={{0,1},{1,0},{2,3},{3,2},{4,5},{5,4},{6,7},{7,6},{8,9},{9,8},{10,11... | collective-permute-start | bytes 3440648 | tf_op jit(solution)/shard_map/ppermute | solution.py:437
  109.4 21.0 %collective-permute-start.26 = (bf16[2,80,3584]{2,1,0:T(8,128)(2,1)}, bf16[2,80,3584]{2,1,0:T(8,128)(2,1)S(1)}, u32[]{:S(2)}, u32[]{:S(2)}) collective-permute-start(bf16[2,80,3584]{2,1,0:T(8,128)(2,1)} %compact.5.own.refs_2_), channel_id=1, source_target_pairs={{0,1},{1,0},{2,3},{3,2},{4,5},{5,4},{6,7},{7,6},{8,9},{9,8},{10,11... | collective-permute-start | bytes 3440648 | tf_op jit(solution)/shard_map/ppermute | solution.py:437
  120.7 19.2 %collective-permute-start.8 = (bf16[160,3712]{1,0:T(8,128)(2,1)}, bf16[160,3712]{1,0:T(8,128)(2,1)S(1)}, u32[]{:S(2)}, u32[]{:S(2)}) collective-permute-start(bf16[160,3712]{1,0:T(8,128)(2,1)} %get-tuple-element.40), channel_id=1, source_target_pairs={{0,1},{1,0},{2,3},{3,2},{4,5},{5,4},{6,7},{7,6},{8,9},{9,8},{10,11... | collective-permute-start | bytes 3563528 | tf_op jit(solution)/shard_map/ppermute | solution.py:437
  130.3 14.7 %collective-permute-start.18 = (bf16[80,3712]{1,0:T(8,128)(2,1)}, bf16[80,3712]{1,0:T(8,128)(2,1)S(1)}, u32[]{:S(2)}, u32[]{:S(2)}) collective-permute-start(bf16[80,3712]{1,0:T(8,128)(2,1)} %get-tuple-element.48), channel_id=1, source_target_pairs={{0,1},{1,0},{2,3},{3,2},{4,5},{5,4},{6,7},{7,6},{8,9},{9,8},{10,11... | collective-permute-start | bytes 1781768 | tf_op jit(solution)/shard_map/ppermute | solution.py:437
  143.6 36.4 %collective-permute-start.9 = (bf16[80,3712]{1,0:T(8,128)(2,1)}, bf16[80,3712]{1,0:T(8,128)(2,1)S(1)}, u32[]{:S(2)}, u32[]{:S(2)}) collective-permute-start(bf16[80,3712]{1,0:T(8,128)(2,1)} %add_half.3), channel_id=1, source_target_pairs={{0,2},{1,3},{2,0},{3,1},{4,6},{5,7},{6,4},{7,5},{8,10},{9,11},{10,... | collective-permute-start | bytes 1781768 | tf_op jit(solution)/shard_map/ppermute | solution.py:437
  147.9 18.5 %collective-permute-start.19 = (bf16[40,3712]{1,0:T(8,128)(2,1)}, bf16[40,3712]{1,0:T(8,128)(2,1)S(1)}, u32[]{:S(2)}, u32[]{:S(2)}) collective-permute-start(bf16[40,3712]{1,0:T(8,128)(2,1)} %add_half.4), channel_id=1, source_target_pairs={{0,2},{1,3},{2,0},{3,1},{4,6},{5,7},{6,4},{7,5},{8,10},{9,11},{10,... | collective-permute-start | bytes 890888 | tf_op jit(solution)/shard_map/ppermute | solution.py:437
  151.4 21.0 %collective-permute-start.28 = (bf16[40,3712]{1,0:T(8,128)(2,1)}, bf16[40,3712]{1,0:T(8,128)(2,1)S(1)}, u32[]{:S(2)}, u32[]{:S(2)}) collective-permute-start(bf16[40,3712]{1,0:T(8,128)(2,1)} %add_half.5), channel_id=1, source_target_pairs={{0,2},{1,3},{2,0},{3,1},{4,6},{5,7},{6,4},{7,5},{8,10},{9,11},{10,... | collective-permute-start | bytes 890888 | tf_op jit(solution)/shard_map/ppermute | solution.py:437
  169.4 19.8 %collective-permute-start.20 = (bf16[40,1920]{1,0:T(8,128)(2,1)}, bf16[40,1920]{1,0:T(8,128)(2,1)S(1)}, u32[]{:S(2)}, u32[]{:S(2)}) collective-permute-start(bf16[40,1920]{1,0:T(8,128)(2,1)} %get-tuple-element.49), channel_id=1, source_target_pairs={{0,16},{1,17},{2,18},{3,19},{4,20},{5,21},{6,22},{7,23},{8,24},{9,... | collective-permute-start | bytes 460808 | tf_op jit(solution)/shard_map/ppermute | solution.py:437
  172.4 20.1 %collective-permute-start.21 = (bf16[40,1920]{1,0:T(8,128)(2,1)}, bf16[40,1920]{1,0:T(8,128)(2,1)S(1)}, u32[]{:S(2)}, u32[]{:S(2)}) collective-permute-start(bf16[40,1920]{1,0:T(8,128)(2,1)} %get-tuple-element.50), channel_id=1, source_target_pairs={{0,20},{1,21},{2,22},{3,23},{4,16},{5,17},{6,18},{7,19},{8,28},{9,... | collective-permute-start | bytes 460808 | tf_op jit(solution)/shard_map/ppermute | solution.py:437
  175.3 27.3 %collective-permute-start.29 = (bf16[40,1920]{1,0:T(8,128)(2,1)}, bf16[40,1920]{1,0:T(8,128)(2,1)S(1)}, u32[]{:S(2)}, u32[]{:S(2)}) collective-permute-start(bf16[40,1920]{1,0:T(8,128)(2,1)} %get-tuple-element.55), channel_id=1, source_target_pairs={{0,24},{1,25},{2,26},{3,27},{4,28},{5,29},{6,30},{7,31},{8,16},{9,... | collective-permute-start | bytes 460808 | tf_op jit(solution)/shard_map/ppermute | solution.py:437
  179.1 23.5 %collective-permute-start.30 = (bf16[40,1920]{1,0:T(8,128)(2,1)}, bf16[40,1920]{1,0:T(8,128)(2,1)S(1)}, u32[]{:S(2)}, u32[]{:S(2)}) collective-permute-start(bf16[40,1920]{1,0:T(8,128)(2,1)} %get-tuple-element.56), channel_id=1, source_target_pairs={{0,28},{1,29},{2,30},{3,31},{4,24},{5,25},{6,26},{7,27},{8,20},{9,... | collective-permute-start | bytes 460808 | tf_op jit(solution)/shard_map/ppermute | solution.py:437
  183.6 18.9 %collective-permute-start.10 = (bf16[40,1920]{1,0:T(8,128)(2,1)}, bf16[40,1920]{1,0:T(8,128)(2,1)S(1)}, u32[]{:S(2)}, u32[]{:S(2)}) collective-permute-start(bf16[40,1920]{1,0:T(8,128)(2,1)} %get-tuple-element.42), channel_id=1, source_target_pairs={{0,4},{1,5},{2,6},{3,7},{4,0},{5,1},{6,2},{7,3},{8,12},{9,13},{10,... | collective-permute-start | bytes 460808 | tf_op jit(solution)/shard_map/ppermute | solution.py:437
  189.2 13.4 %collective-permute-start.11 = (bf16[40,1920]{1,0:T(8,128)(2,1)}, bf16[40,1920]{1,0:T(8,128)(2,1)S(1)}, u32[]{:S(2)}, u32[]{:S(2)}) collective-permute-start(bf16[40,1920]{1,0:T(8,128)(2,1)} %get-tuple-element.43), channel_id=1, source_target_pairs={{0,8},{1,9},{2,10},{3,11},{4,12},{5,13},{6,14},{7,15},{8,0},{9,1},... | collective-permute-start | bytes 460808 | tf_op jit(solution)/shard_map/ppermute | solution.py:437
  (42 other events, 401.0 us)

commit v2 on v1

v2 whole, which is shorter than its diff:
```python
import functools

import jax
import jax.numpy as jnp
from jax import lax
from jax.experimental import pallas as pl
from jax.experimental.pallas import tpu as pltpu
from jax.sharding import PartitionSpec as P

AXES = ("expert", "dp")
VMEM_LIMIT = 56 * 1024 * 1024
EXTRA = 128


def vmem():
    return pl.BlockSpec(memory_space=pltpu.VMEM)


def smem():
    return pl.BlockSpec(memory_space=pltpu.SMEM)


def params():
    return pltpu.CompilerParams(vmem_limit_bytes=VMEM_LIMIT)


def cost(flops, size):
    return pl.CostEstimate(flops=int(flops), bytes_accessed=int(size), transcendentals=0)


def chunks(total, step):
    return [(start, min(step, total - start)) for start in range(0, total, step)]


def find_slots(expert_count, me, ids_t):
    rows = ids_t.shape[1]
    target = lax.broadcasted_iota(jnp.int32, (expert_count, rows), 0) ^ me
    hits = [ids_t[k : k + 1, :] == target for k in range(ids_t.shape[0])]
    has = functools.reduce(jnp.logical_or, hits)
    before = lax.broadcasted_iota(jnp.int32, (rows, rows), 0) < lax.broadcasted_iota(
        jnp.int32, (rows, rows), 1
    )
    rank = jnp.dot(
        has.astype(jnp.float32).astype(jnp.bfloat16),
        before.astype(jnp.float32).astype(jnp.bfloat16),
        preferred_element_type=jnp.float32,
    )
    return hits, jnp.where(has, rank, -1.0)


def pick_kernel(expert_count, capacity, me_ref, ids_ref, weight_ref, tok_ref, grad_ref, *refs):
    outs, pick_x, pick_dy = refs[:expert_count], refs[expert_count], refs[expert_count + 1]
    rows, width = tok_ref.shape
    hits, slot_f = find_slots(expert_count, me_ref[0], ids_ref[...])
    weights = weight_ref[...].astype(jnp.float32)
    weight = jnp.zeros((expert_count, rows), jnp.float32)
    for k, hit in enumerate(hits):
        weight = jnp.where(hit, weights[k : k + 1, :], weight)
    slot = slot_f.astype(jnp.int32)
    block = 2 * capacity
    index = lax.broadcasted_iota(jnp.int32, (block, rows), 0)
    for s in range(expert_count):
        mine = slot[s : s + 1, :]
        place = slice(s * block, (s + 1) * block)
        pick_x[place, :] = jnp.where(mine == index, 1.0, 0.0).astype(jnp.bfloat16)
        taken = (mine >= 0) & (mine + capacity == index)
        pick_dy[place, :] = jnp.where(taken, weight[s : s + 1, :], 0.0).astype(jnp.bfloat16)
    for start, size in chunks(width, 512):
        part = slice(start, start + size)
        picked = jnp.dot(pick_x[...], tok_ref[:, part], preferred_element_type=jnp.float32)
        picked += jnp.dot(pick_dy[...], grad_ref[:, part], preferred_element_type=jnp.float32)
        picked = picked.astype(jnp.bfloat16)
        for s in range(expert_count):
            outs[s][:, part] = picked[s * block : (s + 1) * block]


def pick_rows(me, ids_t, weights_t, tokens, out_grad, expert_count, capacity):
    rows, width = tokens.shape
    block = jax.ShapeDtypeStruct((2 * capacity, width), jnp.bfloat16)
    picks = pltpu.VMEM((expert_count * 2 * capacity, rows), jnp.bfloat16)
    return pl.pallas_call(
        functools.partial(pick_kernel, expert_count, capacity),
        out_shape=[block] * expert_count,
        in_specs=[smem(), vmem(), vmem(), vmem(), vmem()],
        out_specs=[vmem()] * expert_count,
        scratch_shapes=[picks, picks],
        compiler_params=params(),
        cost_estimate=cost(1e9, 4e6),
        name="pick_rows",
    )(me, ids_t, weights_t, tokens, out_grad)


NT = (((1,), (1,)), ((), ()))


def expert_kernel(tiles, capacity, count, *refs):
    blocks, weights = refs[:count], refs[count : count + 6]
    parcel_ref, keep_ref, send_ref, mine_ref = refs[count + 6 : count + 10]
    gate_w, up_w, total = refs[count + 10 :]
    gates, ups, downs = weights[0:2], weights[2:4], weights[4:6]
    step = pl.program_id(0)
    tile, units = gates[0].shape
    rows = count * capacity
    half = rows // 2
    width = tiles * tile
    x_at = pl.multiple_of(step * tile, 128)
    dy_at = pl.multiple_of(width + step * tile, 128)

    @pl.when(step == 0)
    def _():
        total[...] = jnp.zeros_like(total)

    for i, ref in enumerate(blocks):
        value = ref[...].astype(jnp.float32)
        place = slice(i * capacity, (i + 1) * capacity)
        parcel_ref[place, pl.ds(x_at, tile)] = value[:capacity].astype(jnp.bfloat16)
        parcel_ref[place, pl.ds(dy_at, tile)] = value[capacity:].astype(jnp.bfloat16)
    x = parcel_ref[:, pl.ds(x_at, tile)]
    dy = parcel_ref[:, pl.ds(dy_at, tile)]
    for core in range(2):
        gate_w[core, step] = gates[core][...]
        up_w[core, step] = ups[core][...]
        total[core, 0] += jnp.dot(x, gates[core][...], preferred_element_type=jnp.float32)
        total[core, 1] += jnp.dot(x, ups[core][...], preferred_element_type=jnp.float32)
        total[core, 2] += lax.dot_general(
            dy, downs[core][...], NT, preferred_element_type=jnp.float32
        )

    @pl.when(step == tiles - 1)
    def _():
        route = jnp.zeros((rows, 1), jnp.float32)
        unit_refs = (mine_ref, parcel_ref.at[:, 2 * width :])
        for core, out in enumerate(unit_refs):
            gate_value = total[core, 0]
            up_value = total[core, 1]
            back = total[core, 2]
            sigmoid = jax.nn.sigmoid(gate_value)
            silu = gate_value * sigmoid
            hidden = (silu * up_value).astype(jnp.bfloat16)
            d_gate = back * up_value * sigmoid * (1.0 + gate_value * (1.0 - sigmoid))
            out[:, 0:units] = d_gate.astype(jnp.bfloat16)
            out[:, units : 2 * units] = (back * silu).astype(jnp.bfloat16)
            out[:, 2 * units :] = hidden
            route += jnp.sum(hidden.astype(jnp.float32) * back, axis=1, keepdims=True)
        route = jnp.broadcast_to(route, (rows, EXTRA)).astype(jnp.bfloat16)
        keep_ref[:, width:] = route[:half]
        send_ref[:, width:] = route[half:]
        for at in range(tiles):
            part = jnp.zeros((rows, tile), jnp.float32)
            for core, out in enumerate(unit_refs):
                part += lax.dot_general(
                    out[:, 0:units], gate_w[core, at], NT, preferred_element_type=jnp.float32
                )
                part += lax.dot_general(
                    out[:, units : 2 * units],
                    up_w[core, at],
                    NT,
                    preferred_element_type=jnp.float32,
                )
            part = part.astype(jnp.bfloat16)
            keep_ref[:, at * tile : (at + 1) * tile] = part[:half]
            send_ref[:, at * tile : (at + 1) * tile] = part[half:]


def run_expert(blocks, weights, capacity):
    width = blocks[0].shape[1]
    units = weights[0].shape[1]
    count = len(blocks)
    rows = count * capacity
    tile = width // 4 if width % 512 == 0 else width
    tiles = width // tile
    out = jax.ShapeDtypeStruct((rows // 2, width + EXTRA), jnp.bfloat16)
    unit_rows = jax.ShapeDtypeStruct((rows, 3 * units), jnp.bfloat16)
    parcel = jax.ShapeDtypeStruct((rows, 2 * width + 3 * units), jnp.bfloat16)

    def whole(shape):
        return pl.BlockSpec(shape, lambda i: (0, 0))

    return pl.pallas_call(
        functools.partial(expert_kernel, tiles, capacity, count),
        grid=(tiles,),
        out_shape=[parcel, out, out, unit_rows],
        in_specs=[pl.BlockSpec((2 * capacity, tile), lambda i: (0, i))] * count
        + [pl.BlockSpec((tile, units), lambda i: (i, 0))] * 4
        + [pl.BlockSpec((units, tile), lambda i: (0, i))] * 2,
        out_specs=[
            whole(parcel.shape),
            whole(out.shape),
            whole(out.shape),
            whole(unit_rows.shape),
        ],
        scratch_shapes=[
            pltpu.VMEM((2, tiles, tile, units), jnp.bfloat16),
            pltpu.VMEM((2, tiles, tile, units), jnp.bfloat16),
            pltpu.VMEM((2, 3, rows, units), jnp.float32),
        ],
        compiler_params=params(),
        cost_estimate=cost(20 * rows * width * units, 12 * width * units + 10 * rows * width),
        name="run_expert",
    )(*blocks, *weights)


def finish_kernel(capacity, keep_ref, far_ref, *outs):
    half = (far_ref.shape[1] - EXTRA) // 2

    def summed(part):
        return keep_ref[:, part].astype(jnp.float32) + far_ref[:, part].astype(jnp.float32)

    for h in range(2):
        for start, size in chunks(half, 896):
            value = summed(slice(h * half + start, h * half + start + size))
            for i, out in enumerate(outs):
                out[h * capacity : (h + 1) * capacity, start : start + size] = value[
                    i * capacity : (i + 1) * capacity
                ].astype(jnp.bfloat16)
    value = summed(slice(2 * half, 2 * half + EXTRA))
    for i, out in enumerate(outs):
        block = value[i * capacity : (i + 1) * capacity].astype(jnp.bfloat16)
        out[0:capacity, half:] = block
        out[capacity:, half:] = block


def finish(keep, far, capacity):
    rows, width = far.shape
    count = rows // capacity
    half = (width - EXTRA) // 2
    block = jax.ShapeDtypeStruct((2 * capacity, half + EXTRA), jnp.bfloat16)
    return pl.pallas_call(
        functools.partial(finish_kernel, capacity),
        out_shape=[block] * count,
        in_specs=[vmem()] * 2,
        out_specs=[vmem()] * count,
        compiler_params=params(),
        cost_estimate=cost(2 * rows * width, 6 * rows * width),
        name="finish",
    )(keep, far)


def weight_kernel(group_rows, *refs):
    count = len(group_rows)
    x_refs, dy_refs = refs[:count], refs[count : 2 * count]
    unit_refs = refs[2 * count : 5 * count]
    gate_ref, up_ref, down_ref, all_units, x_rows, dy_rows = refs[5 * count :]
    units = gate_ref.shape[1]

    @pl.when(pl.program_id(0) == 0)
    def _():
        at = 0
        for g, rows in enumerate(group_rows):
            for part in range(3):
                all_units[at : at + rows, part * units : (part + 1) * units] = unit_refs[
                    3 * g + part
                ][...]
            at += rows

    at = 0
    for rows, x_ref, dy_ref in zip(group_rows, x_refs, dy_refs):
        x_rows[at : at + rows, :] = x_ref[...]
        dy_rows[at : at + rows, :] = dy_ref[...]
        at += rows
    contract = (((0,), (0,)), ((), ()))
    grads = lax.dot_general(
        x_rows[...], all_units[:, 0 : 2 * units], contract, preferred_element_type=jnp.float32
    )
    gate_ref[...] = grads[:, :units].astype(jnp.bfloat16)
    up_ref[...] = grads[:, units:].astype(jnp.bfloat16)
    down_ref[...] = lax.dot_general(
        all_units[:, 2 * units :], dy_rows[...], contract, preferred_element_type=jnp.float32
    ).astype(jnp.bfloat16)


def weight_grads(parcels, units, width):
    hidden_units = (parcels[0].shape[1] - 2 * width) // 3
    group_rows = [p.shape[0] for p in parcels]
    total = sum(group_rows)
    tile = 512 if width % 512 == 0 else width
    tiles = width // tile
    unit_at = 2 * width // hidden_units
    unit_args, unit_specs = [], []
    for parcel, own in zip(parcels, units):
        shape = (parcel.shape[0], hidden_units)
        first = unit_at if own is None else 0
        for part in range(3):
            unit_args.append(parcel if own is None else own)
            unit_specs.append(pl.BlockSpec(shape, lambda i, at=first + part: (0, at)))
    return pl.pallas_call(
        functools.partial(weight_kernel, group_rows),
        grid=(tiles,),
        out_shape=[
            jax.ShapeDtypeStruct((width, hidden_units), jnp.bfloat16),
            jax.ShapeDtypeStruct((width, hidden_units), jnp.bfloat16),
            jax.ShapeDtypeStruct((hidden_units, width), jnp.bfloat16),
        ],
        in_specs=[pl.BlockSpec((rows, tile), lambda i: (0, i)) for rows in group_rows]
        + [pl.BlockSpec((rows, tile), lambda i: (0, tiles + i)) for rows in group_rows]
        + unit_specs,
        out_specs=[
            pl.BlockSpec((tile, hidden_units), lambda i: (i, 0)),
            pl.BlockSpec((tile, hidden_units), lambda i: (i, 0)),
            pl.BlockSpec((hidden_units, tile), lambda i: (0, i)),
        ],
        scratch_shapes=[
            pltpu.VMEM((total, 3 * hidden_units), jnp.bfloat16),
            pltpu.VMEM((total, tile), jnp.bfloat16),
            pltpu.VMEM((total, tile), jnp.bfloat16),
        ],
        compiler_params=params(),
        cost_estimate=cost(
            6 * total * width * hidden_units, 4 * total * width + 6 * width * hidden_units
        ),
        name="weight_grads",
    )(*parcels, *parcels, *unit_args)


def combine_kernel(expert_count, capacity, me_ref, ids_ref, weight_ref, *refs):
    blocks = refs[:expert_count]
    tok_ref, route_ref, slots, values = refs[expert_count:]
    routes, rows = ids_ref.shape
    half = blocks[0].shape[1] - EXTRA
    hits, slot_t = find_slots(expert_count, me_ref[0], ids_ref[...])
    slots[...] = jnp.full(slots.shape, -1.0, jnp.float32)
    slots[0:expert_count, :] = slot_t
    slot = slots[...].T.astype(jnp.int32)
    lane = lax.broadcasted_iota(jnp.int32, (rows, slots.shape[0]), 1)
    index = lax.broadcasted_iota(jnp.int32, (rows, 2 * capacity), 1)
    picks = []
    for s in range(expert_count):
        column = slot[:, s : s + 1]
        low = jnp.where(column == index, 1.0, 0.0)
        high = jnp.where((column >= 0) & (column + capacity == index), 1.0, 0.0)
        picks.append(jnp.concatenate([low, high], axis=0).astype(jnp.bfloat16))
    for start, size in chunks(half, 896):
        part = jnp.zeros((2 * rows, size), jnp.float32)
        for s in range(expert_count):
            part += jnp.dot(
                picks[s], blocks[s][:, start : start + size], preferred_element_type=jnp.float32
            )
        tok_ref[:, start : start + size] = part[:rows].astype(jnp.bfloat16)
        tok_ref[:, half + start : half + start + size] = part[rows:].astype(jnp.bfloat16)
    value = jnp.zeros((rows, slots.shape[0]), jnp.float32)
    for s in range(expert_count):
        found = jnp.dot(picks[s], blocks[s][:, half:], preferred_element_type=jnp.float32)
        value = jnp.where(lane == s, found[:rows, 0:1], value)
    values[...] = value.T
    value_t = values[0:expert_count, :]
    weights = weight_ref[...].astype(jnp.float32)
    found = [
        jnp.sum(jnp.where(hit, value_t, 0.0), axis=0, keepdims=True) for hit in hits
    ]
    route_ref[...] = (jnp.concatenate(found, axis=0) / weights).astype(jnp.bfloat16)


def combine(me, ids_t, weights_t, blocks, capacity):
    routes, rows = ids_t.shape
    half = blocks[0].shape[1] - EXTRA
    return pl.pallas_call(
        functools.partial(combine_kernel, len(blocks), capacity),
        out_shape=[
            jax.ShapeDtypeStruct((rows, 2 * half), jnp.bfloat16),
            jax.ShapeDtypeStruct((routes, rows), jnp.bfloat16),
        ],
        in_specs=[smem()] + [vmem()] * (2 + len(blocks)),
        out_specs=[vmem(), vmem()],
        scratch_shapes=[pltpu.VMEM((128, rows), jnp.float32), pltpu.VMEM((128, rows), jnp.float32)],
        compiler_params=params(),
        cost_estimate=cost(1e9, 3e6),
        name="combine",
    )(me, ids_t, weights_t, *blocks)


def source_groups(expert_count):
    half, three = expert_count // 2, 3 * expert_count // 4
    return [
        list(range(half)),
        list(range(three, expert_count)),
        list(range(half, three)),
    ]


def after(*values):
    return lax.optimization_barrier(values)


def shards(tokens, out_grad, expert_ids, route_weights, w_gate, w_up, w_down):
    expert_count = lax.axis_size("expert")
    group_count = lax.axis_size("dp")
    device_count = expert_count * group_count
    capacity = 5 * tokens.shape[0] // (4 * expert_count)
    if (2 * capacity) % 8:
        capacity = -(-capacity // 8) * 8
    me = lax.axis_index("expert").astype(jnp.int32).reshape(1)
    ids_t, weights_t = expert_ids.T, route_weights.T

    def swap(value, distance):
        return lax.ppermute(value, AXES, [(i, i ^ distance) for i in range(device_count)])

    near, first, second = source_groups(expert_count)
    got, crossed, back = {}, {}, {}
    parcels, units = [], []

    def fetch(group, source):
        for s in group:
            got[s] = swap(source[s], s * group_count) if s else source[s]

    def cross(group):
        for s in group:
            crossed[s] = swap(got[s], 2)

    def work(group):
        parcel, keep, send, mine = run_expert(
            [got[s] for s in group] + [crossed[s] for s in group], weights, capacity
        )
        parcels.append(parcel)
        units.append(mine)
        return parcel, keep, send

    def ready(group, keep, far):
        return dict(zip(group, finish(keep, far, capacity)))

    def give(blocks):
        for s, block in blocks.items():
            back[s] = swap(block, s * group_count) if s else block

    weights = []
    for own in (w_gate[0], w_up[0], w_down[0]):
        weights += [own, swap(own, 1)]
    blocks = list(pick_rows(me, ids_t, weights_t, tokens, out_grad, expert_count, capacity))
    fetch(first, blocks)
    weights, close = after(weights, {s: blocks[s] for s in near})
    fetch(near, close)
    cross(near[:2])
    got, crossed, later = after(got, crossed, {s: blocks[s] for s in second})
    fetch(second, later)
    cross(near[2:])
    cross(first)
    near_parcel, near_keep, near_send = work(near)
    near_far = swap(near_send, 2)
    first_parcel, first_keep, first_send = work(first)
    first_far = swap(first_send, 2)
    moved = {s: got[s] for s in second}
    near_keep, first_keep, moved = after(near_keep, first_keep, moved)
    got.update(moved)
    cross(second)
    near_ready = ready(near, near_keep, near_far)
    first_ready = ready(first, first_keep, first_far)
    moved = {s: crossed[s] for s in second}
    near_ready, first_ready, moved = after(near_ready, first_ready, moved)
    crossed.update(moved)
    give(first_ready)
    give(near_ready)
    second_parcel, second_keep, second_send = work(second)
    back, second_send, parcels = after(back, second_send, parcels)
    second_far = swap(second_send, 2)
    others = [swap(parcel, 1) for parcel in parcels]
    second_ready = ready(second, second_keep, second_far)
    others, second_ready = after(others, second_ready)
    give(second_ready)
    grads = weight_grads(parcels + others, units + [None] * 3, tokens.shape[1])
    grads, back = after(list(grads), back)
    grad_gate, grad_up, grad_down = grads
    grad_tokens, grad_route_t = combine(
        me, ids_t, weights_t, [back[s] for s in range(expert_count)], capacity
    )
    return (grad_tokens, grad_route_t.T, grad_gate[None], grad_up[None], grad_down[None])


def solution(mesh):
    rows = P(AXES, None)
    columns = P("expert", None, "dp")
    return jax.shard_map(
        shards,
        mesh=mesh,
        in_specs=(rows, rows, rows, rows, columns, columns, P("expert", "dp", None)),
        out_specs=(rows, rows, columns, columns, P("expert", "dp", None)),
        check_vma=False,
    )
```

time: 211 us -> 164 us (0.78)
  waiting for transfers between devices: 88.1 us -> 54.6 us
  Pallas kernels: 67.9 us -> 56.7 us
  local copies, waits for them, and re-layouts: 15.6 us -> 5.92 us
  starting transfers between devices: 37.3 us -> 45.2 us
    ppermute x31, waiting for transfers between devices: 88.1 us -> 54.6 us  [swap(): lax.ppermute(value, AXES, [(i, i ^ distance) for i in range(device_count)])]
    unnamed x73 -> x64, local copies, waits for them, and re-layouts: 15.6 us -> 5.92 us
    pallas_call x10 -> x4, Pallas kernels: 50.6 us -> 41.4 us  [the longest x3 31.3 us: run_expert(): pl.pallas_call(functools.partial(expert_kernel, tiles, capacity, count),...]
    ppermute x31, starting transfers between devices: 37.3 us -> 45.2 us  [swap(): lax.ppermute(value, AXES, [(i, i ^ distance) for i in range(device_count)])]
  transfers between devices with their start and end apart: 31 -> 31, of which waited for: 14 -> 11; matrix products, arithmetic and copies ran while one was open for 0% -> 0% of each run, Pallas kernels for 26% -> 32%
where the time goes in v2:
time: 164 us; the launch traced here: 163 us
  Pallas kernels  56.7 us (35%)
  waiting for transfers between devices  54.6 us (33%)
  starting transfers between devices  45.2 us (28%)
  local copies, waits for them, and re-layouts  5.92 us (4%)
    ppermute x31, waiting for transfers between devices, swap(): lax.ppermute(value, AXES, [(i, i ^ distance) for i in range(device_count)])  54.6 us
    ppermute x31, starting transfers between devices, swap(): lax.ppermute(value, AXES, [(i, i ^ distance) for i in range(device_count)])  45.2 us
    pallas_call x3, Pallas kernels, run_expert(): pl.pallas_call(functools.partial(expert_kernel, tiles, capacity, count),...  31.3 us
    pallas_call x1, Pallas kernels, weight_grads(): pl.pallas_call(functools.partial(weight_kernel, group_rows), grid=(tiles,...  10.1 us
    pallas_call x3, Pallas kernels, finish(): pl.pallas_call(functools.partial(finish_kernel, capacity), out_shape=[blo...  6.02 us
    unnamed x64, local copies, waits for them, and re-layouts  5.92 us
    pallas_call x1, Pallas kernels, combine(): pl.pallas_call(functools.partial(combine_kernel, len(blocks), capacity),...  4.95 us
    pallas_call x1, Pallas kernels, pick_rows(): pl.pallas_call(functools.partial(pick_kernel, expert_count, capacity), ou...  4.32 us
  transfers between devices with their start and end apart: 31, of which 11 were waited for; matrix products, arithmetic and copies ran while one was open for 0% of the time, Pallas kernels for 32%

profile of v2, /device:TPU:0, one launch (start us, length us, event | category | flops | bytes accessed | tf_op | source)
XLA Modules:
  0.0 163.3 jit_solution(17622825095825571016)
XLA Ops:
  1.7 4.3 %pick_rows.1 = (bf16[40,3584]{1,0:T(8,128)(2,1)}, bf16[40,3584]{1,0:T(8,128)(2,1)}, bf16[40,3584]{1,0:T(8,128)(2,1)}, bf16[40,3584]{1,0:T(8,128)(2,1)}, bf16[40,...) custom-call(s32[1]{0:T(128)} %bitcast.me_ref, ...), custom_call_target="tpu_custom_call" | custom-call | flops 1000000000 | bytes 4000000 | tf_op jit(solution)/shard_map/pick_rows/pallas_call | solution.py:81
  6.0 4.7 %collective-permute-start.6 = (bf16[40,3584]{1,0:T(8,128)(2,1)}, bf16[40,3584]{1,0:T(8,128)(2,1)S(1)}, u32[]{:S(2)}, u32[]{:S(2)}) collective-permute-start(bf16[40,3584]{1,0:T(8,128)(2,1)} %get-tuple-element.104), channel_id=1, source_target_pairs={{0,24},{1,25},{2,26},{3,27},{4,28},{5,29},{6,30},{7,31},{8,16},{9,... | collective-permute-start | bytes 860168 | tf_op jit(solution)/shard_map/ppermute | solution.py:395
  10.7 2.4 %collective-permute-start.3 = (bf16[40,3584]{1,0:T(8,128)(2,1)}, bf16[40,3584]{1,0:T(8,128)(2,1)S(1)}, u32[]{:S(2)}, u32[]{:S(2)}) collective-permute-start(bf16[40,3584]{1,0:T(8,128)(2,1)} %get-tuple-element.101), channel_id=1, source_target_pairs={{0,4},{1,5},{2,6},{3,7},{4,0},{5,1},{6,2},{7,3},{8,12},{9,13},{10,... | collective-permute-start | bytes 860168 | tf_op jit(solution)/shard_map/ppermute | solution.py:395
  13.0 3.5 %collective-permute-start.7 = (bf16[40,3584]{1,0:T(8,128)(2,1)}, bf16[40,3584]{1,0:T(8,128)(2,1)S(1)}, u32[]{:S(2)}, u32[]{:S(2)}) collective-permute-start(bf16[40,3584]{1,0:T(8,128)(2,1)} %get-tuple-element.105), channel_id=1, source_target_pairs={{0,28},{1,29},{2,30},{3,31},{4,24},{5,25},{6,26},{7,27},{8,20},{9,... | collective-permute-start | bytes 860168 | tf_op jit(solution)/shard_map/ppermute | solution.py:395
  16.6 3.0 %collective-permute-start.5 = (bf16[40,3584]{1,0:T(8,128)(2,1)}, bf16[40,3584]{1,0:T(8,128)(2,1)S(1)}, u32[]{:S(2)}, u32[]{:S(2)}) collective-permute-start(bf16[40,3584]{1,0:T(8,128)(2,1)} %get-tuple-element.103), channel_id=1, source_target_pairs={{0,12},{1,13},{2,14},{3,15},{4,8},{5,9},{6,10},{7,11},{8,4},{9,5},... | collective-permute-start | bytes 860168 | tf_op jit(solution)/shard_map/ppermute | solution.py:395
  21.1 5.5 %collective-permute-done.3.refs_1_ = bf16[40,3584]{1,0:T(8,128)(2,1)S(1)} collective-permute-done((bf16[40,3584]{1,0:T(8,128)(2,1)}, bf16[40,3584]{1,0:T(8,128)(2,1)S(1)}, u32[]{:S(2)}, u32[]{:S(2)}) %collective-permute-start.3) | collective-permute-done | bytes 286752 | tf_op jit(solution)/shard_map/ppermute | solution.py:395
  28.2 2.5 %collective-permute-done.4.refs_2_ = bf16[40,3584]{1,0:T(8,128)(2,1)S(1)} collective-permute-done((bf16[40,3584]{1,0:T(8,128)(2,1)}, bf16[40,3584]{1,0:T(8,128)(2,1)S(1)}, u32[]{:S(2)}, u32[]{:S(2)}) %collective-permute-start.4) | collective-permute-done | bytes 286752 | tf_op jit(solution)/shard_map/ppermute | solution.py:395
  30.8 9.4 %collective-permute-done.5.refs_3_ = bf16[40,3584]{1,0:T(8,128)(2,1)S(1)} collective-permute-done((bf16[40,3584]{1,0:T(8,128)(2,1)}, bf16[40,3584]{1,0:T(8,128)(2,1)S(1)}, u32[]{:S(2)}, u32[]{:S(2)}) %collective-permute-start.5) | collective-permute-done | bytes 286752 | tf_op jit(solution)/shard_map/ppermute | solution.py:395
  44.3 5.7 %collective-permute-done.10.refs_6_ = bf16[40,3584]{1,0:T(8,128)(2,1)S(1)} collective-permute-done((bf16[40,3584]{1,0:T(8,128)(2,1)S(1)}, bf16[40,3584]{1,0:T(8,128)(2,1)S(1)}, u32[]{:S(2)}, u32[]{:S(2)}) %collective-permute-start.10) | collective-permute-done | bytes 286752 | tf_op jit(solution)/shard_map/ppermute | solution.py:395
  50.0 6.1 %collective-permute-done.11.refs_7_ = bf16[40,3584]{1,0:T(8,128)(2,1)S(1)} collective-permute-done((bf16[40,3584]{1,0:T(8,128)(2,1)S(1)}, bf16[40,3584]{1,0:T(8,128)(2,1)S(1)}, u32[]{:S(2)}, u32[]{:S(2)}) %collective-permute-start.11) | collective-permute-done | bytes 286752 | tf_op jit(solution)/shard_map/ppermute | solution.py:395
  56.9 11.4 %run_expert.3 = (bf16[160,7936]{1,0:T(8,128)(2,1)}, bf16[80,3712]{1,0:T(8,128)(2,1)}, bf16[80,3712]{1,0:T(8,128)(2,1)}, bf16[160,768]{1,0:T(8,128)(2,1)}) custom-call(bf16[40,3584]{1,0:T(8,128)(2,1)} %get-tuple-element.108.refs_0_, bf16[40,3584]{1,0:T(8,128)(2,1)} %copy-done.8, bf16[40,3584]{1,0:T(8,128)(2,1)} %copy-done.9, bf16[40,3584]{1,0:T(8,128)(2,1)} %copy-done.10, ...), custom_call_target="tpu_custom_call" | custom-call | flops 2936012800 | bytes 16744448 | tf_op jit(solution)/shard_map/run_expert/pallas_call | solution.py:179
  69.9 5.8 %collective-permute-start.14 = (bf16[40,3584]{1,0:T(8,128)(2,1)S(1)}, bf16[40,3584]{1,0:T(8,128)(2,1)S(1)}, u32[]{:S(2)}, u32[]{:S(2)}) collective-permute-start(bf16[40,3584]{1,0:T(8,128)(2,1)S(1)} %copy-done.24), channel_id=1, source_target_pairs={{0,16},{1,17},{2,18},{3,19},{4,20},{5,21},{6,22},{7,23},{8,24},{9,... | collective-permute-start | bytes 860168 | tf_op jit(solution)/shard_map/ppermute | solution.py:395
  78.2 9.9 %run_expert.4 = (bf16[80,7936]{1,0:T(8,128)(2,1)}, bf16[40,3712]{1,0:T(8,128)(2,1)}, bf16[40,3712]{1,0:T(8,128)(2,1)}, bf16[80,768]{1,0:T(8,128)(2,1)}) custom-call(bf16[40,3584]{1,0:T(8,128)(2,1)} %copy-done.15, bf16[40,3584]{1,0:T(8,128)(2,1)} %copy-done.16, bf16[40,3584]{1,0:T(8,128)(2,1)} %copy-done.21, bf16[40,3584]{1,0:T(8,128)(2,1)} %copy-done.22, ...), custom_call_target="tpu_custom_call" | custom-call | flops 1468006400 | bytes 13877248 | tf_op jit(solution)/shard_map/run_expert/pallas_call | solution.py:179
  90.6 5.9 %collective-permute-done.15.refs_1_ = bf16[40,3584]{1,0:T(8,128)(2,1)S(1)} collective-permute-done((bf16[40,3584]{1,0:T(8,128)(2,1)S(1)}, bf16[40,3584]{1,0:T(8,128)(2,1)S(1)}, u32[]{:S(2)}, u32[]{:S(2)}) %collective-permute-start.15) | collective-permute-done | bytes 286752 | tf_op jit(solution)/shard_map/ppermute | solution.py:395
  101.9 2.3 %finish.3 = (bf16[40,1920]{1,0:T(8,128)(2,1)}, bf16[40,1920]{1,0:T(8,128)(2,1)}, bf16[40,1920]{1,0:T(8,128)(2,1)}, bf16[40,1920]{1,0:T(8,128)(2,1)}) custom-call(bf16[80,3712]{1,0:T(8,128)(2,1)} %get-tuple-element.126.keep_ref, bf16[80,3712]{1,0:T(8,128)(2,1)} %copy-done.5), custom_call_target="tpu_custom_call" | custom-call | flops 593920 | bytes 1781760 | tf_op jit(solution)/shard_map/finish/pallas_call | solution.py:228
  106.2 4.0 %collective-permute-done.19.refs_3_ = bf16[40,3584]{1,0:T(8,128)(2,1)S(1)} collective-permute-done((bf16[40,3584]{1,0:T(8,128)(2,1)S(1)}, bf16[40,3584]{1,0:T(8,128)(2,1)S(1)}, u32[]{:S(2)}, u32[]{:S(2)}) %collective-permute-start.19) | collective-permute-done | bytes 286752 | tf_op jit(solution)/shard_map/ppermute | solution.py:395
  110.6 3.1 %collective-permute-start.22 = (bf16[40,1920]{1,0:T(8,128)(2,1)}, bf16[40,1920]{1,0:T(8,128)(2,1)S(1)}, u32[]{:S(2)}, u32[]{:S(2)}) collective-permute-start(bf16[40,1920]{1,0:T(8,128)(2,1)} %get-tuple-element.141), channel_id=1, source_target_pairs={{0,12},{1,13},{2,14},{3,15},{4,8},{5,9},{6,10},{7,11},{8,4},{9,5},... | collective-permute-start | bytes 460808 | tf_op jit(solution)/shard_map/ppermute | solution.py:395
  113.8 3.5 %collective-permute-start.24 = (bf16[40,1920]{1,0:T(8,128)(2,1)}, bf16[40,1920]{1,0:T(8,128)(2,1)S(1)}, u32[]{:S(2)}, u32[]{:S(2)}) collective-permute-start(bf16[40,1920]{1,0:T(8,128)(2,1)} %get-tuple-element.143), channel_id=1, source_target_pairs={{0,28},{1,29},{2,30},{3,31},{4,24},{5,25},{6,26},{7,27},{8,20},{9,... | collective-permute-start | bytes 460808 | tf_op jit(solution)/shard_map/ppermute | solution.py:395
  117.4 10.0 %run_expert.5 = (bf16[80,7936]{1,0:T(8,128)(2,1)}, bf16[40,3712]{1,0:T(8,128)(2,1)}, bf16[40,3712]{1,0:T(8,128)(2,1)}, bf16[80,768]{1,0:T(8,128)(2,1)}) custom-call(bf16[40,3584]{1,0:T(8,128)(2,1)} %copy-done.17, bf16[40,3584]{1,0:T(8,128)(2,1)} %copy-done.18, bf16[40,3584]{1,0:T(8,128)(2,1)} %copy-done.19, bf16[40,3584]{1,0:T(8,128)(2,1)} %copy-done.20, ...), custom_call_target="tpu_custom_call" | custom-call | flops 1468006400 | bytes 13877248 | tf_op jit(solution)/shard_map/run_expert/pallas_call | solution.py:179
  129.3 9.1 %collective-permute-done.28.far_ref = bf16[40,3712]{1,0:T(8,128)(2,1)S(1)} collective-permute-done((bf16[40,3712]{1,0:T(8,128)(2,1)}, bf16[40,3712]{1,0:T(8,128)(2,1)S(1)}, u32[]{:S(2)}, u32[]{:S(2)}) %collective-permute-start.28) | collective-permute-done | bytes 296992 | tf_op jit(solution)/shard_map/ppermute | solution.py:395
  141.2 4.0 %collective-permute-start.30 = (bf16[40,1920]{1,0:T(8,128)(2,1)}, bf16[40,1920]{1,0:T(8,128)(2,1)S(1)}, u32[]{:S(2)}, u32[]{:S(2)}) collective-permute-start(bf16[40,1920]{1,0:T(8,128)(2,1)} %get-tuple-element.171), channel_id=1, source_target_pairs={{0,20},{1,21},{2,22},{3,23},{4,16},{5,17},{6,18},{7,19},{8,28},{9,... | collective-permute-start | bytes 460808 | tf_op jit(solution)/shard_map/ppermute | solution.py:395
  145.2 10.1 %weight_grads.1 = (bf16[3584,256]{1,0:T(8,128)(2,1)}, bf16[3584,256]{1,0:T(8,128)(2,1)}, bf16[256,3584]{1,0:T(8,128)(2,1)}) custom-call(bf16[160,7936]{1,0:T(8,128)(2,1)} %get-tuple-element.150.refs_0_.refs_6_, bf16[80,7936]{1,0:T(8,128)(2,1)} %get-tuple-element.151.refs_1_.refs_7_, bf16[80,7936]{1,0:T(8,128)(2,1)} %get-tuple-element.152.refs_2_.refs_8_, ...), custom_call_target="tpu_custom_call" | custom-call | flops 3523215360 | bytes 14680064 | tf_op jit(solution)/shard_map/weight_grads/pallas_call | solution.py:286
  155.3 2.4 %collective-permute-done.30.refs_5_ = bf16[40,1920]{1,0:T(8,128)(2,1)S(1)} collective-permute-done((bf16[40,1920]{1,0:T(8,128)(2,1)}, bf16[40,1920]{1,0:T(8,128)(2,1)S(1)}, u32[]{:S(2)}, u32[]{:S(2)}) %collective-permute-start.30) | collective-permute-done | bytes 153632 | tf_op jit(solution)/shard_map/ppermute | solution.py:395
  158.4 4.9 %combine.1 = (bf16[128,3584]{1,0:T(8,128)(2,1)}, bf16[8,128]{1,0:T(8,128)(2,1)}) custom-call(s32[1]{0:T(128)} %bitcast.me_ref, s32[8,128]{1,0:T(8,128)} %bitcast.26, bf16[8,128]{1,0:T(8,128)(2,1)} %bitcast.28, bf16[40,1920]{1,0:T(8,128)(2,1)} %get-tuple-element.174.refs_0_, bf16[40,1920]{1,0:T(8,128)(2,1)} %copy-done.25, bf16[40,1920]{1,0:T(8,128)(2,1)} %copy-done.26, ...), custom_call_target="tpu_custom_call" | custom-call | flops 1000000000 | bytes 3000000 | tf_op jit(solution)/shard_map/combine/pallas_call | solution.py:356
  (111 shorter events, 28.8 us)
Async XLA Ops:
  6.0 13.6 %collective-permute-start.6 = (bf16[40,3584]{1,0:T(8,128)(2,1)}, bf16[40,3584]{1,0:T(8,128)(2,1)S(1)}, u32[]{:S(2)}, u32[]{:S(2)}) collective-permute-start(bf16[40,3584]{1,0:T(8,128)(2,1)} %get-tuple-element.104), channel_id=1, source_target_pairs={{0,24},{1,25},{2,26},{3,27},{4,28},{5,29},{6,30},{7,31},{8,16},{9,... | collective-permute-start | bytes 860168 | tf_op jit(solution)/shard_map/ppermute | solution.py:395
  10.7 15.8 %collective-permute-start.3 = (bf16[40,3584]{1,0:T(8,128)(2,1)}, bf16[40,3584]{1,0:T(8,128)(2,1)S(1)}, u32[]{:S(2)}, u32[]{:S(2)}) collective-permute-start(bf16[40,3584]{1,0:T(8,128)(2,1)} %get-tuple-element.101), channel_id=1, source_target_pairs={{0,4},{1,5},{2,6},{3,7},{4,0},{5,1},{6,2},{7,3},{8,12},{9,13},{10,... | collective-permute-start | bytes 860168 | tf_op jit(solution)/shard_map/ppermute | solution.py:395
  13.0 15.2 %collective-permute-start.7 = (bf16[40,3584]{1,0:T(8,128)(2,1)}, bf16[40,3584]{1,0:T(8,128)(2,1)S(1)}, u32[]{:S(2)}, u32[]{:S(2)}) collective-permute-start(bf16[40,3584]{1,0:T(8,128)(2,1)} %get-tuple-element.105), channel_id=1, source_target_pairs={{0,28},{1,29},{2,30},{3,31},{4,24},{5,25},{6,26},{7,27},{8,20},{9,... | collective-permute-start | bytes 860168 | tf_op jit(solution)/shard_map/ppermute | solution.py:395
  16.6 14.2 %collective-permute-start.4 = (bf16[40,3584]{1,0:T(8,128)(2,1)}, bf16[40,3584]{1,0:T(8,128)(2,1)S(1)}, u32[]{:S(2)}, u32[]{:S(2)}) collective-permute-start(bf16[40,3584]{1,0:T(8,128)(2,1)} %get-tuple-element.102), channel_id=1, source_target_pairs={{0,8},{1,9},{2,10},{3,11},{4,12},{5,13},{6,14},{7,15},{8,0},{9,1},... | collective-permute-start | bytes 860168 | tf_op jit(solution)/shard_map/ppermute | solution.py:395
  16.6 23.6 %collective-permute-start.5 = (bf16[40,3584]{1,0:T(8,128)(2,1)}, bf16[40,3584]{1,0:T(8,128)(2,1)S(1)}, u32[]{:S(2)}, u32[]{:S(2)}) collective-permute-start(bf16[40,3584]{1,0:T(8,128)(2,1)} %get-tuple-element.103), channel_id=1, source_target_pairs={{0,12},{1,13},{2,14},{3,15},{4,8},{5,9},{6,10},{7,11},{8,4},{9,5},... | collective-permute-start | bytes 860168 | tf_op jit(solution)/shard_map/ppermute | solution.py:395
  19.6 20.6 %collective-permute-start.8 = (bf16[40,3584]{1,0:T(8,128)(2,1)}, bf16[40,3584]{1,0:T(8,128)(2,1)S(1)}, u32[]{:S(2)}, u32[]{:S(2)}) collective-permute-start(bf16[40,3584]{1,0:T(8,128)(2,1)} %get-tuple-element.108.refs_0_), channel_id=1, source_target_pairs={{0,2},{1,3},{2,0},{3,1},{4,6},{5,7},{6,4},{7,5},{8,10},{9,11},{10,... | collective-permute-start | bytes 860168 | tf_op jit(solution)/shard_map/ppermute | solution.py:395
  26.5 13.6 %collective-permute-start.9 = (bf16[40,3584]{1,0:T(8,128)(2,1)S(1)}, bf16[40,3584]{1,0:T(8,128)(2,1)S(1)}, u32[]{:S(2)}, u32[]{:S(2)}) collective-permute-start(bf16[40,3584]{1,0:T(8,128)(2,1)S(1)} %collective-permute-done.3.refs_1_), channel_id=1, source_target_pairs={{0,2},{1,3},{2,0},{3,1},{4,6},{5,7},{6,4},{7,5},{8,10},{9,11},{10,... | collective-permute-start | bytes 860168 | tf_op jit(solution)/shard_map/ppermute | solution.py:395
  41.8 14.4 %collective-permute-start.11 = (bf16[40,3584]{1,0:T(8,128)(2,1)S(1)}, bf16[40,3584]{1,0:T(8,128)(2,1)S(1)}, u32[]{:S(2)}, u32[]{:S(2)}) collective-permute-start(bf16[40,3584]{1,0:T(8,128)(2,1)S(1)} %collective-permute-done.5.refs_3_), channel_id=1, source_target_pairs={{0,2},{1,3},{2,0},{3,1},{4,6},{5,7},{6,4},{7,5},{8,10},{9,11},{10,... | collective-permute-start | bytes 860168 | tf_op jit(solution)/shard_map/ppermute | solution.py:395
  42.3 34.5 %collective-permute-start.12 = (bf16[40,3584]{1,0:T(8,128)(2,1)S(1)}, bf16[40,3584]{1,0:T(8,128)(2,1)S(1)}, u32[]{:S(2)}, u32[]{:S(2)}) collective-permute-start(bf16[40,3584]{1,0:T(8,128)(2,1)S(1)} %collective-permute-done.6.refs_0_), channel_id=1, source_target_pairs={{0,2},{1,3},{2,0},{3,1},{4,6},{5,7},{6,4},{7,5},{8,10},{9,11},{10,... | collective-permute-start | bytes 860168 | tf_op jit(solution)/shard_map/ppermute | solution.py:395
  43.8 33.0 %collective-permute-start.13 = (bf16[40,3584]{1,0:T(8,128)(2,1)S(1)}, bf16[40,3584]{1,0:T(8,128)(2,1)S(1)}, u32[]{:S(2)}, u32[]{:S(2)}) collective-permute-start(bf16[40,3584]{1,0:T(8,128)(2,1)S(1)} %collective-permute-done.7.refs_1_), channel_id=1, source_target_pairs={{0,2},{1,3},{2,0},{3,1},{4,6},{5,7},{6,4},{7,5},{8,10},{9,11},{10,... | collective-permute-start | bytes 860168 | tf_op jit(solution)/shard_map/ppermute | solution.py:395
  68.3 32.8 %collective-permute-start.16 = (bf16[80,3712]{1,0:T(8,128)(2,1)}, bf16[80,3712]{1,0:T(8,128)(2,1)S(1)}, u32[]{:S(2)}, u32[]{:S(2)}) collective-permute-start(bf16[80,3712]{1,0:T(8,128)(2,1)} %get-tuple-element.127), channel_id=1, source_target_pairs={{0,2},{1,3},{2,0},{3,1},{4,6},{5,7},{6,4},{7,5},{8,10},{9,11},{10,... | collective-permute-start | bytes 1781768 | tf_op jit(solution)/shard_map/ppermute | solution.py:395
  69.9 20.7 %collective-permute-start.14 = (bf16[40,3584]{1,0:T(8,128)(2,1)S(1)}, bf16[40,3584]{1,0:T(8,128)(2,1)S(1)}, u32[]{:S(2)}, u32[]{:S(2)}) collective-permute-start(bf16[40,3584]{1,0:T(8,128)(2,1)S(1)} %copy-done.24), channel_id=1, source_target_pairs={{0,16},{1,17},{2,18},{3,19},{4,20},{5,21},{6,22},{7,23},{8,24},{9,... | collective-permute-start | bytes 860168 | tf_op jit(solution)/shard_map/ppermute | solution.py:395
  75.7 20.7 %collective-permute-start.15 = (bf16[40,3584]{1,0:T(8,128)(2,1)S(1)}, bf16[40,3584]{1,0:T(8,128)(2,1)S(1)}, u32[]{:S(2)}, u32[]{:S(2)}) collective-permute-start(bf16[40,3584]{1,0:T(8,128)(2,1)S(1)} %copy-done.23), channel_id=1, source_target_pairs={{0,20},{1,21},{2,22},{3,23},{4,16},{5,17},{6,18},{7,19},{8,28},{9,... | collective-permute-start | bytes 860168 | tf_op jit(solution)/shard_map/ppermute | solution.py:395
  96.9 13.3 %collective-permute-start.19 = (bf16[40,3584]{1,0:T(8,128)(2,1)S(1)}, bf16[40,3584]{1,0:T(8,128)(2,1)S(1)}, u32[]{:S(2)}, u32[]{:S(2)}) collective-permute-start(bf16[40,3584]{1,0:T(8,128)(2,1)S(1)} %collective-permute-done.15.refs_1_), channel_id=1, source_target_pairs={{0,2},{1,3},{2,0},{3,1},{4,6},{5,7},{6,4},{7,5},{8,10},{9,11},{10,... | collective-permute-start | bytes 860168 | tf_op jit(solution)/shard_map/ppermute | solution.py:395
  110.3 17.1 %collective-permute-start.20 = (bf16[40,1920]{1,0:T(8,128)(2,1)}, bf16[40,1920]{1,0:T(8,128)(2,1)S(1)}, u32[]{:S(2)}, u32[]{:S(2)}) collective-permute-start(bf16[40,1920]{1,0:T(8,128)(2,1)} %get-tuple-element.139), channel_id=1, source_target_pairs={{0,4},{1,5},{2,6},{3,7},{4,0},{5,1},{6,2},{7,3},{8,12},{9,13},{10,... | collective-permute-start | bytes 460808 | tf_op jit(solution)/shard_map/ppermute | solution.py:395
  110.6 16.7 %collective-permute-start.21 = (bf16[40,1920]{1,0:T(8,128)(2,1)}, bf16[40,1920]{1,0:T(8,128)(2,1)S(1)}, u32[]{:S(2)}, u32[]{:S(2)}) collective-permute-start(bf16[40,1920]{1,0:T(8,128)(2,1)} %get-tuple-element.140), channel_id=1, source_target_pairs={{0,8},{1,9},{2,10},{3,11},{4,12},{5,13},{6,14},{7,15},{8,0},{9,1},... | collective-permute-start | bytes 460808 | tf_op jit(solution)/shard_map/ppermute | solution.py:395
  110.6 16.8 %collective-permute-start.22 = (bf16[40,1920]{1,0:T(8,128)(2,1)}, bf16[40,1920]{1,0:T(8,128)(2,1)S(1)}, u32[]{:S(2)}, u32[]{:S(2)}) collective-permute-start(bf16[40,1920]{1,0:T(8,128)(2,1)} %get-tuple-element.141), channel_id=1, source_target_pairs={{0,12},{1,13},{2,14},{3,15},{4,8},{5,9},{6,10},{7,11},{8,4},{9,5},... | collective-permute-start | bytes 460808 | tf_op jit(solution)/shard_map/ppermute | solution.py:395
  113.8 13.6 %collective-permute-start.23 = (bf16[40,1920]{1,0:T(8,128)(2,1)}, bf16[40,1920]{1,0:T(8,128)(2,1)S(1)}, u32[]{:S(2)}, u32[]{:S(2)}) collective-permute-start(bf16[40,1920]{1,0:T(8,128)(2,1)} %get-tuple-element.142), channel_id=1, source_target_pairs={{0,24},{1,25},{2,26},{3,27},{4,28},{5,29},{6,30},{7,31},{8,16},{9,... | collective-permute-start | bytes 460808 | tf_op jit(solution)/shard_map/ppermute | solution.py:395
  113.8 13.6 %collective-permute-start.24 = (bf16[40,1920]{1,0:T(8,128)(2,1)}, bf16[40,1920]{1,0:T(8,128)(2,1)S(1)}, u32[]{:S(2)}, u32[]{:S(2)}) collective-permute-start(bf16[40,1920]{1,0:T(8,128)(2,1)} %get-tuple-element.143), channel_id=1, source_target_pairs={{0,28},{1,29},{2,30},{3,31},{4,24},{5,25},{6,26},{7,27},{8,20},{9,... | collective-permute-start | bytes 460808 | tf_op jit(solution)/shard_map/ppermute | solution.py:395
  128.2 12.8 %collective-permute-start.25 = (bf16[160,7936]{1,0:T(8,128)(2,1)S(1)}, bf16[160,7936]{1,0:T(8,128)(2,1)S(1)}, u32[]{:S(2)}, u32[]{:S(2)}) collective-permute-start(bf16[160,7936]{1,0:T(8,128)(2,1)S(1)} %copy-done.4), channel_id=1, source_target_pairs={{0,1},{1,0},{2,3},{3,2},{4,5},{5,4},{6,7},{7,6},{8,9},{9,8},{10,11... | collective-permute-start | bytes 7618568 | tf_op jit(solution)/shard_map/ppermute | solution.py:395
  128.2 12.8 %collective-permute-start.26 = (bf16[80,7936]{1,0:T(8,128)(2,1)}, bf16[80,7936]{1,0:T(8,128)(2,1)S(1)}, u32[]{:S(2)}, u32[]{:S(2)}) collective-permute-start(bf16[80,7936]{1,0:T(8,128)(2,1)} %get-tuple-element.151.refs_1_.refs_7_), channel_id=1, source_target_pairs={{0,1},{1,0},{2,3},{3,2},{4,5},{5,4},{6,7},{7,6},{8,9},{9,8},{10,11... | collective-permute-start | bytes 3809288 | tf_op jit(solution)/shard_map/ppermute | solution.py:395
  128.8 12.3 %collective-permute-start.27 = (bf16[80,7936]{1,0:T(8,128)(2,1)}, bf16[80,7936]{1,0:T(8,128)(2,1)S(1)}, u32[]{:S(2)}, u32[]{:S(2)}) collective-permute-start(bf16[80,7936]{1,0:T(8,128)(2,1)} %get-tuple-element.152.refs_2_.refs_8_), channel_id=1, source_target_pairs={{0,1},{1,0},{2,3},{3,2},{4,5},{5,4},{6,7},{7,6},{8,9},{9,8},{10,11... | collective-permute-start | bytes 3809288 | tf_op jit(solution)/shard_map/ppermute | solution.py:395
  141.1 14.2 %collective-permute-start.29 = (bf16[40,1920]{1,0:T(8,128)(2,1)}, bf16[40,1920]{1,0:T(8,128)(2,1)S(1)}, u32[]{:S(2)}, u32[]{:S(2)}) collective-permute-start(bf16[40,1920]{1,0:T(8,128)(2,1)} %get-tuple-element.170), channel_id=1, source_target_pairs={{0,16},{1,17},{2,18},{3,19},{4,20},{5,21},{6,22},{7,23},{8,24},{9,... | collective-permute-start | bytes 460808 | tf_op jit(solution)/shard_map/ppermute | solution.py:395
  141.2 16.5 %collective-permute-start.30 = (bf16[40,1920]{1,0:T(8,128)(2,1)}, bf16[40,1920]{1,0:T(8,128)(2,1)S(1)}, u32[]{:S(2)}, u32[]{:S(2)}) collective-permute-start(bf16[40,1920]{1,0:T(8,128)(2,1)} %get-tuple-element.171), channel_id=1, source_target_pairs={{0,20},{1,21},{2,22},{3,23},{4,16},{5,17},{6,18},{7,19},{8,28},{9,... | collective-permute-start | bytes 460808 | tf_op jit(solution)/shard_map/ppermute | solution.py:395
  (39 other events, 539.4 us)

commit v3 on v2

--- a/solution.py
+++ b/solution.py
@@ -8,8 +8,9 @@
 from jax.sharding import PartitionSpec as P
 
 AXES = ("expert", "dp")
-VMEM_LIMIT = 56 * 1024 * 1024
+VMEM_LIMIT = 24 * 1024 * 1024
 EXTRA = 128
+EXPERT_VMEM = 24 * 1024 * 1024
 
 
 def vmem():
@@ -93,111 +94,86 @@
 NT = (((1,), (1,)), ((), ()))
 
 
-def expert_kernel(tiles, capacity, count, *refs):
+def expert_kernel(capacity, count, groups, *refs):
     blocks, weights = refs[:count], refs[count : count + 6]
-    parcel_ref, keep_ref, send_ref, mine_ref = refs[count + 6 : count + 10]
-    gate_w, up_w, total = refs[count + 10 :]
+    parcel_ref, mine_ref = refs[count + 6 : count + 8]
+    keep_refs = refs[count + 8 : count + 8 + len(groups)]
+    send_refs = refs[count + 8 + len(groups) :]
     gates, ups, downs = weights[0:2], weights[2:4], weights[4:6]
-    step = pl.program_id(0)
-    tile, units = gates[0].shape
+    width, units = gates[0].shape
     rows = count * capacity
-    half = rows // 2
-    width = tiles * tile
-    x_at = pl.multiple_of(step * tile, 128)
-    dy_at = pl.multiple_of(width + step * tile, 128)
-
-    @pl.when(step == 0)
-    def _():
-        total[...] = jnp.zeros_like(total)
-
-    for i, ref in enumerate(blocks):
-        value = ref[...].astype(jnp.float32)
-        place = slice(i * capacity, (i + 1) * capacity)
-        parcel_ref[place, pl.ds(x_at, tile)] = value[:capacity].astype(jnp.bfloat16)
-        parcel_ref[place, pl.ds(dy_at, tile)] = value[capacity:].astype(jnp.bfloat16)
-    x = parcel_ref[:, pl.ds(x_at, tile)]
-    dy = parcel_ref[:, pl.ds(dy_at, tile)]
-    for core in range(2):
-        gate_w[core, step] = gates[core][...]
-        up_w[core, step] = ups[core][...]
-        total[core, 0] += jnp.dot(x, gates[core][...], preferred_element_type=jnp.float32)
-        total[core, 1] += jnp.dot(x, ups[core][...], preferred_element_type=jnp.float32)
-        total[core, 2] += lax.dot_general(
-            dy, downs[core][...], NT, preferred_element_type=jnp.float32
-        )
-
-    @pl.when(step == tiles - 1)
-    def _():
-        route = jnp.zeros((rows, 1), jnp.float32)
-        unit_refs = (mine_ref, parcel_ref.at[:, 2 * width :])
+    tiles = chunks(width, 896)
+    totals = [[jnp.zeros((rows, units), jnp.float32)] * 3 for _ in range(2)]
+    for at, tile in tiles:
+        here = slice(at, at + tile)
+        there = slice(width + at, width + at + tile)
+        for i, ref in enumerate(blocks):
+            value = ref[:, here].astype(jnp.float32)
+            place = slice(i * capacity, (i + 1) * capacity)
+            parcel_ref[place, here] = value[:capacity].astype(jnp.bfloat16)
+            parcel_ref[place, there] = value[capacity:].astype(jnp.bfloat16)
+        x = parcel_ref[:, here]
+        dy = parcel_ref[:, there]
+        for core, total in enumerate(totals):
+            total[0] += jnp.dot(x, gates[core][here, :], preferred_element_type=jnp.float32)
+            total[1] += jnp.dot(x, ups[core][here, :], preferred_element_type=jnp.float32)
+            total[2] += lax.dot_general(
+                dy, downs[core][:, here], NT, preferred_element_type=jnp.float32
+            )
+    route = jnp.zeros((rows, 1), jnp.float32)
+    unit_refs = (mine_ref, parcel_ref.at[:, 2 * width :])
+    for (gate_value, up_value, back), out in zip(totals, unit_refs):
+        sigmoid = jax.nn.sigmoid(gate_value)
+        silu = gate_value * sigmoid
+        hidden = (silu * up_value).astype(jnp.bfloat16)
+        d_gate = back * up_value * sigmoid * (1.0 + gate_value * (1.0 - sigmoid))
+        out[:, 0:units] = d_gate.astype(jnp.bfloat16)
+        out[:, units : 2 * units] = (back * silu).astype(jnp.bfloat16)
+        out[:, 2 * units :] = hidden
+        route += jnp.sum(hidden.astype(jnp.float32) * back, axis=1, keepdims=True)
+
+    def put(value, here):
+        value = value.astype(jnp.bfloat16)
+        for out_refs, at in ((keep_refs, 0), (send_refs, rows // 2)):
+            for out, size in zip(out_refs, groups):
+                out[:, here] = value[at : at + size * capacity]
+                at += size * capacity
+
+    put(jnp.broadcast_to(route, (rows, EXTRA)), slice(width, width + EXTRA))
+    for at, tile in tiles:
+        here = slice(at, at + tile)
+        part = jnp.zeros((rows, tile), jnp.float32)
         for core, out in enumerate(unit_refs):
-            gate_value = total[core, 0]
-            up_value = total[core, 1]
-            back = total[core, 2]
-            sigmoid = jax.nn.sigmoid(gate_value)
-            silu = gate_value * sigmoid
-            hidden = (silu * up_value).astype(jnp.bfloat16)
-            d_gate = back * up_value * sigmoid * (1.0 + gate_value * (1.0 - sigmoid))
-            out[:, 0:units] = d_gate.astype(jnp.bfloat16)
-            out[:, units : 2 * units] = (back * silu).astype(jnp.bfloat16)
-            out[:, 2 * units :] = hidden
-            route += jnp.sum(hidden.astype(jnp.float32) * back, axis=1, keepdims=True)
-        route = jnp.broadcast_to(route, (rows, EXTRA)).astype(jnp.bfloat16)
-        keep_ref[:, width:] = route[:half]
-        send_ref[:, width:] = route[half:]
-        for at in range(tiles):
-            part = jnp.zeros((rows, tile), jnp.float32)
-            for core, out in enumerate(unit_refs):
-                part += lax.dot_general(
-                    out[:, 0:units], gate_w[core, at], NT, preferred_element_type=jnp.float32
-                )
-                part += lax.dot_general(
-                    out[:, units : 2 * units],
-                    up_w[core, at],
-                    NT,
-                    preferred_element_type=jnp.float32,
-                )
-            part = part.astype(jnp.bfloat16)
-            keep_ref[:, at * tile : (at + 1) * tile] = part[:half]
-            send_ref[:, at * tile : (at + 1) * tile] = part[half:]
-
-
-def run_expert(blocks, weights, capacity):
+            part += lax.dot_general(
+                out[:, 0:units], gates[core][here, :], NT, preferred_element_type=jnp.float32
+            )
+            part += lax.dot_general(
+                out[:, units : 2 * units],
+                ups[core][here, :],
+                NT,
+                preferred_element_type=jnp.float32,
+            )
+        put(part, here)
+
+
+def run_expert(blocks, weights, capacity, groups):
     width = blocks[0].shape[1]
     units = weights[0].shape[1]
     count = len(blocks)
     rows = count * capacity
-    tile = width // 4 if width % 512 == 0 else width
-    tiles = width // tile
-    out = jax.ShapeDtypeStruct((rows // 2, width + EXTRA), jnp.bfloat16)
+    outs = [jax.ShapeDtypeStruct((size * capacity, width + EXTRA), jnp.bfloat16) for size in groups]
     unit_rows = jax.ShapeDtypeStruct((rows, 3 * units), jnp.bfloat16)
     parcel = jax.ShapeDtypeStruct((rows, 2 * width + 3 * units), jnp.bfloat16)
-
-    def whole(shape):
-        return pl.BlockSpec(shape, lambda i: (0, 0))
-
-    return pl.pallas_call(
-        functools.partial(expert_kernel, tiles, capacity, count),
-        grid=(tiles,),
-        out_shape=[parcel, out, out, unit_rows],
-        in_specs=[pl.BlockSpec((2 * capacity, tile), lambda i: (0, i))] * count
-        + [pl.BlockSpec((tile, units), lambda i: (i, 0))] * 4
-        + [pl.BlockSpec((units, tile), lambda i: (0, i))] * 2,
-        out_specs=[
-            whole(parcel.shape),
-            whole(out.shape),
-            whole(out.shape),
-            whole(unit_rows.shape),
-        ],
-        scratch_shapes=[
-            pltpu.VMEM((2, tiles, tile, units), jnp.bfloat16),
-            pltpu.VMEM((2, tiles, tile, units), jnp.bfloat16),
-            pltpu.VMEM((2, 3, rows, units), jnp.float32),
-        ],
-        compiler_params=params(),
+    out = pl.pallas_call(
+        functools.partial(expert_kernel, capacity, count, groups),
+        out_shape=[parcel, unit_rows] + outs + outs,
+        in_specs=[vmem()] * (count + 6),
+        out_specs=[vmem()] * (2 + 2 * len(groups)),
+        compiler_params=pltpu.CompilerParams(vmem_limit_bytes=EXPERT_VMEM),
         cost_estimate=cost(20 * rows * width * units, 12 * width * units + 10 * rows * width),
         name="run_expert",
     )(*blocks, *weights)
+    return out[0], out[1], out[2 : 2 + len(groups)], out[2 + len(groups) :]
 
 
 def finish_kernel(capacity, keep_ref, far_ref, *outs):
@@ -396,7 +372,6 @@
 
     near, first, second = source_groups(expert_count)
     got, crossed, back = {}, {}, {}
-    parcels, units = [], []
 
     def fetch(group, source):
         for s in group:
@@ -405,14 +380,6 @@
     def cross(group):
         for s in group:
             crossed[s] = swap(got[s], 2)
-
-    def work(group):
-        parcel, keep, send, mine = run_expert(
-            [got[s] for s in group] + [crossed[s] for s in group], weights, capacity
-        )
-        parcels.append(parcel)
-        units.append(mine)
-        return parcel, keep, send
 
     def ready(group, keep, far):
         return dict(zip(group, finish(keep, far, capacity)))
@@ -428,34 +395,49 @@
     fetch(first, blocks)
     weights, close = after(weights, {s: blocks[s] for s in near})
     fetch(near, close)
-    cross(near[:2])
-    got, crossed, later = after(got, crossed, {s: blocks[s] for s in second})
-    fetch(second, later)
-    cross(near[2:])
-    cross(first)
-    near_parcel, near_keep, near_send = work(near)
-    near_far = swap(near_send, 2)
-    first_parcel, first_keep, first_send = work(first)
-    first_far = swap(first_send, 2)
-    moved = {s: got[s] for s in second}
-    near_keep, first_keep, moved = after(near_keep, first_keep, moved)
-    got.update(moved)
+    cross(near[:-1])
+    early, waiting = {s: crossed[s] for s in near[:-2]}, {s: blocks[s] for s in second}
+    got, early, weights, waiting = after(got, early, weights, waiting)
+    crossed.update(early)
+    fetch(second, waiting)
+    cross(near[-1:] + first)
+    got, crossed = after(got, crossed)
     cross(second)
-    near_ready = ready(near, near_keep, near_far)
-    first_ready = ready(first, first_keep, first_far)
-    moved = {s: crossed[s] for s in second}
-    near_ready, first_ready, moved = after(near_ready, first_ready, moved)
-    crossed.update(moved)
+
+    def work(*groups):
+        order = sum(groups, [])
+        return run_expert(
+            [got[s] for s in order] + [crossed[s] for s in order],
+            weights,
+            capacity,
+            [len(group) for group in groups],
+        )
+
+    parcel, units, keeps, sends = work(first, near)
+    ahead = {s: crossed[s] for s in second}
+    keeps, ahead = after(keeps, ahead)
+    crossed.update(ahead)
+    last_parcel, last_units, last_keeps, last_sends = work(second)
+    first_far = swap(sends[0], 2)
+    first_ready = ready(first, keeps[0], first_far)
+    first_ready, last_sends, parcel = after(first_ready, last_sends, parcel)
     give(first_ready)
+    second_far = swap(last_sends[0], 2)
+    near_far = swap(sends[1], 2)
+    second_ready = ready(second, last_keeps[0], second_far)
+    other = swap(parcel, 1)
+    returned = {s: back[s] for s in first}
+    returned, near_far, second_ready, other, last_parcel = after(
+        returned, near_far, second_ready, other, last_parcel
+    )
+    back.update(returned)
+    give(second_ready)
+    last_other = swap(last_parcel, 1)
+    near_ready = ready(near, keeps[1], near_far)
+    last_other, near_ready = after(last_other, near_ready)
     give(near_ready)
-    second_parcel, second_keep, second_send = work(second)
-    back, second_send, parcels = after(back, second_send, parcels)
-    second_far = swap(second_send, 2)
-    others = [swap(parcel, 1) for parcel in parcels]
-    second_ready = ready(second, second_keep, second_far)
-    others, second_ready = after(others, second_ready)
-    give(second_ready)
-    grads = weight_grads(parcels + others, units + [None] * 3, tokens.shape[1])
+    parcels = [parcel, last_parcel, other, last_other]
+    grads = weight_grads(parcels, [units, last_units, None, None], tokens.shape[1])
     grads, back = after(list(grads), back)
     grad_gate, grad_up, grad_down = grads
     grad_tokens, grad_route_t = combine(

time: 164 us -> 136 us (0.83)
  Pallas kernels: 56.7 us -> 29.6 us
  waiting for transfers between devices: 54.6 us -> 59.8 us
  starting transfers between devices: 45.2 us -> 40.4 us
    pallas_call x3 -> x2, Pallas kernels: 31.3 us -> 14.7 us  [run_expert(): pl.pallas_call(functools.partial(expert_kernel, capacity, count, groups),...]
    pallas_call x3, Pallas kernels: 6.02 us -> 0.4 us  [finish(): pl.pallas_call(functools.partial(finish_kernel, capacity), out_shape=[blo...]
    ppermute x31 -> x30, waiting for transfers between devices: 54.6 us -> 59.8 us  [swap(): lax.ppermute(value, AXES, [(i, i ^ distance) for i in range(device_count)])]
    ppermute x31 -> x30, starting transfers between devices: 45.2 us -> 40.4 us  [swap(): lax.ppermute(value, AXES, [(i, i ^ distance) for i in range(device_count)])]
    pallas_call x1, Pallas kernels: 4.32 us -> 1.5 us  [pick_rows(): pl.pallas_call(functools.partial(pick_kernel, expert_count, capacity), ou...]
    unnamed x64 -> x20, local copies, waits for them, and re-layouts: 5.92 us -> 5.24 us
  transfers between devices with their start and end apart: 31 -> 30, of which waited for: 11 -> 11; matrix products, arithmetic and copies ran while one was open for 0% -> 0% of each run, Pallas kernels for 32% -> 19%
where the time goes in v3:
time: 136 us
  waiting for transfers between devices  59.8 us (44%)
  starting transfers between devices  40.4 us (30%)
  Pallas kernels  29.6 us (22%)
  local copies, waits for them, and re-layouts  5.24 us (4%)
    ppermute x30, waiting for transfers between devices, swap(): lax.ppermute(value, AXES, [(i, i ^ distance) for i in range(device_count)])  59.8 us
    ppermute x30, starting transfers between devices, swap(): lax.ppermute(value, AXES, [(i, i ^ distance) for i in range(device_count)])  40.4 us
    pallas_call x2, Pallas kernels, run_expert(): pl.pallas_call(functools.partial(expert_kernel, capacity, count, groups),...  14.7 us
    pallas_call x1, Pallas kernels, weight_grads(): pl.pallas_call(functools.partial(weight_kernel, group_rows), grid=(tiles,...  9.43 us
    unnamed x20, local copies, waits for them, and re-layouts  5.24 us
    pallas_call x1, Pallas kernels, combine(): pl.pallas_call(functools.partial(combine_kernel, len(blocks), capacity),...  3.57 us
  transfers between devices with their start and end apart: 30, of which 11 were waited for; matrix products, arithmetic and copies ran while one was open for 0% of the time, Pallas kernels for 19%

profile of v3, /device:TPU:0, one launch (start us, length us, event | category | flops | bytes accessed | tf_op | source)
XLA Modules:
  0.0 135.7 jit_solution(15980959665787719781)
XLA Ops:
  5.4 1.5 %pick_rows.1 = (bf16[40,3584]{1,0:T(8,128)(2,1)S(1)}, bf16[40,3584]{1,0:T(8,128)(2,1)S(1)}, bf16[40,3584]{1,0:T(8,128)(2,1)S(1)}, bf16[40,3584]{1,0:T(8,128)(2,1...) custom-call(s32[1]{0:T(128)} %bitcast.me_ref, ...), custom_call_target="tpu_custom_call" | custom-call | flops 1000000000 | bytes 4000000 | tf_op jit(solution)/shard_map/pick_rows/pallas_call | solution.py:82
  6.9 4.7 %collective-permute-start.6 = (bf16[40,3584]{1,0:T(8,128)(2,1)S(1)}, bf16[40,3584]{1,0:T(8,128)(2,1)S(1)}, u32[]{:S(2)}, u32[]{:S(2)}) collective-permute-start(bf16[40,3584]{1,0:T(8,128)(2,1)S(1)} %get-tuple-element.115), channel_id=1, source_target_pairs={{0,24},{1,25},{2,26},{3,27},{4,28},{5,29},{6,30},{7,31},{8,16},{9,... | collective-permute-start | bytes 860168 | tf_op jit(solution)/shard_map/ppermute | solution.py:371
  11.7 1.6 %collective-permute-start.3 = (bf16[40,3584]{1,0:T(8,128)(2,1)S(1)}, bf16[40,3584]{1,0:T(8,128)(2,1)S(1)}, u32[]{:S(2)}, u32[]{:S(2)}) collective-permute-start(bf16[40,3584]{1,0:T(8,128)(2,1)S(1)} %get-tuple-element.112), channel_id=1, source_target_pairs={{0,4},{1,5},{2,6},{3,7},{4,0},{5,1},{6,2},{7,3},{8,12},{9,13},{10,... | collective-permute-start | bytes 860168 | tf_op jit(solution)/shard_map/ppermute | solution.py:371
  14.6 2.4 %collective-permute-start.7 = (bf16[40,3584]{1,0:T(8,128)(2,1)S(1)}, bf16[40,3584]{1,0:T(8,128)(2,1)S(1)}, u32[]{:S(2)}, u32[]{:S(2)}) collective-permute-start(bf16[40,3584]{1,0:T(8,128)(2,1)S(1)} %get-tuple-element.116), channel_id=1, source_target_pairs={{0,28},{1,29},{2,30},{3,31},{4,24},{5,25},{6,26},{7,27},{8,20},{9,... | collective-permute-start | bytes 860168 | tf_op jit(solution)/shard_map/ppermute | solution.py:371
  17.0 1.6 %collective-permute-start.5 = (bf16[40,3584]{1,0:T(8,128)(2,1)S(1)}, bf16[40,3584]{1,0:T(8,128)(2,1)S(1)}, u32[]{:S(2)}, u32[]{:S(2)}) collective-permute-start(bf16[40,3584]{1,0:T(8,128)(2,1)S(1)} %get-tuple-element.114), channel_id=1, source_target_pairs={{0,12},{1,13},{2,14},{3,15},{4,8},{5,9},{6,10},{7,11},{8,4},{9,5},... | collective-permute-start | bytes 860168 | tf_op jit(solution)/shard_map/ppermute | solution.py:371
  19.4 1.6 %collective-permute-start.8 = (bf16[40,3584]{1,0:T(8,128)(2,1)S(1)}, bf16[40,3584]{1,0:T(8,128)(2,1)S(1)}, u32[]{:S(2)}, u32[]{:S(2)}) collective-permute-start(bf16[40,3584]{1,0:T(8,128)(2,1)S(1)} %get-tuple-element.137.refs_2_), channel_id=1, source_target_pairs={{0,2},{1,3},{2,0},{3,1},{4,6},{5,7},{6,4},{7,5},{8,10},{9,11},{10,... | collective-permute-start | bytes 860168 | tf_op jit(solution)/shard_map/ppermute | solution.py:371
  22.1 9.2 %collective-permute-done.4.refs_4_ = bf16[40,3584]{1,0:T(8,128)(2,1)S(1)} collective-permute-done((bf16[40,3584]{1,0:T(8,128)(2,1)S(1)}, bf16[40,3584]{1,0:T(8,128)(2,1)S(1)}, u32[]{:S(2)}, u32[]{:S(2)}) %collective-permute-start.4) | collective-permute-done | bytes 286752 | tf_op jit(solution)/shard_map/ppermute | solution.py:371
  32.8 8.0 %collective-permute-done.5.refs_5_ = bf16[40,3584]{1,0:T(8,128)(2,1)S(1)} collective-permute-done((bf16[40,3584]{1,0:T(8,128)(2,1)S(1)}, bf16[40,3584]{1,0:T(8,128)(2,1)S(1)}, u32[]{:S(2)}, u32[]{:S(2)}) %collective-permute-start.5) | collective-permute-done | bytes 286752 | tf_op jit(solution)/shard_map/ppermute | solution.py:371
  40.8 2.4 %collective-permute-start.10 = (bf16[40,3584]{1,0:T(8,128)(2,1)S(1)}, bf16[40,3584]{1,0:T(8,128)(2,1)S(1)}, u32[]{:S(2)}, u32[]{:S(2)}) collective-permute-start(bf16[40,3584]{1,0:T(8,128)(2,1)S(1)} %get-tuple-element.129), channel_id=1, source_target_pairs={{0,16},{1,17},{2,18},{3,19},{4,20},{5,21},{6,22},{7,23},{8,24},{9,... | collective-permute-start | bytes 860168 | tf_op jit(solution)/shard_map/ppermute | solution.py:371
  43.2 1.5 %collective-permute-start.11 = (bf16[40,3584]{1,0:T(8,128)(2,1)S(1)}, bf16[40,3584]{1,0:T(8,128)(2,1)S(1)}, u32[]{:S(2)}, u32[]{:S(2)}) collective-permute-start(bf16[40,3584]{1,0:T(8,128)(2,1)S(1)} %get-tuple-element.130), channel_id=1, source_target_pairs={{0,20},{1,21},{2,22},{3,23},{4,16},{5,17},{6,18},{7,19},{8,28},{9,... | collective-permute-start | bytes 860168 | tf_op jit(solution)/shard_map/ppermute | solution.py:371
  48.2 15.5 %collective-permute-done.10.refs_0_ = bf16[40,3584]{1,0:T(8,128)(2,1)S(1)} collective-permute-done((bf16[40,3584]{1,0:T(8,128)(2,1)S(1)}, bf16[40,3584]{1,0:T(8,128)(2,1)S(1)}, u32[]{:S(2)}, u32[]{:S(2)}) %collective-permute-start.10) | collective-permute-done | bytes 286752 | tf_op jit(solution)/shard_map/ppermute | solution.py:371
  63.8 5.8 %collective-permute-done.11.refs_1_ = bf16[40,3584]{1,0:T(8,128)(2,1)S(1)} collective-permute-done((bf16[40,3584]{1,0:T(8,128)(2,1)S(1)}, bf16[40,3584]{1,0:T(8,128)(2,1)S(1)}, u32[]{:S(2)}, u32[]{:S(2)}) %collective-permute-start.11) | collective-permute-done | bytes 286752 | tf_op jit(solution)/shard_map/ppermute | solution.py:371
  69.5 1.6 %collective-permute-start.16 = (bf16[40,3584]{1,0:T(8,128)(2,1)S(1)}, bf16[40,3584]{1,0:T(8,128)(2,1)S(1)}, u32[]{:S(2)}, u32[]{:S(2)}) collective-permute-start(bf16[40,3584]{1,0:T(8,128)(2,1)S(1)} %collective-permute-done.10.refs_0_), channel_id=1, source_target_pairs={{0,2},{1,3},{2,0},{3,1},{4,6},{5,7},{6,4},{7,5},{8,10},{9,11},{10,... | collective-permute-start | bytes 860168 | tf_op jit(solution)/shard_map/ppermute | solution.py:371
  71.6 1.5 %copy-done.2 = bf16[1,256,3584]{2,1,0:T(8,128)(2,1)S(1)} copy-done((bf16[1,256,3584]{2,1,0:T(8,128)(2,1)S(1)}, bf16[1,256,3584]{2,1,0:T(8,128)(2,1)}, u32[]{:S(2)}) %copy-start.2) | copy-done | bytes 1835032
  73.1 8.2 %run_expert.2 = (bf16[240,7936]{1,0:T(8,128)(2,1)S(1)}, bf16[240,768]{1,0:T(8,128)(2,1)S(1)}, bf16[40,3712]{1,0:T(8,128)(2,1)S(1)}, bf16[80,3712]{1,0:T(8,128)(2...) custom-call(bf16[40,3584]{1,0:T(8,128)(2,1)S(1)} %collective-permute-done.6.refs_0_, ...), custom_call_target="tpu_custom_call" | custom-call | flops 4404019200 | bytes 19611648 | tf_op jit(solution)/shard_map/run_expert/pallas_call | solution.py:167
  81.3 1.6 %collective-permute-start.18 = (bf16[40,3712]{1,0:T(8,128)(2,1)S(1)}, bf16[40,3712]{1,0:T(8,128)(2,1)S(1)}, u32[]{:S(2)}, u32[]{:S(2)}) collective-permute-start(bf16[40,3712]{1,0:T(8,128)(2,1)S(1)} %get-tuple-element.158), channel_id=1, source_target_pairs={{0,2},{1,3},{2,0},{3,1},{4,6},{5,7},{6,4},{7,5},{8,10},{9,11},{10,... | collective-permute-start | bytes 890888 | tf_op jit(solution)/shard_map/ppermute | solution.py:371
  84.3 6.5 %run_expert.3 = (bf16[80,7936]{1,0:T(8,128)(2,1)S(1)}, bf16[80,768]{1,0:T(8,128)(2,1)S(1)}, bf16[40,3712]{1,0:T(8,128)(2,1)S(1)}, bf16[40,3712]{1,0:T(8,128)(2,1)S(1)}) custom-call(bf16[40,3584]{1,0:T(8,128)(2,1)S(1)} %collective-permute-done.10.refs_0_, bf16[40,3584]{1,0:T(8,128)(2,1)S(1)} %collective-permute-done.11.refs_1_, ...), custom_call_target="tpu_custom_call" | custom-call | flops 1468006400 | bytes 13877248 | tf_op jit(solution)/shard_map/run_expert/pallas_call | solution.py:167
  90.9 1.6 %collective-permute-start.21 = (bf16[80,3712]{1,0:T(8,128)(2,1)S(1)}, bf16[80,3712]{1,0:T(8,128)(2,1)S(1)}, u32[]{:S(2)}, u32[]{:S(2)}) collective-permute-start(bf16[80,3712]{1,0:T(8,128)(2,1)S(1)} %get-tuple-element.168), channel_id=1, source_target_pairs={{0,2},{1,3},{2,0},{3,1},{4,6},{5,7},{6,4},{7,5},{8,10},{9,11},{10,... | collective-permute-start | bytes 1781768 | tf_op jit(solution)/shard_map/ppermute | solution.py:371
  93.0 3.1 %collective-permute-start.19 = (bf16[40,1920]{1,0:T(8,128)(2,1)S(1)}, bf16[40,1920]{1,0:T(8,128)(2,1)S(1)}, u32[]{:S(2)}, u32[]{:S(2)}) collective-permute-start(bf16[40,1920]{1,0:T(8,128)(2,1)S(1)} %get-tuple-element.166), channel_id=1, source_target_pairs={{0,24},{1,25},{2,26},{3,27},{4,28},{5,29},{6,30},{7,31},{8,16},{9,... | collective-permute-start | bytes 460808 | tf_op jit(solution)/shard_map/ppermute | solution.py:371
  96.8 16.3 %collective-permute-done.22.far_ref = bf16[40,3712]{1,0:T(8,128)(2,1)S(1)} collective-permute-done((bf16[40,3712]{1,0:T(8,128)(2,1)S(1)}, bf16[40,3712]{1,0:T(8,128)(2,1)S(1)}, u32[]{:S(2)}, u32[]{:S(2)}) %collective-permute-start.22) | collective-permute-done | bytes 296992 | tf_op jit(solution)/shard_map/ppermute | solution.py:371
  113.4 2.9 %collective-permute-start.29 = (bf16[40,1920]{1,0:T(8,128)(2,1)S(1)}, bf16[40,1920]{1,0:T(8,128)(2,1)S(1)}, u32[]{:S(2)}, u32[]{:S(2)}) collective-permute-start(bf16[40,1920]{1,0:T(8,128)(2,1)S(1)} %get-tuple-element.193), channel_id=1, source_target_pairs={{0,20},{1,21},{2,22},{3,23},{4,16},{5,17},{6,18},{7,19},{8,28},{9,... | collective-permute-start | bytes 460808 | tf_op jit(solution)/shard_map/ppermute | solution.py:371
  116.5 1.6 %collective-permute-start.25 = (bf16[40,1920]{1,0:T(8,128)(2,1)S(1)}, bf16[40,1920]{1,0:T(8,128)(2,1)S(1)}, u32[]{:S(2)}, u32[]{:S(2)}) collective-permute-start(bf16[40,1920]{1,0:T(8,128)(2,1)S(1)} %get-tuple-element.189), channel_id=1, source_target_pairs={{0,4},{1,5},{2,6},{3,7},{4,0},{5,1},{6,2},{7,3},{8,12},{9,13},{10,... | collective-permute-start | bytes 460808 | tf_op jit(solution)/shard_map/ppermute | solution.py:371
  120.1 9.4 %weight_grads.1 = (bf16[3584,256]{1,0:T(8,128)(2,1)}, bf16[3584,256]{1,0:T(8,128)(2,1)}, bf16[256,3584]{1,0:T(8,128)(2,1)}) custom-call(bf16[240,7936]{1,0:T(8,128)(2,1)S(1)} %get-tuple-element.165.refs_0_.refs_4_, bf16[80,7936]{1,0:T(8,128)(2,1)S(1)} %get-tuple-element.174.refs_1_.refs_5_, ...), custom_call_target="tpu_custom_call" | custom-call | flops 3523215360 | bytes 14680064 | tf_op jit(solution)/shard_map/weight_grads/pallas_call | solution.py:262
  132.1 3.6 %combine.1 = (bf16[128,3584]{1,0:T(8,128)(2,1)}, bf16[8,128]{1,0:T(8,128)(2,1)}) custom-call(s32[1]{0:T(128)} %bitcast.me_ref, s32[8,128]{1,0:T(8,128)S(1)} %bitcast.20, bf16[8,128]{1,0:T(8,128)(2,1)S(1)} %bitcast.22, bf16[40,1920]{1,0:T(8,128)(2,1)S(1)} %get-tuple-element.196.refs_0_, bf16[40,1920]{1,0:T(8,128)(2,1)S(1)} %collective-permute-done.25.refs_1_, ...), custom_call_target="tpu_custom_call" | custom-call | flops 1000000000 | bytes 3000000 | tf_op jit(solution)/shard_map/combine/pallas_call | solution.py:332
  (64 shorter events, 21.3 us)
Async XLA Ops:
  6.9 12.5 %collective-permute-start.6 = (bf16[40,3584]{1,0:T(8,128)(2,1)S(1)}, bf16[40,3584]{1,0:T(8,128)(2,1)S(1)}, u32[]{:S(2)}, u32[]{:S(2)}) collective-permute-start(bf16[40,3584]{1,0:T(8,128)(2,1)S(1)} %get-tuple-element.115), channel_id=1, source_target_pairs={{0,24},{1,25},{2,26},{3,27},{4,28},{5,29},{6,30},{7,31},{8,16},{9,... | collective-permute-start | bytes 860168 | tf_op jit(solution)/shard_map/ppermute | solution.py:371
  13.2 18.1 %collective-permute-start.4 = (bf16[40,3584]{1,0:T(8,128)(2,1)S(1)}, bf16[40,3584]{1,0:T(8,128)(2,1)S(1)}, u32[]{:S(2)}, u32[]{:S(2)}) collective-permute-start(bf16[40,3584]{1,0:T(8,128)(2,1)S(1)} %get-tuple-element.113), channel_id=1, source_target_pairs={{0,8},{1,9},{2,10},{3,11},{4,12},{5,13},{6,14},{7,15},{8,0},{9,1},... | collective-permute-start | bytes 860168 | tf_op jit(solution)/shard_map/ppermute | solution.py:371
  14.6 18.2 %collective-permute-start.7 = (bf16[40,3584]{1,0:T(8,128)(2,1)S(1)}, bf16[40,3584]{1,0:T(8,128)(2,1)S(1)}, u32[]{:S(2)}, u32[]{:S(2)}) collective-permute-start(bf16[40,3584]{1,0:T(8,128)(2,1)S(1)} %get-tuple-element.116), channel_id=1, source_target_pairs={{0,28},{1,29},{2,30},{3,31},{4,24},{5,25},{6,26},{7,27},{8,20},{9,... | collective-permute-start | bytes 860168 | tf_op jit(solution)/shard_map/ppermute | solution.py:371
  17.0 23.8 %collective-permute-start.5 = (bf16[40,3584]{1,0:T(8,128)(2,1)S(1)}, bf16[40,3584]{1,0:T(8,128)(2,1)S(1)}, u32[]{:S(2)}, u32[]{:S(2)}) collective-permute-start(bf16[40,3584]{1,0:T(8,128)(2,1)S(1)} %get-tuple-element.114), channel_id=1, source_target_pairs={{0,12},{1,13},{2,14},{3,15},{4,8},{5,9},{6,10},{7,11},{8,4},{9,5},... | collective-permute-start | bytes 860168 | tf_op jit(solution)/shard_map/ppermute | solution.py:371
  19.4 21.4 %collective-permute-start.8 = (bf16[40,3584]{1,0:T(8,128)(2,1)S(1)}, bf16[40,3584]{1,0:T(8,128)(2,1)S(1)}, u32[]{:S(2)}, u32[]{:S(2)}) collective-permute-start(bf16[40,3584]{1,0:T(8,128)(2,1)S(1)} %get-tuple-element.137.refs_2_), channel_id=1, source_target_pairs={{0,2},{1,3},{2,0},{3,1},{4,6},{5,7},{6,4},{7,5},{8,10},{9,11},{10,... | collective-permute-start | bytes 860168 | tf_op jit(solution)/shard_map/ppermute | solution.py:371
  21.1 19.8 %collective-permute-start.9 = (bf16[40,3584]{1,0:T(8,128)(2,1)S(1)}, bf16[40,3584]{1,0:T(8,128)(2,1)S(1)}, u32[]{:S(2)}, u32[]{:S(2)}) collective-permute-start(bf16[40,3584]{1,0:T(8,128)(2,1)S(1)} %collective-permute-done.3.refs_3_), channel_id=1, source_target_pairs={{0,2},{1,3},{2,0},{3,1},{4,6},{5,7},{6,4},{7,5},{8,10},{9,11},{10,... | collective-permute-start | bytes 860168 | tf_op jit(solution)/shard_map/ppermute | solution.py:371
  31.4 15.4 %collective-permute-start.12 = (bf16[40,3584]{1,0:T(8,128)(2,1)S(1)}, bf16[40,3584]{1,0:T(8,128)(2,1)S(1)}, u32[]{:S(2)}, u32[]{:S(2)}) collective-permute-start(bf16[40,3584]{1,0:T(8,128)(2,1)S(1)} %collective-permute-done.4.refs_4_), channel_id=1, source_target_pairs={{0,2},{1,3},{2,0},{3,1},{4,6},{5,7},{6,4},{7,5},{8,10},{9,11},{10,... | collective-permute-start | bytes 860168 | tf_op jit(solution)/shard_map/ppermute | solution.py:371
  40.8 22.9 %collective-permute-start.10 = (bf16[40,3584]{1,0:T(8,128)(2,1)S(1)}, bf16[40,3584]{1,0:T(8,128)(2,1)S(1)}, u32[]{:S(2)}, u32[]{:S(2)}) collective-permute-start(bf16[40,3584]{1,0:T(8,128)(2,1)S(1)} %get-tuple-element.129), channel_id=1, source_target_pairs={{0,16},{1,17},{2,18},{3,19},{4,20},{5,21},{6,22},{7,23},{8,24},{9,... | collective-permute-start | bytes 860168 | tf_op jit(solution)/shard_map/ppermute | solution.py:371
  43.2 26.3 %collective-permute-start.11 = (bf16[40,3584]{1,0:T(8,128)(2,1)S(1)}, bf16[40,3584]{1,0:T(8,128)(2,1)S(1)}, u32[]{:S(2)}, u32[]{:S(2)}) collective-permute-start(bf16[40,3584]{1,0:T(8,128)(2,1)S(1)} %get-tuple-element.130), channel_id=1, source_target_pairs={{0,20},{1,21},{2,22},{3,23},{4,16},{5,17},{6,18},{7,19},{8,28},{9,... | collective-permute-start | bytes 860168 | tf_op jit(solution)/shard_map/ppermute | solution.py:371
  44.7 24.8 %collective-permute-start.13 = (bf16[40,3584]{1,0:T(8,128)(2,1)S(1)}, bf16[40,3584]{1,0:T(8,128)(2,1)S(1)}, u32[]{:S(2)}, u32[]{:S(2)}) collective-permute-start(bf16[40,3584]{1,0:T(8,128)(2,1)S(1)} %collective-permute-done.5.refs_5_), channel_id=1, source_target_pairs={{0,2},{1,3},{2,0},{3,1},{4,6},{5,7},{6,4},{7,5},{8,10},{9,11},{10,... | collective-permute-start | bytes 860168 | tf_op jit(solution)/shard_map/ppermute | solution.py:371
  46.2 23.3 %collective-permute-start.14 = (bf16[40,3584]{1,0:T(8,128)(2,1)S(1)}, bf16[40,3584]{1,0:T(8,128)(2,1)S(1)}, u32[]{:S(2)}, u32[]{:S(2)}) collective-permute-start(bf16[40,3584]{1,0:T(8,128)(2,1)S(1)} %collective-permute-done.6.refs_0_), channel_id=1, source_target_pairs={{0,2},{1,3},{2,0},{3,1},{4,6},{5,7},{6,4},{7,5},{8,10},{9,11},{10,... | collective-permute-start | bytes 860168 | tf_op jit(solution)/shard_map/ppermute | solution.py:371
  46.8 22.8 %collective-permute-start.15 = (bf16[40,3584]{1,0:T(8,128)(2,1)S(1)}, bf16[40,3584]{1,0:T(8,128)(2,1)S(1)}, u32[]{:S(2)}, u32[]{:S(2)}) collective-permute-start(bf16[40,3584]{1,0:T(8,128)(2,1)S(1)} %collective-permute-done.7.refs_1_), channel_id=1, source_target_pairs={{0,2},{1,3},{2,0},{3,1},{4,6},{5,7},{6,4},{7,5},{8,10},{9,11},{10,... | collective-permute-start | bytes 860168 | tf_op jit(solution)/shard_map/ppermute | solution.py:371
  69.5 13.3 %collective-permute-start.16 = (bf16[40,3584]{1,0:T(8,128)(2,1)S(1)}, bf16[40,3584]{1,0:T(8,128)(2,1)S(1)}, u32[]{:S(2)}, u32[]{:S(2)}) collective-permute-start(bf16[40,3584]{1,0:T(8,128)(2,1)S(1)} %collective-permute-done.10.refs_0_), channel_id=1, source_target_pairs={{0,2},{1,3},{2,0},{3,1},{4,6},{5,7},{6,4},{7,5},{8,10},{9,11},{10,... | collective-permute-start | bytes 860168 | tf_op jit(solution)/shard_map/ppermute | solution.py:371
  71.1 13.1 %collective-permute-start.17 = (bf16[40,3584]{1,0:T(8,128)(2,1)S(1)}, bf16[40,3584]{1,0:T(8,128)(2,1)S(1)}, u32[]{:S(2)}, u32[]{:S(2)}) collective-permute-start(bf16[40,3584]{1,0:T(8,128)(2,1)S(1)} %collective-permute-done.11.refs_1_), channel_id=1, source_target_pairs={{0,2},{1,3},{2,0},{3,1},{4,6},{5,7},{6,4},{7,5},{8,10},{9,11},{10,... | collective-permute-start | bytes 860168 | tf_op jit(solution)/shard_map/ppermute | solution.py:371
  90.9 22.4 %collective-permute-start.23 = (bf16[240,7936]{1,0:T(8,128)(2,1)S(1)}, bf16[240,7936]{1,0:T(8,128)(2,1)S(1)}, u32[]{:S(2)}, u32[]{:S(2)}) collective-permute-start(bf16[240,7936]{1,0:T(8,128)(2,1)S(1)} %get-tuple-element.165.refs_0_.refs_4_), channel_id=1, source_target_pairs={{0,1},{1,0},{2,3},{3,2},{4,5},{5,4},{6,7},{7,6},{8,9},{9,8},{10,11... | collective-permute-start | bytes 11427848 | tf_op jit(solution)/shard_map/ppermute | solution.py:371
  90.9 22.3 %collective-permute-start.21 = (bf16[80,3712]{1,0:T(8,128)(2,1)S(1)}, bf16[80,3712]{1,0:T(8,128)(2,1)S(1)}, u32[]{:S(2)}, u32[]{:S(2)}) collective-permute-start(bf16[80,3712]{1,0:T(8,128)(2,1)S(1)} %get-tuple-element.168), channel_id=1, source_target_pairs={{0,2},{1,3},{2,0},{3,1},{4,6},{5,7},{6,4},{7,5},{8,10},{9,11},{10,... | collective-permute-start | bytes 1781768 | tf_op jit(solution)/shard_map/ppermute | solution.py:371
  92.5 20.6 %collective-permute-start.22 = (bf16[40,3712]{1,0:T(8,128)(2,1)S(1)}, bf16[40,3712]{1,0:T(8,128)(2,1)S(1)}, u32[]{:S(2)}, u32[]{:S(2)}) collective-permute-start(bf16[40,3712]{1,0:T(8,128)(2,1)S(1)} %get-tuple-element.170), channel_id=1, source_target_pairs={{0,2},{1,3},{2,0},{3,1},{4,6},{5,7},{6,4},{7,5},{8,10},{9,11},{10,... | collective-permute-start | bytes 890888 | tf_op jit(solution)/shard_map/ppermute | solution.py:371
  93.0 20.2 %collective-permute-start.19 = (bf16[40,1920]{1,0:T(8,128)(2,1)S(1)}, bf16[40,1920]{1,0:T(8,128)(2,1)S(1)}, u32[]{:S(2)}, u32[]{:S(2)}) collective-permute-start(bf16[40,1920]{1,0:T(8,128)(2,1)S(1)} %get-tuple-element.166), channel_id=1, source_target_pairs={{0,24},{1,25},{2,26},{3,27},{4,28},{5,29},{6,30},{7,31},{8,16},{9,... | collective-permute-start | bytes 460808 | tf_op jit(solution)/shard_map/ppermute | solution.py:371
  96.2 17.1 %collective-permute-start.20 = (bf16[40,1920]{1,0:T(8,128)(2,1)S(1)}, bf16[40,1920]{1,0:T(8,128)(2,1)S(1)}, u32[]{:S(2)}, u32[]{:S(2)}) collective-permute-start(bf16[40,1920]{1,0:T(8,128)(2,1)S(1)} %get-tuple-element.167), channel_id=1, source_target_pairs={{0,28},{1,29},{2,30},{3,31},{4,24},{5,25},{6,26},{7,27},{8,20},{9,... | collective-permute-start | bytes 460808 | tf_op jit(solution)/shard_map/ppermute | solution.py:371
  113.4 16.1 %collective-permute-start.28 = (bf16[40,1920]{1,0:T(8,128)(2,1)S(1)}, bf16[40,1920]{1,0:T(8,128)(2,1)S(1)}, u32[]{:S(2)}, u32[]{:S(2)}) collective-permute-start(bf16[40,1920]{1,0:T(8,128)(2,1)S(1)} %get-tuple-element.192), channel_id=1, source_target_pairs={{0,16},{1,17},{2,18},{3,19},{4,20},{5,21},{6,22},{7,23},{8,24},{9,... | collective-permute-start | bytes 460808 | tf_op jit(solution)/shard_map/ppermute | solution.py:371
  113.4 17.1 %collective-permute-start.29 = (bf16[40,1920]{1,0:T(8,128)(2,1)S(1)}, bf16[40,1920]{1,0:T(8,128)(2,1)S(1)}, u32[]{:S(2)}, u32[]{:S(2)}) collective-permute-start(bf16[40,1920]{1,0:T(8,128)(2,1)S(1)} %get-tuple-element.193), channel_id=1, source_target_pairs={{0,20},{1,21},{2,22},{3,23},{4,16},{5,17},{6,18},{7,19},{8,28},{9,... | collective-permute-start | bytes 460808 | tf_op jit(solution)/shard_map/ppermute | solution.py:371
  116.5 14.1 %collective-permute-start.25 = (bf16[40,1920]{1,0:T(8,128)(2,1)S(1)}, bf16[40,1920]{1,0:T(8,128)(2,1)S(1)}, u32[]{:S(2)}, u32[]{:S(2)}) collective-permute-start(bf16[40,1920]{1,0:T(8,128)(2,1)S(1)} %get-tuple-element.189), channel_id=1, source_target_pairs={{0,4},{1,5},{2,6},{3,7},{4,0},{5,1},{6,2},{7,3},{8,12},{9,13},{10,... | collective-permute-start | bytes 460808 | tf_op jit(solution)/shard_map/ppermute | solution.py:371
  118.1 12.9 %collective-permute-start.26 = (bf16[40,1920]{1,0:T(8,128)(2,1)S(1)}, bf16[40,1920]{1,0:T(8,128)(2,1)S(1)}, u32[]{:S(2)}, u32[]{:S(2)}) collective-permute-start(bf16[40,1920]{1,0:T(8,128)(2,1)S(1)} %get-tuple-element.190), channel_id=1, source_target_pairs={{0,8},{1,9},{2,10},{3,11},{4,12},{5,13},{6,14},{7,15},{8,0},{9,1},... | collective-permute-start | bytes 460808 | tf_op jit(solution)/shard_map/ppermute | solution.py:371
  118.9 13.2 %collective-permute-start.27 = (bf16[40,1920]{1,0:T(8,128)(2,1)S(1)}, bf16[40,1920]{1,0:T(8,128)(2,1)S(1)}, u32[]{:S(2)}, u32[]{:S(2)}) collective-permute-start(bf16[40,1920]{1,0:T(8,128)(2,1)S(1)} %get-tuple-element.191), channel_id=1, source_target_pairs={{0,12},{1,13},{2,14},{3,15},{4,8},{5,9},{6,10},{7,11},{8,4},{9,5},... | collective-permute-start | bytes 460808 | tf_op jit(solution)/shard_map/ppermute | solution.py:371
  (16 other events, 226.9 us)

commit v4 on v3

--- a/solution.py
+++ b/solution.py
@@ -212,36 +212,32 @@
     )(keep, far)
 
 
-def weight_kernel(group_rows, *refs):
+def weight_kernel(group_rows, width, *refs):
     count = len(group_rows)
-    x_refs, dy_refs = refs[:count], refs[count : 2 * count]
-    unit_refs = refs[2 * count : 5 * count]
-    gate_ref, up_ref, down_ref, all_units, x_rows, dy_rows = refs[5 * count :]
-    units = gate_ref.shape[1]
+    parcels, unit_refs = refs[:count], refs[count : 2 * count]
+    gate_ref, up_ref, down_ref, all_units = refs[2 * count :]
+    tile, units = gate_ref.shape
 
     @pl.when(pl.program_id(0) == 0)
     def _():
         at = 0
-        for g, rows in enumerate(group_rows):
-            for part in range(3):
-                all_units[at : at + rows, part * units : (part + 1) * units] = unit_refs[
-                    3 * g + part
-                ][...]
+        for rows, parcel, own in zip(group_rows, parcels, unit_refs):
+            source = parcel if own is None else own
+            all_units[at : at + rows, :] = source[:, source.shape[1] - 3 * units :]
             at += rows
 
-    at = 0
-    for rows, x_ref, dy_ref in zip(group_rows, x_refs, dy_refs):
-        x_rows[at : at + rows, :] = x_ref[...]
-        dy_rows[at : at + rows, :] = dy_ref[...]
-        at += rows
+    x_at = pl.multiple_of(pl.program_id(0) * tile, 128)
+    dy_at = pl.multiple_of(width + pl.program_id(0) * tile, 128)
+    x_rows = jnp.concatenate([parcel[:, pl.ds(x_at, tile)] for parcel in parcels], axis=0)
+    dy_rows = jnp.concatenate([parcel[:, pl.ds(dy_at, tile)] for parcel in parcels], axis=0)
     contract = (((0,), (0,)), ((), ()))
     grads = lax.dot_general(
-        x_rows[...], all_units[:, 0 : 2 * units], contract, preferred_element_type=jnp.float32
+        x_rows, all_units[:, 0 : 2 * units], contract, preferred_element_type=jnp.float32
     )
     gate_ref[...] = grads[:, :units].astype(jnp.bfloat16)
     up_ref[...] = grads[:, units:].astype(jnp.bfloat16)
     down_ref[...] = lax.dot_general(
-        all_units[:, 2 * units :], dy_rows[...], contract, preferred_element_type=jnp.float32
+        all_units[:, 2 * units :], dy_rows, contract, preferred_element_type=jnp.float32
     ).astype(jnp.bfloat16)
 
 
@@ -249,43 +245,37 @@
     hidden_units = (parcels[0].shape[1] - 2 * width) // 3
     group_rows = [p.shape[0] for p in parcels]
     total = sum(group_rows)
-    tile = 512 if width % 512 == 0 else width
-    tiles = width // tile
-    unit_at = 2 * width // hidden_units
-    unit_args, unit_specs = [], []
-    for parcel, own in zip(parcels, units):
-        shape = (parcel.shape[0], hidden_units)
-        first = unit_at if own is None else 0
-        for part in range(3):
-            unit_args.append(parcel if own is None else own)
-            unit_specs.append(pl.BlockSpec(shape, lambda i, at=first + part: (0, at)))
+    tile = width // 4 if width % (128 * 4) == 0 else width
+    given = [own for own in units if own is not None]
+
+    def kernel(*refs):
+        rest = list(refs[len(parcels) : len(parcels) + len(given)])
+        owns = [None if own is None else rest.pop(0) for own in units]
+        weight_kernel(
+            group_rows, width, *refs[: len(parcels)], *owns, *refs[len(parcels) + len(given) :]
+        )
+
     return pl.pallas_call(
-        functools.partial(weight_kernel, group_rows),
-        grid=(tiles,),
+        kernel,
+        grid=(width // tile,),
         out_shape=[
             jax.ShapeDtypeStruct((width, hidden_units), jnp.bfloat16),
             jax.ShapeDtypeStruct((width, hidden_units), jnp.bfloat16),
             jax.ShapeDtypeStruct((hidden_units, width), jnp.bfloat16),
         ],
-        in_specs=[pl.BlockSpec((rows, tile), lambda i: (0, i)) for rows in group_rows]
-        + [pl.BlockSpec((rows, tile), lambda i: (0, tiles + i)) for rows in group_rows]
-        + unit_specs,
+        in_specs=[vmem()] * (len(parcels) + len(given)),
         out_specs=[
             pl.BlockSpec((tile, hidden_units), lambda i: (i, 0)),
             pl.BlockSpec((tile, hidden_units), lambda i: (i, 0)),
             pl.BlockSpec((hidden_units, tile), lambda i: (0, i)),
         ],
-        scratch_shapes=[
-            pltpu.VMEM((total, 3 * hidden_units), jnp.bfloat16),
-            pltpu.VMEM((total, tile), jnp.bfloat16),
-            pltpu.VMEM((total, tile), jnp.bfloat16),
-        ],
+        scratch_shapes=[pltpu.VMEM((total, 3 * hidden_units), jnp.bfloat16)],
         compiler_params=params(),
         cost_estimate=cost(
             6 * total * width * hidden_units, 4 * total * width + 6 * width * hidden_units
         ),
         name="weight_grads",
-    )(*parcels, *parcels, *unit_args)
+    )(*parcels, *given)
 
 
 def combine_kernel(expert_count, capacity, me_ref, ids_ref, weight_ref, *refs):
@@ -413,29 +403,35 @@
             [len(group) for group in groups],
         )
 
-    parcel, units, keeps, sends = work(first, near)
+    left, right = near[: len(near) // 2], near[len(near) // 2 :]
+    parcel, units, keeps, sends = work(first, left, right)
     ahead = {s: crossed[s] for s in second}
     keeps, ahead = after(keeps, ahead)
     crossed.update(ahead)
     last_parcel, last_units, last_keeps, last_sends = work(second)
     first_far = swap(sends[0], 2)
+    left_far = swap(sends[1], 2)
     first_ready = ready(first, keeps[0], first_far)
-    first_ready, last_sends, parcel = after(first_ready, last_sends, parcel)
+    first_ready, last_sends = after(first_ready, last_sends)
     give(first_ready)
     second_far = swap(last_sends[0], 2)
-    near_far = swap(sends[1], 2)
+    right_far = swap(sends[2], 2)
     second_ready = ready(second, last_keeps[0], second_far)
+    left_ready = ready(left, keeps[1], left_far)
+    returned = {s: back[s] for s in first}
+    returned, left_ready, second_ready, parcel, last_parcel = after(
+        returned, left_ready, second_ready, parcel, last_parcel
+    )
     other = swap(parcel, 1)
-    returned = {s: back[s] for s in first}
-    returned, near_far, second_ready, other, last_parcel = after(
-        returned, near_far, second_ready, other, last_parcel
-    )
     back.update(returned)
     give(second_ready)
+    give(left_ready)
     last_other = swap(last_parcel, 1)
-    near_ready = ready(near, keeps[1], near_far)
-    last_other, near_ready = after(last_other, near_ready)
-    give(near_ready)
+    forth = second[0]
+    back[forth], right_far = after(back[forth], right_far)
+    right_ready = ready(right, keeps[2], right_far)
+    other, last_other, right_ready = after(other, last_other, right_ready)
+    give(right_ready)
     parcels = [parcel, last_parcel, other, last_other]
     grads = weight_grads(parcels, [units, last_units, None, None], tokens.shape[1])
     grads, back = after(list(grads), back)

time: 136 us -> 130 us (0.956)
  waiting for transfers between devices: 59.8 us -> 52.3 us
  starting transfers between devices: 40.4 us -> 45.3 us
  Pallas kernels: 29.6 us -> 26.3 us
    ppermute x30 -> x31, waiting for transfers between devices: 59.8 us -> 52.3 us  [swap(): lax.ppermute(value, AXES, [(i, i ^ distance) for i in range(device_count)])]
    ppermute x30 -> x31, starting transfers between devices: 40.4 us -> 45.3 us  [swap(): lax.ppermute(value, AXES, [(i, i ^ distance) for i in range(device_count)])]
    pallas_call x1, Pallas kernels: 9.43 us -> 6.19 us  [weight_grads(): pl.pallas_call(kernel, grid=(width // tile,), out_shape=[jax.ShapeDtypeSt...]
  transfers between devices with their start and end apart: 30 -> 31, of which waited for: 11 -> 13; matrix products, arithmetic and copies ran while one was open for 0% -> 0% of each run, Pallas kernels for 19% -> 18%
where the time goes in v4:
time: 130 us
  waiting for transfers between devices  52.3 us (40%)
  starting transfers between devices  45.3 us (35%)
  Pallas kernels  26.3 us (20%)
  local copies, waits for them, and re-layouts  5.24 us (4%)
    ppermute x31, waiting for transfers between devices, swap(): lax.ppermute(value, AXES, [(i, i ^ distance) for i in range(device_count)])  52.3 us
    ppermute x31, starting transfers between devices, swap(): lax.ppermute(value, AXES, [(i, i ^ distance) for i in range(device_count)])  45.3 us
    pallas_call x2, Pallas kernels, run_expert(): pl.pallas_call(functools.partial(expert_kernel, capacity, count, groups),...  14.7 us
    pallas_call x1, Pallas kernels, weight_grads(): pl.pallas_call(kernel, grid=(width // tile,), out_shape=[jax.ShapeDtypeSt...  6.19 us
    unnamed x20, local copies, waits for them, and re-layouts  5.24 us
    pallas_call x1, Pallas kernels, combine(): pl.pallas_call(functools.partial(combine_kernel, len(blocks), capacity),...  3.57 us
  transfers between devices with their start and end apart: 31, of which 13 were waited for; matrix products, arithmetic and copies ran while one was open for 0% of the time, Pallas kernels for 18%

profile of v4, /device:TPU:0, one launch (start us, length us, event | category | flops | bytes accessed | tf_op | source)
XLA Modules:
  0.0 129.9 jit_solution(15387458408989706661)
XLA Ops:
  6.9 4.7 %collective-permute-start.6 = (bf16[40,3584]{1,0:T(8,128)(2,1)S(1)}, bf16[40,3584]{1,0:T(8,128)(2,1)S(1)}, u32[]{:S(2)}, u32[]{:S(2)}) collective-permute-start(bf16[40,3584]{1,0:T(8,128)(2,1)S(1)} %get-tuple-element.119), channel_id=1, source_target_pairs={{0,24},{1,25},{2,26},{3,27},{4,28},{5,29},{6,30},{7,31},{8,16},{9,... | collective-permute-start | bytes 860168 | tf_op jit(solution)/shard_map/ppermute | solution.py:361
  11.7 1.6 %collective-permute-start.3 = (bf16[40,3584]{1,0:T(8,128)(2,1)S(1)}, bf16[40,3584]{1,0:T(8,128)(2,1)S(1)}, u32[]{:S(2)}, u32[]{:S(2)}) collective-permute-start(bf16[40,3584]{1,0:T(8,128)(2,1)S(1)} %get-tuple-element.116), channel_id=1, source_target_pairs={{0,4},{1,5},{2,6},{3,7},{4,0},{5,1},{6,2},{7,3},{8,12},{9,13},{10,... | collective-permute-start | bytes 860168 | tf_op jit(solution)/shard_map/ppermute | solution.py:361
  14.6 2.4 %collective-permute-start.7 = (bf16[40,3584]{1,0:T(8,128)(2,1)S(1)}, bf16[40,3584]{1,0:T(8,128)(2,1)S(1)}, u32[]{:S(2)}, u32[]{:S(2)}) collective-permute-start(bf16[40,3584]{1,0:T(8,128)(2,1)S(1)} %get-tuple-element.120), channel_id=1, source_target_pairs={{0,28},{1,29},{2,30},{3,31},{4,24},{5,25},{6,26},{7,27},{8,20},{9,... | collective-permute-start | bytes 860168 | tf_op jit(solution)/shard_map/ppermute | solution.py:361
  17.0 1.6 %collective-permute-start.5 = (bf16[40,3584]{1,0:T(8,128)(2,1)S(1)}, bf16[40,3584]{1,0:T(8,128)(2,1)S(1)}, u32[]{:S(2)}, u32[]{:S(2)}) collective-permute-start(bf16[40,3584]{1,0:T(8,128)(2,1)S(1)} %get-tuple-element.118), channel_id=1, source_target_pairs={{0,12},{1,13},{2,14},{3,15},{4,8},{5,9},{6,10},{7,11},{8,4},{9,5},... | collective-permute-start | bytes 860168 | tf_op jit(solution)/shard_map/ppermute | solution.py:361
  19.4 1.6 %collective-permute-start.8 = (bf16[40,3584]{1,0:T(8,128)(2,1)S(1)}, bf16[40,3584]{1,0:T(8,128)(2,1)S(1)}, u32[]{:S(2)}, u32[]{:S(2)}) collective-permute-start(bf16[40,3584]{1,0:T(8,128)(2,1)S(1)} %get-tuple-element.141.refs_2_), channel_id=1, source_target_pairs={{0,2},{1,3},{2,0},{3,1},{4,6},{5,7},{6,4},{7,5},{8,10},{9,11},{10,... | collective-permute-start | bytes 860168 | tf_op jit(solution)/shard_map/ppermute | solution.py:361
  22.1 9.2 %collective-permute-done.4.refs_4_ = bf16[40,3584]{1,0:T(8,128)(2,1)S(1)} collective-permute-done((bf16[40,3584]{1,0:T(8,128)(2,1)S(1)}, bf16[40,3584]{1,0:T(8,128)(2,1)S(1)}, u32[]{:S(2)}, u32[]{:S(2)}) %collective-permute-start.4) | collective-permute-done | bytes 286752 | tf_op jit(solution)/shard_map/ppermute | solution.py:361
  32.8 8.0 %collective-permute-done.5.refs_5_ = bf16[40,3584]{1,0:T(8,128)(2,1)S(1)} collective-permute-done((bf16[40,3584]{1,0:T(8,128)(2,1)S(1)}, bf16[40,3584]{1,0:T(8,128)(2,1)S(1)}, u32[]{:S(2)}, u32[]{:S(2)}) %collective-permute-start.5) | collective-permute-done | bytes 286752 | tf_op jit(solution)/shard_map/ppermute | solution.py:361
  40.8 2.4 %collective-permute-start.10 = (bf16[40,3584]{1,0:T(8,128)(2,1)S(1)}, bf16[40,3584]{1,0:T(8,128)(2,1)S(1)}, u32[]{:S(2)}, u32[]{:S(2)}) collective-permute-start(bf16[40,3584]{1,0:T(8,128)(2,1)S(1)} %get-tuple-element.133), channel_id=1, source_target_pairs={{0,16},{1,17},{2,18},{3,19},{4,20},{5,21},{6,22},{7,23},{8,24},{9,... | collective-permute-start | bytes 860168 | tf_op jit(solution)/shard_map/ppermute | solution.py:361
  48.2 15.5 %collective-permute-done.10.refs_0_ = bf16[40,3584]{1,0:T(8,128)(2,1)S(1)} collective-permute-done((bf16[40,3584]{1,0:T(8,128)(2,1)S(1)}, bf16[40,3584]{1,0:T(8,128)(2,1)S(1)}, u32[]{:S(2)}, u32[]{:S(2)}) %collective-permute-start.10) | collective-permute-done | bytes 286752 | tf_op jit(solution)/shard_map/ppermute | solution.py:361
  63.8 5.8 %collective-permute-done.11.refs_1_ = bf16[40,3584]{1,0:T(8,128)(2,1)S(1)} collective-permute-done((bf16[40,3584]{1,0:T(8,128)(2,1)S(1)}, bf16[40,3584]{1,0:T(8,128)(2,1)S(1)}, u32[]{:S(2)}, u32[]{:S(2)}) %collective-permute-start.11) | collective-permute-done | bytes 286752 | tf_op jit(solution)/shard_map/ppermute | solution.py:361
  69.5 1.6 %collective-permute-start.16 = (bf16[40,3584]{1,0:T(8,128)(2,1)S(1)}, bf16[40,3584]{1,0:T(8,128)(2,1)S(1)}, u32[]{:S(2)}, u32[]{:S(2)}) collective-permute-start(bf16[40,3584]{1,0:T(8,128)(2,1)S(1)} %collective-permute-done.10.refs_0_), channel_id=1, source_target_pairs={{0,2},{1,3},{2,0},{3,1},{4,6},{5,7},{6,4},{7,5},{8,10},{9,11},{10,... | collective-permute-start | bytes 860168 | tf_op jit(solution)/shard_map/ppermute | solution.py:361
  73.1 8.2 %run_expert.2 = (bf16[240,7936]{1,0:T(8,128)(2,1)S(1)}, bf16[240,768]{1,0:T(8,128)(2,1)S(1)}, bf16[40,3712]{1,0:T(8,128)(2,1)S(1)}, bf16[40,3712]{1,0:T(8,128)(2...) custom-call(bf16[40,3584]{1,0:T(8,128)(2,1)S(1)} %collective-permute, ...), custom_call_target="tpu_custom_call" | custom-call | flops 4404019200 | bytes 19611648 | tf_op jit(solution)/shard_map/run_expert/pallas_call | solution.py:167
  81.3 1.6 %collective-permute-start.18 = (bf16[40,3712]{1,0:T(8,128)(2,1)S(1)}, bf16[40,3712]{1,0:T(8,128)(2,1)S(1)}, u32[]{:S(2)}, u32[]{:S(2)}) collective-permute-start(bf16[40,3712]{1,0:T(8,128)(2,1)S(1)} %get-tuple-element.163), channel_id=1, source_target_pairs={{0,2},{1,3},{2,0},{3,1},{4,6},{5,7},{6,4},{7,5},{8,10},{9,11},{10,... | collective-permute-start | bytes 890888 | tf_op jit(solution)/shard_map/ppermute | solution.py:361
  84.3 6.5 %run_expert.3 = (bf16[80,7936]{1,0:T(8,128)(2,1)S(1)}, bf16[80,768]{1,0:T(8,128)(2,1)S(1)}, bf16[40,3712]{1,0:T(8,128)(2,1)S(1)}, bf16[40,3712]{1,0:T(8,128)(2,1)S(1)}) custom-call(bf16[40,3584]{1,0:T(8,128)(2,1)S(1)} %collective-permute-done.10.refs_0_, bf16[40,3584]{1,0:T(8,128)(2,1)S(1)} %collective-permute-done.11.refs_1_, ...), custom_call_target="tpu_custom_call" | custom-call | flops 1468006400 | bytes 13877248 | tf_op jit(solution)/shard_map/run_expert/pallas_call | solution.py:167
  91.5 1.6 %collective-permute-start.22 = (bf16[40,3712]{1,0:T(8,128)(2,1)S(1)}, bf16[40,3712]{1,0:T(8,128)(2,1)S(1)}, u32[]{:S(2)}, u32[]{:S(2)}) collective-permute-start(bf16[40,3712]{1,0:T(8,128)(2,1)S(1)} %get-tuple-element.176), channel_id=1, source_target_pairs={{0,2},{1,3},{2,0},{3,1},{4,6},{5,7},{6,4},{7,5},{8,10},{9,11},{10,... | collective-permute-start | bytes 890888 | tf_op jit(solution)/shard_map/ppermute | solution.py:361
  93.0 2.2 %collective-permute-start.19 = (bf16[40,1920]{1,0:T(8,128)(2,1)S(1)}, bf16[40,1920]{1,0:T(8,128)(2,1)S(1)}, u32[]{:S(2)}, u32[]{:S(2)}) collective-permute-start(bf16[40,1920]{1,0:T(8,128)(2,1)S(1)} %get-tuple-element.169), channel_id=1, source_target_pairs={{0,24},{1,25},{2,26},{3,27},{4,28},{5,29},{6,30},{7,31},{8,16},{9,... | collective-permute-start | bytes 460808 | tf_op jit(solution)/shard_map/ppermute | solution.py:361
  95.2 1.6 %collective-permute-start.20 = (bf16[40,1920]{1,0:T(8,128)(2,1)S(1)}, bf16[40,1920]{1,0:T(8,128)(2,1)S(1)}, u32[]{:S(2)}, u32[]{:S(2)}) collective-permute-start(bf16[40,1920]{1,0:T(8,128)(2,1)S(1)} %get-tuple-element.170), channel_id=1, source_target_pairs={{0,28},{1,29},{2,30},{3,31},{4,24},{5,25},{6,26},{7,27},{8,20},{9,... | collective-permute-start | bytes 460808 | tf_op jit(solution)/shard_map/ppermute | solution.py:361
  97.8 4.5 %collective-permute-done.22.far_ref = bf16[40,3712]{1,0:T(8,128)(2,1)S(1)} collective-permute-done((bf16[40,3712]{1,0:T(8,128)(2,1)S(1)}, bf16[40,3712]{1,0:T(8,128)(2,1)S(1)}, u32[]{:S(2)}, u32[]{:S(2)}) %collective-permute-start.22) | collective-permute-done | bytes 296992 | tf_op jit(solution)/shard_map/ppermute | solution.py:361
  104.6 3.1 %collective-permute-start.25 = (bf16[40,1920]{1,0:T(8,128)(2,1)S(1)}, bf16[40,1920]{1,0:T(8,128)(2,1)S(1)}, u32[]{:S(2)}, u32[]{:S(2)}) collective-permute-start(bf16[40,1920]{1,0:T(8,128)(2,1)S(1)} %get-tuple-element.184), channel_id=1, source_target_pairs={{0,16},{1,17},{2,18},{3,19},{4,20},{5,21},{6,22},{7,23},{8,24},{9,... | collective-permute-start | bytes 460808 | tf_op jit(solution)/shard_map/ppermute | solution.py:361
  108.5 4.2 %collective-permute-done.26.far_ref = bf16[40,3712]{1,0:T(8,128)(2,1)S(1)} collective-permute-done((bf16[40,3712]{1,0:T(8,128)(2,1)S(1)}, bf16[40,3712]{1,0:T(8,128)(2,1)S(1)}, u32[]{:S(2)}, u32[]{:S(2)}) %collective-permute-start.26) | collective-permute-done | bytes 296992 | tf_op jit(solution)/shard_map/ppermute | solution.py:361
  112.7 3.5 %collective-permute-start.30 = (bf16[40,1920]{1,0:T(8,128)(2,1)S(1)}, bf16[40,1920]{1,0:T(8,128)(2,1)S(1)}, u32[]{:S(2)}, u32[]{:S(2)}) collective-permute-start(bf16[40,1920]{1,0:T(8,128)(2,1)S(1)} %get-tuple-element.201), channel_id=1, source_target_pairs={{0,20},{1,21},{2,22},{3,23},{4,16},{5,17},{6,18},{7,19},{8,28},{9,... | collective-permute-start | bytes 460808 | tf_op jit(solution)/shard_map/ppermute | solution.py:361
  116.7 2.5 %collective-permute-start.29 = (bf16[40,1920]{1,0:T(8,128)(2,1)S(1)}, bf16[40,1920]{1,0:T(8,128)(2,1)S(1)}, u32[]{:S(2)}, u32[]{:S(2)}) collective-permute-start(bf16[40,1920]{1,0:T(8,128)(2,1)S(1)} %get-tuple-element.199), channel_id=1, source_target_pairs={{0,12},{1,13},{2,14},{3,15},{4,8},{5,9},{6,10},{7,11},{8,4},{9,5},... | collective-permute-start | bytes 460808 | tf_op jit(solution)/shard_map/ppermute | solution.py:361
  119.2 6.2 %weight_grads.1 = (bf16[3584,256]{1,0:T(8,128)(2,1)}, bf16[3584,256]{1,0:T(8,128)(2,1)}, bf16[256,3584]{1,0:T(8,128)(2,1)}) custom-call(bf16[240,7936]{1,0:T(8,128)(2,1)S(1)} %get-tuple-element.181.refs_0_, bf16[80,7936]{1,0:T(8,128)(2,1)S(1)} %get-tuple-element.182.refs_1_, bf16[240,7936]{1,0:T(8,128)(2,1)S(1)} %collective-permute-done.23.refs_2_, ...), custom_call_target="tpu_custom_call" | custom-call | flops 3523215360 | bytes 14680064 | tf_op jit(solution)/shard_map/weight_grads/pallas_call | solution.py:258
  126.3 3.6 %combine.1 = (bf16[128,3584]{1,0:T(8,128)(2,1)}, bf16[8,128]{1,0:T(8,128)(2,1)}) custom-call(s32[1]{0:T(128)} %bitcast.me_ref, s32[8,128]{1,0:T(8,128)S(1)} %bitcast.20, bf16[8,128]{1,0:T(8,128)(2,1)S(1)} %bitcast.22, bf16[40,1920]{1,0:T(8,128)(2,1)S(1)} %get-tuple-element.204.refs_0_, bf16[40,1920]{1,0:T(8,128)(2,1)S(1)} %collective-permute-done.27.refs_1_, ...), custom_call_target="tpu_custom_call" | custom-call | flops 1000000000 | bytes 3000000 | tf_op jit(solution)/shard_map/combine/pallas_call | solution.py:322
  (67 shorter events, 25.5 us)
Async XLA Ops:
  0.6 11.0 %collective-permute-start = (bf16[3584,256]{1,0:T(8,128)(2,1)}, bf16[3584,256]{1,0:T(8,128)(2,1)S(1)}, u32[]{:S(2)}, u32[]{:S(2)}) collective-permute-start(bf16[3584,256]{1,0:T(8,128)(2,1)} %bitcast.10), channel_id=1, source_target_pairs={{0,1},{1,0},{2,3},{3,2},{4,5},{5,4},{6,7},{7,6},{8,9},{9,8},{10,11... | collective-permute-start | bytes 5505032 | tf_op jit(solution)/shard_map/ppermute | solution.py:361
  1.1 10.5 %collective-permute-start.1 = (bf16[3584,256]{1,0:T(8,128)(2,1)}, bf16[3584,256]{1,0:T(8,128)(2,1)}, u32[]{:S(2)}, u32[]{:S(2)}) collective-permute-start(bf16[3584,256]{1,0:T(8,128)(2,1)} %bitcast.13), channel_id=1, source_target_pairs={{0,1},{1,0},{2,3},{3,2},{4,5},{5,4},{6,7},{7,6},{8,9},{9,8},{10,11... | collective-permute-start | bytes 5505032 | tf_op jit(solution)/shard_map/ppermute | solution.py:361
  1.2 10.4 %collective-permute-start.2 = (bf16[256,3584]{1,0:T(8,128)(2,1)}, bf16[256,3584]{1,0:T(8,128)(2,1)}, u32[]{:S(2)}, u32[]{:S(2)}) collective-permute-start(bf16[256,3584]{1,0:T(8,128)(2,1)} %bitcast.16), channel_id=1, source_target_pairs={{0,1},{1,0},{2,3},{3,2},{4,5},{5,4},{6,7},{7,6},{8,9},{9,8},{10,11... | collective-permute-start | bytes 5505032 | tf_op jit(solution)/shard_map/ppermute | solution.py:361
  6.9 12.5 %collective-permute-start.6 = (bf16[40,3584]{1,0:T(8,128)(2,1)S(1)}, bf16[40,3584]{1,0:T(8,128)(2,1)S(1)}, u32[]{:S(2)}, u32[]{:S(2)}) collective-permute-start(bf16[40,3584]{1,0:T(8,128)(2,1)S(1)} %get-tuple-element.119), channel_id=1, source_target_pairs={{0,24},{1,25},{2,26},{3,27},{4,28},{5,29},{6,30},{7,31},{8,16},{9,... | collective-permute-start | bytes 860168 | tf_op jit(solution)/shard_map/ppermute | solution.py:361
  13.2 18.1 %collective-permute-start.4 = (bf16[40,3584]{1,0:T(8,128)(2,1)S(1)}, bf16[40,3584]{1,0:T(8,128)(2,1)S(1)}, u32[]{:S(2)}, u32[]{:S(2)}) collective-permute-start(bf16[40,3584]{1,0:T(8,128)(2,1)S(1)} %get-tuple-element.117), channel_id=1, source_target_pairs={{0,8},{1,9},{2,10},{3,11},{4,12},{5,13},{6,14},{7,15},{8,0},{9,1},... | collective-permute-start | bytes 860168 | tf_op jit(solution)/shard_map/ppermute | solution.py:361
  14.6 18.2 %collective-permute-start.7 = (bf16[40,3584]{1,0:T(8,128)(2,1)S(1)}, bf16[40,3584]{1,0:T(8,128)(2,1)S(1)}, u32[]{:S(2)}, u32[]{:S(2)}) collective-permute-start(bf16[40,3584]{1,0:T(8,128)(2,1)S(1)} %get-tuple-element.120), channel_id=1, source_target_pairs={{0,28},{1,29},{2,30},{3,31},{4,24},{5,25},{6,26},{7,27},{8,20},{9,... | collective-permute-start | bytes 860168 | tf_op jit(solution)/shard_map/ppermute | solution.py:361
  17.0 23.8 %collective-permute-start.5 = (bf16[40,3584]{1,0:T(8,128)(2,1)S(1)}, bf16[40,3584]{1,0:T(8,128)(2,1)S(1)}, u32[]{:S(2)}, u32[]{:S(2)}) collective-permute-start(bf16[40,3584]{1,0:T(8,128)(2,1)S(1)} %get-tuple-element.118), channel_id=1, source_target_pairs={{0,12},{1,13},{2,14},{3,15},{4,8},{5,9},{6,10},{7,11},{8,4},{9,5},... | collective-permute-start | bytes 860168 | tf_op jit(solution)/shard_map/ppermute | solution.py:361
  19.4 21.4 %collective-permute-start.8 = (bf16[40,3584]{1,0:T(8,128)(2,1)S(1)}, bf16[40,3584]{1,0:T(8,128)(2,1)S(1)}, u32[]{:S(2)}, u32[]{:S(2)}) collective-permute-start(bf16[40,3584]{1,0:T(8,128)(2,1)S(1)} %get-tuple-element.141.refs_2_), channel_id=1, source_target_pairs={{0,2},{1,3},{2,0},{3,1},{4,6},{5,7},{6,4},{7,5},{8,10},{9,11},{10,... | collective-permute-start | bytes 860168 | tf_op jit(solution)/shard_map/ppermute | solution.py:361
  21.1 19.8 %collective-permute-start.9 = (bf16[40,3584]{1,0:T(8,128)(2,1)S(1)}, bf16[40,3584]{1,0:T(8,128)(2,1)S(1)}, u32[]{:S(2)}, u32[]{:S(2)}) collective-permute-start(bf16[40,3584]{1,0:T(8,128)(2,1)S(1)} %collective-permute-done.3.refs_3_), channel_id=1, source_target_pairs={{0,2},{1,3},{2,0},{3,1},{4,6},{5,7},{6,4},{7,5},{8,10},{9,11},{10,... | collective-permute-start | bytes 860168 | tf_op jit(solution)/shard_map/ppermute | solution.py:361
  31.4 15.4 %collective-permute-start.12 = (bf16[40,3584]{1,0:T(8,128)(2,1)S(1)}, bf16[40,3584]{1,0:T(8,128)(2,1)S(1)}, u32[]{:S(2)}, u32[]{:S(2)}) collective-permute-start(bf16[40,3584]{1,0:T(8,128)(2,1)S(1)} %collective-permute-done.4.refs_4_), channel_id=1, source_target_pairs={{0,2},{1,3},{2,0},{3,1},{4,6},{5,7},{6,4},{7,5},{8,10},{9,11},{10,... | collective-permute-start | bytes 860168 | tf_op jit(solution)/shard_map/ppermute | solution.py:361
  40.8 22.9 %collective-permute-start.10 = (bf16[40,3584]{1,0:T(8,128)(2,1)S(1)}, bf16[40,3584]{1,0:T(8,128)(2,1)S(1)}, u32[]{:S(2)}, u32[]{:S(2)}) collective-permute-start(bf16[40,3584]{1,0:T(8,128)(2,1)S(1)} %get-tuple-element.133), channel_id=1, source_target_pairs={{0,16},{1,17},{2,18},{3,19},{4,20},{5,21},{6,22},{7,23},{8,24},{9,... | collective-permute-start | bytes 860168 | tf_op jit(solution)/shard_map/ppermute | solution.py:361
  43.2 26.3 %collective-permute-start.11 = (bf16[40,3584]{1,0:T(8,128)(2,1)S(1)}, bf16[40,3584]{1,0:T(8,128)(2,1)S(1)}, u32[]{:S(2)}, u32[]{:S(2)}) collective-permute-start(bf16[40,3584]{1,0:T(8,128)(2,1)S(1)} %get-tuple-element.134), channel_id=1, source_target_pairs={{0,20},{1,21},{2,22},{3,23},{4,16},{5,17},{6,18},{7,19},{8,28},{9,... | collective-permute-start | bytes 860168 | tf_op jit(solution)/shard_map/ppermute | solution.py:361
  44.7 24.8 %collective-permute-start.13 = (bf16[40,3584]{1,0:T(8,128)(2,1)S(1)}, bf16[40,3584]{1,0:T(8,128)(2,1)S(1)}, u32[]{:S(2)}, u32[]{:S(2)}) collective-permute-start(bf16[40,3584]{1,0:T(8,128)(2,1)S(1)} %collective-permute-done.5.refs_5_), channel_id=1, source_target_pairs={{0,2},{1,3},{2,0},{3,1},{4,6},{5,7},{6,4},{7,5},{8,10},{9,11},{10,... | collective-permute-start | bytes 860168 | tf_op jit(solution)/shard_map/ppermute | solution.py:361
  46.2 23.3 %collective-permute-start.14 = (bf16[40,3584]{1,0:T(8,128)(2,1)S(1)}, bf16[40,3584]{1,0:T(8,128)(2,1)S(1)}, u32[]{:S(2)}, u32[]{:S(2)}) collective-permute-start(bf16[40,3584]{1,0:T(8,128)(2,1)S(1)} %collective-permute-done.6.refs_0_), channel_id=1, source_target_pairs={{0,2},{1,3},{2,0},{3,1},{4,6},{5,7},{6,4},{7,5},{8,10},{9,11},{10,... | collective-permute-start | bytes 860168 | tf_op jit(solution)/shard_map/ppermute | solution.py:361
  46.8 22.8 %collective-permute-start.15 = (bf16[40,3584]{1,0:T(8,128)(2,1)S(1)}, bf16[40,3584]{1,0:T(8,128)(2,1)S(1)}, u32[]{:S(2)}, u32[]{:S(2)}) collective-permute-start(bf16[40,3584]{1,0:T(8,128)(2,1)S(1)} %collective-permute-done.7.refs_1_), channel_id=1, source_target_pairs={{0,2},{1,3},{2,0},{3,1},{4,6},{5,7},{6,4},{7,5},{8,10},{9,11},{10,... | collective-permute-start | bytes 860168 | tf_op jit(solution)/shard_map/ppermute | solution.py:361
  69.5 13.9 %collective-permute-start.16 = (bf16[40,3584]{1,0:T(8,128)(2,1)S(1)}, bf16[40,3584]{1,0:T(8,128)(2,1)S(1)}, u32[]{:S(2)}, u32[]{:S(2)}) collective-permute-start(bf16[40,3584]{1,0:T(8,128)(2,1)S(1)} %collective-permute-done.10.refs_0_), channel_id=1, source_target_pairs={{0,2},{1,3},{2,0},{3,1},{4,6},{5,7},{6,4},{7,5},{8,10},{9,11},{10,... | collective-permute-start | bytes 860168 | tf_op jit(solution)/shard_map/ppermute | solution.py:361
  71.1 13.1 %collective-permute-start.17 = (bf16[40,3584]{1,0:T(8,128)(2,1)S(1)}, bf16[40,3584]{1,0:T(8,128)(2,1)S(1)}, u32[]{:S(2)}, u32[]{:S(2)}) collective-permute-start(bf16[40,3584]{1,0:T(8,128)(2,1)S(1)} %collective-permute-done.11.refs_1_), channel_id=1, source_target_pairs={{0,2},{1,3},{2,0},{3,1},{4,6},{5,7},{6,4},{7,5},{8,10},{9,11},{10,... | collective-permute-start | bytes 860168 | tf_op jit(solution)/shard_map/ppermute | solution.py:361
  82.9 14.9 %collective-permute-start.21 = (bf16[40,3712]{1,0:T(8,128)(2,1)S(1)}, bf16[40,3712]{1,0:T(8,128)(2,1)S(1)}, u32[]{:S(2)}, u32[]{:S(2)}) collective-permute-start(bf16[40,3712]{1,0:T(8,128)(2,1)S(1)} %get-tuple-element.172), channel_id=1, source_target_pairs={{0,2},{1,3},{2,0},{3,1},{4,6},{5,7},{6,4},{7,5},{8,10},{9,11},{10,... | collective-permute-start | bytes 890888 | tf_op jit(solution)/shard_map/ppermute | solution.py:361
  91.5 10.9 %collective-permute-start.22 = (bf16[40,3712]{1,0:T(8,128)(2,1)S(1)}, bf16[40,3712]{1,0:T(8,128)(2,1)S(1)}, u32[]{:S(2)}, u32[]{:S(2)}) collective-permute-start(bf16[40,3712]{1,0:T(8,128)(2,1)S(1)} %get-tuple-element.176), channel_id=1, source_target_pairs={{0,2},{1,3},{2,0},{3,1},{4,6},{5,7},{6,4},{7,5},{8,10},{9,11},{10,... | collective-permute-start | bytes 890888 | tf_op jit(solution)/shard_map/ppermute | solution.py:361
  103.2 13.1 %collective-permute-start.23 = (bf16[240,7936]{1,0:T(8,128)(2,1)S(1)}, bf16[240,7936]{1,0:T(8,128)(2,1)S(1)}, u32[]{:S(2)}, u32[]{:S(2)}) collective-permute-start(bf16[240,7936]{1,0:T(8,128)(2,1)S(1)} %get-tuple-element.181.refs_0_), channel_id=1, source_target_pairs={{0,1},{1,0},{2,3},{3,2},{4,5},{5,4},{6,7},{7,6},{8,9},{9,8},{10,11... | collective-permute-start | bytes 11427848 | tf_op jit(solution)/shard_map/ppermute | solution.py:361
  103.2 13.1 %collective-permute-start.24 = (bf16[80,7936]{1,0:T(8,128)(2,1)S(1)}, bf16[80,7936]{1,0:T(8,128)(2,1)S(1)}, u32[]{:S(2)}, u32[]{:S(2)}) collective-permute-start(bf16[80,7936]{1,0:T(8,128)(2,1)S(1)} %get-tuple-element.182.refs_1_), channel_id=1, source_target_pairs={{0,1},{1,0},{2,3},{3,2},{4,5},{5,4},{6,7},{7,6},{8,9},{9,8},{10,11... | collective-permute-start | bytes 3809288 | tf_op jit(solution)/shard_map/ppermute | solution.py:361
  104.6 11.7 %collective-permute-start.25 = (bf16[40,1920]{1,0:T(8,128)(2,1)S(1)}, bf16[40,1920]{1,0:T(8,128)(2,1)S(1)}, u32[]{:S(2)}, u32[]{:S(2)}) collective-permute-start(bf16[40,1920]{1,0:T(8,128)(2,1)S(1)} %get-tuple-element.184), channel_id=1, source_target_pairs={{0,16},{1,17},{2,18},{3,19},{4,20},{5,21},{6,22},{7,23},{8,24},{9,... | collective-permute-start | bytes 460808 | tf_op jit(solution)/shard_map/ppermute | solution.py:361
  107.7 17.7 %collective-permute-start.27 = (bf16[40,1920]{1,0:T(8,128)(2,1)S(1)}, bf16[40,1920]{1,0:T(8,128)(2,1)S(1)}, u32[]{:S(2)}, u32[]{:S(2)}) collective-permute-start(bf16[40,1920]{1,0:T(8,128)(2,1)S(1)} %get-tuple-element.197), channel_id=1, source_target_pairs={{0,4},{1,5},{2,6},{3,7},{4,0},{5,1},{6,2},{7,3},{8,12},{9,13},{10,... | collective-permute-start | bytes 460808 | tf_op jit(solution)/shard_map/ppermute | solution.py:361
  112.7 12.7 %collective-permute-start.30 = (bf16[40,1920]{1,0:T(8,128)(2,1)S(1)}, bf16[40,1920]{1,0:T(8,128)(2,1)S(1)}, u32[]{:S(2)}, u32[]{:S(2)}) collective-permute-start(bf16[40,1920]{1,0:T(8,128)(2,1)S(1)} %get-tuple-element.201), channel_id=1, source_target_pairs={{0,20},{1,21},{2,22},{3,23},{4,16},{5,17},{6,18},{7,19},{8,28},{9,... | collective-permute-start | bytes 460808 | tf_op jit(solution)/shard_map/ppermute | solution.py:361
  (17 other events, 227.6 us)

commit v5 on v4

--- a/solution.py
+++ b/solution.py
@@ -286,27 +286,30 @@
     hits, slot_t = find_slots(expert_count, me_ref[0], ids_ref[...])
     slots[...] = jnp.full(slots.shape, -1.0, jnp.float32)
     slots[0:expert_count, :] = slot_t
-    slot = slots[...].T.astype(jnp.int32)
-    lane = lax.broadcasted_iota(jnp.int32, (rows, slots.shape[0]), 1)
-    index = lax.broadcasted_iota(jnp.int32, (rows, 2 * capacity), 1)
-    picks = []
-    for s in range(expert_count):
-        column = slot[:, s : s + 1]
-        low = jnp.where(column == index, 1.0, 0.0)
-        high = jnp.where((column >= 0) & (column + capacity == index), 1.0, 0.0)
-        picks.append(jnp.concatenate([low, high], axis=0).astype(jnp.bfloat16))
+    block = 2 * capacity
+    columns = expert_count * block
+    column = lax.broadcasted_iota(jnp.int32, (slots.shape[0], columns), 1)
+    source = lax.broadcasted_iota(jnp.int32, (slots.shape[0], columns), 0)
+    spread = (column >= source * block) & (column < (source + 1) * block)
+    spread = spread.astype(jnp.float32).astype(jnp.bfloat16)
+    slot = jnp.dot(slots[...].T.astype(jnp.bfloat16), spread, preferred_element_type=jnp.float32)
+    index = (lax.broadcasted_iota(jnp.int32, (rows, columns), 1) % block).astype(jnp.float32)
+    low = jnp.where(slot == index, 1.0, 0.0)
+    high = jnp.where((slot >= 0.0) & (slot + capacity == index), 1.0, 0.0)
+    picks = jnp.concatenate([low, high], axis=0).astype(jnp.bfloat16)
     for start, size in chunks(half, 896):
-        part = jnp.zeros((2 * rows, size), jnp.float32)
-        for s in range(expert_count):
-            part += jnp.dot(
-                picks[s], blocks[s][:, start : start + size], preferred_element_type=jnp.float32
-            )
+        rows_in = jnp.concatenate([ref[:, start : start + size] for ref in blocks], axis=0)
+        part = jnp.dot(picks, rows_in, preferred_element_type=jnp.float32)
         tok_ref[:, start : start + size] = part[:rows].astype(jnp.bfloat16)
         tok_ref[:, half + start : half + start + size] = part[rows:].astype(jnp.bfloat16)
-    value = jnp.zeros((rows, slots.shape[0]), jnp.float32)
-    for s in range(expert_count):
-        found = jnp.dot(picks[s], blocks[s][:, half:], preferred_element_type=jnp.float32)
-        value = jnp.where(lane == s, found[:rows, 0:1], value)
+    lane = lax.broadcasted_iota(jnp.int32, (block, slots.shape[0]), 1)
+    apart = [
+        jnp.where(lane == s, ref[:, half:].astype(jnp.float32), 0.0).astype(jnp.bfloat16)
+        for s, ref in enumerate(blocks)
+    ]
+    value = jnp.dot(
+        picks[:rows], jnp.concatenate(apart, axis=0), preferred_element_type=jnp.float32
+    )
     values[...] = value.T
     value_t = values[0:expert_count, :]
     weights = weight_ref[...].astype(jnp.float32)
@@ -434,7 +437,6 @@
     give(right_ready)
     parcels = [parcel, last_parcel, other, last_other]
     grads = weight_grads(parcels, [units, last_units, None, None], tokens.shape[1])
-    grads, back = after(list(grads), back)
     grad_gate, grad_up, grad_down = grads
     grad_tokens, grad_route_t = combine(
         me, ids_t, weights_t, [back[s] for s in range(expert_count)], capacity

time: 130 us -> 128 us (0.985)
  Pallas kernels: 26.3 us -> 24.7 us
    pallas_call x1, Pallas kernels: 3.57 us -> 1.92 us  [combine(): pl.pallas_call(functools.partial(combine_kernel, len(blocks), capacity),...]
where the time goes in v5:
time: 128 us
  waiting for transfers between devices  52 us (41%)
  starting transfers between devices  45.5 us (36%)
  Pallas kernels  24.7 us (19%)
  local copies, waits for them, and re-layouts  5.24 us (4%)
    ppermute x31, waiting for transfers between devices, swap(): lax.ppermute(value, AXES, [(i, i ^ distance) for i in range(device_count)])  52 us
    ppermute x31, starting transfers between devices, swap(): lax.ppermute(value, AXES, [(i, i ^ distance) for i in range(device_count)])  45.5 us
    pallas_call x2, Pallas kernels, run_expert(): pl.pallas_call(functools.partial(expert_kernel, capacity, count, groups),...  14.7 us
    pallas_call x1, Pallas kernels, weight_grads(): pl.pallas_call(kernel, grid=(width // tile,), out_shape=[jax.ShapeDtypeSt...  6.19 us
    unnamed x20, local copies, waits for them, and re-layouts  5.24 us
  transfers between devices with their start and end apart: 31, of which 13 were waited for; matrix products, arithmetic and copies ran while one was open for 0% of the time, Pallas kernels for 18%

profile of v5, /device:TPU:0, one launch (start us, length us, event | category | flops | bytes accessed | tf_op | source)
XLA Modules:
  0.0 128.2 jit_solution(14419155619760469954)
XLA Ops:
  6.9 4.7 %collective-permute-start.6 = (bf16[40,3584]{1,0:T(8,128)(2,1)S(1)}, bf16[40,3584]{1,0:T(8,128)(2,1)S(1)}, u32[]{:S(2)}, u32[]{:S(2)}) collective-permute-start(bf16[40,3584]{1,0:T(8,128)(2,1)S(1)} %get-tuple-element.108), channel_id=1, source_target_pairs={{0,24},{1,25},{2,26},{3,27},{4,28},{5,29},{6,30},{7,31},{8,16},{9,... | collective-permute-start | bytes 860168 | tf_op jit(solution)/shard_map/ppermute | solution.py:364
  11.7 1.6 %collective-permute-start.3 = (bf16[40,3584]{1,0:T(8,128)(2,1)S(1)}, bf16[40,3584]{1,0:T(8,128)(2,1)S(1)}, u32[]{:S(2)}, u32[]{:S(2)}) collective-permute-start(bf16[40,3584]{1,0:T(8,128)(2,1)S(1)} %get-tuple-element.105), channel_id=1, source_target_pairs={{0,4},{1,5},{2,6},{3,7},{4,0},{5,1},{6,2},{7,3},{8,12},{9,13},{10,... | collective-permute-start | bytes 860168 | tf_op jit(solution)/shard_map/ppermute | solution.py:364
  14.6 2.4 %collective-permute-start.7 = (bf16[40,3584]{1,0:T(8,128)(2,1)S(1)}, bf16[40,3584]{1,0:T(8,128)(2,1)S(1)}, u32[]{:S(2)}, u32[]{:S(2)}) collective-permute-start(bf16[40,3584]{1,0:T(8,128)(2,1)S(1)} %get-tuple-element.109), channel_id=1, source_target_pairs={{0,28},{1,29},{2,30},{3,31},{4,24},{5,25},{6,26},{7,27},{8,20},{9,... | collective-permute-start | bytes 860168 | tf_op jit(solution)/shard_map/ppermute | solution.py:364
  17.0 1.6 %collective-permute-start.5 = (bf16[40,3584]{1,0:T(8,128)(2,1)S(1)}, bf16[40,3584]{1,0:T(8,128)(2,1)S(1)}, u32[]{:S(2)}, u32[]{:S(2)}) collective-permute-start(bf16[40,3584]{1,0:T(8,128)(2,1)S(1)} %get-tuple-element.107), channel_id=1, source_target_pairs={{0,12},{1,13},{2,14},{3,15},{4,8},{5,9},{6,10},{7,11},{8,4},{9,5},... | collective-permute-start | bytes 860168 | tf_op jit(solution)/shard_map/ppermute | solution.py:364
  19.4 1.6 %collective-permute-start.8 = (bf16[40,3584]{1,0:T(8,128)(2,1)S(1)}, bf16[40,3584]{1,0:T(8,128)(2,1)S(1)}, u32[]{:S(2)}, u32[]{:S(2)}) collective-permute-start(bf16[40,3584]{1,0:T(8,128)(2,1)S(1)} %get-tuple-element.130.refs_2_), channel_id=1, source_target_pairs={{0,2},{1,3},{2,0},{3,1},{4,6},{5,7},{6,4},{7,5},{8,10},{9,11},{10,... | collective-permute-start | bytes 860168 | tf_op jit(solution)/shard_map/ppermute | solution.py:364
  22.1 9.2 %collective-permute-done.4.refs_4_ = bf16[40,3584]{1,0:T(8,128)(2,1)S(1)} collective-permute-done((bf16[40,3584]{1,0:T(8,128)(2,1)S(1)}, bf16[40,3584]{1,0:T(8,128)(2,1)S(1)}, u32[]{:S(2)}, u32[]{:S(2)}) %collective-permute-start.4) | collective-permute-done | bytes 286752 | tf_op jit(solution)/shard_map/ppermute | solution.py:364
  32.8 8.0 %collective-permute-done.5.refs_5_ = bf16[40,3584]{1,0:T(8,128)(2,1)S(1)} collective-permute-done((bf16[40,3584]{1,0:T(8,128)(2,1)S(1)}, bf16[40,3584]{1,0:T(8,128)(2,1)S(1)}, u32[]{:S(2)}, u32[]{:S(2)}) %collective-permute-start.5) | collective-permute-done | bytes 286752 | tf_op jit(solution)/shard_map/ppermute | solution.py:364
  40.8 2.4 %collective-permute-start.10 = (bf16[40,3584]{1,0:T(8,128)(2,1)S(1)}, bf16[40,3584]{1,0:T(8,128)(2,1)S(1)}, u32[]{:S(2)}, u32[]{:S(2)}) collective-permute-start(bf16[40,3584]{1,0:T(8,128)(2,1)S(1)} %get-tuple-element.122), channel_id=1, source_target_pairs={{0,16},{1,17},{2,18},{3,19},{4,20},{5,21},{6,22},{7,23},{8,24},{9,... | collective-permute-start | bytes 860168 | tf_op jit(solution)/shard_map/ppermute | solution.py:364
  48.2 15.5 %collective-permute-done.10.refs_0_ = bf16[40,3584]{1,0:T(8,128)(2,1)S(1)} collective-permute-done((bf16[40,3584]{1,0:T(8,128)(2,1)S(1)}, bf16[40,3584]{1,0:T(8,128)(2,1)S(1)}, u32[]{:S(2)}, u32[]{:S(2)}) %collective-permute-start.10) | collective-permute-done | bytes 286752 | tf_op jit(solution)/shard_map/ppermute | solution.py:364
  63.8 5.7 %collective-permute-done.11.refs_1_ = bf16[40,3584]{1,0:T(8,128)(2,1)S(1)} collective-permute-done((bf16[40,3584]{1,0:T(8,128)(2,1)S(1)}, bf16[40,3584]{1,0:T(8,128)(2,1)S(1)}, u32[]{:S(2)}, u32[]{:S(2)}) %collective-permute-start.11) | collective-permute-done | bytes 286752 | tf_op jit(solution)/shard_map/ppermute | solution.py:364
  69.5 1.6 %collective-permute-start.16 = (bf16[40,3584]{1,0:T(8,128)(2,1)S(1)}, bf16[40,3584]{1,0:T(8,128)(2,1)S(1)}, u32[]{:S(2)}, u32[]{:S(2)}) collective-permute-start(bf16[40,3584]{1,0:T(8,128)(2,1)S(1)} %collective-permute-done.10.refs_0_), channel_id=1, source_target_pairs={{0,2},{1,3},{2,0},{3,1},{4,6},{5,7},{6,4},{7,5},{8,10},{9,11},{10,... | collective-permute-start | bytes 860168 | tf_op jit(solution)/shard_map/ppermute | solution.py:364
  73.1 8.2 %run_expert.2 = (bf16[240,7936]{1,0:T(8,128)(2,1)S(1)}, bf16[240,768]{1,0:T(8,128)(2,1)S(1)}, bf16[40,3712]{1,0:T(8,128)(2,1)S(1)}, bf16[40,3712]{1,0:T(8,128)(2...) custom-call(bf16[40,3584]{1,0:T(8,128)(2,1)S(1)} %collective-permute, ...), custom_call_target="tpu_custom_call" | custom-call | flops 4404019200 | bytes 19611648 | tf_op jit(solution)/shard_map/run_expert/pallas_call | solution.py:167
  81.3 1.6 %collective-permute-start.18 = (bf16[40,3712]{1,0:T(8,128)(2,1)S(1)}, bf16[40,3712]{1,0:T(8,128)(2,1)S(1)}, u32[]{:S(2)}, u32[]{:S(2)}) collective-permute-start(bf16[40,3712]{1,0:T(8,128)(2,1)S(1)} %get-tuple-element.152), channel_id=1, source_target_pairs={{0,2},{1,3},{2,0},{3,1},{4,6},{5,7},{6,4},{7,5},{8,10},{9,11},{10,... | collective-permute-start | bytes 890888 | tf_op jit(solution)/shard_map/ppermute | solution.py:364
  84.2 6.5 %run_expert.3 = (bf16[80,7936]{1,0:T(8,128)(2,1)S(1)}, bf16[80,768]{1,0:T(8,128)(2,1)S(1)}, bf16[40,3712]{1,0:T(8,128)(2,1)S(1)}, bf16[40,3712]{1,0:T(8,128)(2,1)S(1)}) custom-call(bf16[40,3584]{1,0:T(8,128)(2,1)S(1)} %collective-permute-done.10.refs_0_, bf16[40,3584]{1,0:T(8,128)(2,1)S(1)} %collective-permute-done.11.refs_1_, ...), custom_call_target="tpu_custom_call" | custom-call | flops 1468006400 | bytes 13877248 | tf_op jit(solution)/shard_map/run_expert/pallas_call | solution.py:167
  91.5 1.6 %collective-permute-start.22 = (bf16[40,3712]{1,0:T(8,128)(2,1)S(1)}, bf16[40,3712]{1,0:T(8,128)(2,1)S(1)}, u32[]{:S(2)}, u32[]{:S(2)}) collective-permute-start(bf16[40,3712]{1,0:T(8,128)(2,1)S(1)} %get-tuple-element.165), channel_id=1, source_target_pairs={{0,2},{1,3},{2,0},{3,1},{4,6},{5,7},{6,4},{7,5},{8,10},{9,11},{10,... | collective-permute-start | bytes 890888 | tf_op jit(solution)/shard_map/ppermute | solution.py:364
  93.0 2.2 %collective-permute-start.19 = (bf16[40,1920]{1,0:T(8,128)(2,1)S(1)}, bf16[40,1920]{1,0:T(8,128)(2,1)S(1)}, u32[]{:S(2)}, u32[]{:S(2)}) collective-permute-start(bf16[40,1920]{1,0:T(8,128)(2,1)S(1)} %get-tuple-element.158), channel_id=1, source_target_pairs={{0,24},{1,25},{2,26},{3,27},{4,28},{5,29},{6,30},{7,31},{8,16},{9,... | collective-permute-start | bytes 460808 | tf_op jit(solution)/shard_map/ppermute | solution.py:364
  95.2 1.6 %collective-permute-start.20 = (bf16[40,1920]{1,0:T(8,128)(2,1)S(1)}, bf16[40,1920]{1,0:T(8,128)(2,1)S(1)}, u32[]{:S(2)}, u32[]{:S(2)}) collective-permute-start(bf16[40,1920]{1,0:T(8,128)(2,1)S(1)} %get-tuple-element.159), channel_id=1, source_target_pairs={{0,28},{1,29},{2,30},{3,31},{4,24},{5,25},{6,26},{7,27},{8,20},{9,... | collective-permute-start | bytes 460808 | tf_op jit(solution)/shard_map/ppermute | solution.py:364
  97.8 4.5 %collective-permute-done.22.far_ref = bf16[40,3712]{1,0:T(8,128)(2,1)S(1)} collective-permute-done((bf16[40,3712]{1,0:T(8,128)(2,1)S(1)}, bf16[40,3712]{1,0:T(8,128)(2,1)S(1)}, u32[]{:S(2)}, u32[]{:S(2)}) %collective-permute-start.22) | collective-permute-done | bytes 296992 | tf_op jit(solution)/shard_map/ppermute | solution.py:364
  104.5 3.2 %collective-permute-start.26 = (bf16[40,1920]{1,0:T(8,128)(2,1)S(1)}, bf16[40,1920]{1,0:T(8,128)(2,1)S(1)}, u32[]{:S(2)}, u32[]{:S(2)}) collective-permute-start(bf16[40,1920]{1,0:T(8,128)(2,1)S(1)} %get-tuple-element.175), channel_id=1, source_target_pairs={{0,16},{1,17},{2,18},{3,19},{4,20},{5,21},{6,22},{7,23},{8,24},{9,... | collective-permute-start | bytes 460808 | tf_op jit(solution)/shard_map/ppermute | solution.py:364
  108.5 4.1 %collective-permute-done.27.far_ref = bf16[40,3712]{1,0:T(8,128)(2,1)S(1)} collective-permute-done((bf16[40,3712]{1,0:T(8,128)(2,1)S(1)}, bf16[40,3712]{1,0:T(8,128)(2,1)S(1)}, u32[]{:S(2)}, u32[]{:S(2)}) %collective-permute-start.27) | collective-permute-done | bytes 296992 | tf_op jit(solution)/shard_map/ppermute | solution.py:364
  112.7 3.6 %collective-permute-start.30 = (bf16[40,1920]{1,0:T(8,128)(2,1)S(1)}, bf16[40,1920]{1,0:T(8,128)(2,1)S(1)}, u32[]{:S(2)}, u32[]{:S(2)}) collective-permute-start(bf16[40,1920]{1,0:T(8,128)(2,1)S(1)} %get-tuple-element.183), channel_id=1, source_target_pairs={{0,20},{1,21},{2,22},{3,23},{4,16},{5,17},{6,18},{7,19},{8,28},{9,... | collective-permute-start | bytes 460808 | tf_op jit(solution)/shard_map/ppermute | solution.py:364
  116.7 2.5 %collective-permute-start.29 = (bf16[40,1920]{1,0:T(8,128)(2,1)S(1)}, bf16[40,1920]{1,0:T(8,128)(2,1)S(1)}, u32[]{:S(2)}, u32[]{:S(2)}) collective-permute-start(bf16[40,1920]{1,0:T(8,128)(2,1)S(1)} %get-tuple-element.181), channel_id=1, source_target_pairs={{0,12},{1,13},{2,14},{3,15},{4,8},{5,9},{6,10},{7,11},{8,4},{9,5},... | collective-permute-start | bytes 460808 | tf_op jit(solution)/shard_map/ppermute | solution.py:364
  119.2 6.2 %weight_grads.1 = (bf16[3584,256]{1,0:T(8,128)(2,1)}, bf16[3584,256]{1,0:T(8,128)(2,1)}, bf16[256,3584]{1,0:T(8,128)(2,1)}) custom-call(bf16[240,7936]{1,0:T(8,128)(2,1)S(1)} %get-tuple-element.172.refs_0_, bf16[80,7936]{1,0:T(8,128)(2,1)S(1)} %get-tuple-element.173.refs_1_, bf16[240,7936]{1,0:T(8,128)(2,1)S(1)} %collective-permute-done.24.refs_2_, ...), custom_call_target="tpu_custom_call" | custom-call | flops 3523215360 | bytes 14680064 | tf_op jit(solution)/shard_map/weight_grads/pallas_call | solution.py:258
  126.3 1.9 %combine.1 = (bf16[128,3584]{1,0:T(8,128)(2,1)}, bf16[8,128]{1,0:T(8,128)(2,1)}) custom-call(s32[1]{0:T(128)} %bitcast.me_ref, s32[8,128]{1,0:T(8,128)S(1)} %bitcast.20, bf16[8,128]{1,0:T(8,128)(2,1)S(1)} %bitcast.22, bf16[40,1920]{1,0:T(8,128)(2,1)S(1)} %get-tuple-element.170.refs_0_, bf16[40,1920]{1,0:T(8,128)(2,1)S(1)} %collective-permute-done.23.refs_1_, ...), custom_call_target="tpu_custom_call" | custom-call | flops 1000000000 | bytes 3000000 | tf_op jit(solution)/shard_map/combine/pallas_call | solution.py:325
  (67 shorter events, 25.4 us)
Async XLA Ops:
  0.6 11.0 %collective-permute-start = (bf16[3584,256]{1,0:T(8,128)(2,1)}, bf16[3584,256]{1,0:T(8,128)(2,1)S(1)}, u32[]{:S(2)}, u32[]{:S(2)}) collective-permute-start(bf16[3584,256]{1,0:T(8,128)(2,1)} %bitcast.10), channel_id=1, source_target_pairs={{0,1},{1,0},{2,3},{3,2},{4,5},{5,4},{6,7},{7,6},{8,9},{9,8},{10,11... | collective-permute-start | bytes 5505032 | tf_op jit(solution)/shard_map/ppermute | solution.py:364
  1.1 10.5 %collective-permute-start.1 = (bf16[3584,256]{1,0:T(8,128)(2,1)}, bf16[3584,256]{1,0:T(8,128)(2,1)}, u32[]{:S(2)}, u32[]{:S(2)}) collective-permute-start(bf16[3584,256]{1,0:T(8,128)(2,1)} %bitcast.13), channel_id=1, source_target_pairs={{0,1},{1,0},{2,3},{3,2},{4,5},{5,4},{6,7},{7,6},{8,9},{9,8},{10,11... | collective-permute-start | bytes 5505032 | tf_op jit(solution)/shard_map/ppermute | solution.py:364
  1.2 10.4 %collective-permute-start.2 = (bf16[256,3584]{1,0:T(8,128)(2,1)}, bf16[256,3584]{1,0:T(8,128)(2,1)}, u32[]{:S(2)}, u32[]{:S(2)}) collective-permute-start(bf16[256,3584]{1,0:T(8,128)(2,1)} %bitcast.16), channel_id=1, source_target_pairs={{0,1},{1,0},{2,3},{3,2},{4,5},{5,4},{6,7},{7,6},{8,9},{9,8},{10,11... | collective-permute-start | bytes 5505032 | tf_op jit(solution)/shard_map/ppermute | solution.py:364
  6.9 12.5 %collective-permute-start.6 = (bf16[40,3584]{1,0:T(8,128)(2,1)S(1)}, bf16[40,3584]{1,0:T(8,128)(2,1)S(1)}, u32[]{:S(2)}, u32[]{:S(2)}) collective-permute-start(bf16[40,3584]{1,0:T(8,128)(2,1)S(1)} %get-tuple-element.108), channel_id=1, source_target_pairs={{0,24},{1,25},{2,26},{3,27},{4,28},{5,29},{6,30},{7,31},{8,16},{9,... | collective-permute-start | bytes 860168 | tf_op jit(solution)/shard_map/ppermute | solution.py:364
  13.2 18.1 %collective-permute-start.4 = (bf16[40,3584]{1,0:T(8,128)(2,1)S(1)}, bf16[40,3584]{1,0:T(8,128)(2,1)S(1)}, u32[]{:S(2)}, u32[]{:S(2)}) collective-permute-start(bf16[40,3584]{1,0:T(8,128)(2,1)S(1)} %get-tuple-element.106), channel_id=1, source_target_pairs={{0,8},{1,9},{2,10},{3,11},{4,12},{5,13},{6,14},{7,15},{8,0},{9,1},... | collective-permute-start | bytes 860168 | tf_op jit(solution)/shard_map/ppermute | solution.py:364
  14.6 18.2 %collective-permute-start.7 = (bf16[40,3584]{1,0:T(8,128)(2,1)S(1)}, bf16[40,3584]{1,0:T(8,128)(2,1)S(1)}, u32[]{:S(2)}, u32[]{:S(2)}) collective-permute-start(bf16[40,3584]{1,0:T(8,128)(2,1)S(1)} %get-tuple-element.109), channel_id=1, source_target_pairs={{0,28},{1,29},{2,30},{3,31},{4,24},{5,25},{6,26},{7,27},{8,20},{9,... | collective-permute-start | bytes 860168 | tf_op jit(solution)/shard_map/ppermute | solution.py:364
  17.0 23.8 %collective-permute-start.5 = (bf16[40,3584]{1,0:T(8,128)(2,1)S(1)}, bf16[40,3584]{1,0:T(8,128)(2,1)S(1)}, u32[]{:S(2)}, u32[]{:S(2)}) collective-permute-start(bf16[40,3584]{1,0:T(8,128)(2,1)S(1)} %get-tuple-element.107), channel_id=1, source_target_pairs={{0,12},{1,13},{2,14},{3,15},{4,8},{5,9},{6,10},{7,11},{8,4},{9,5},... | collective-permute-start | bytes 860168 | tf_op jit(solution)/shard_map/ppermute | solution.py:364
  19.4 21.4 %collective-permute-start.8 = (bf16[40,3584]{1,0:T(8,128)(2,1)S(1)}, bf16[40,3584]{1,0:T(8,128)(2,1)S(1)}, u32[]{:S(2)}, u32[]{:S(2)}) collective-permute-start(bf16[40,3584]{1,0:T(8,128)(2,1)S(1)} %get-tuple-element.130.refs_2_), channel_id=1, source_target_pairs={{0,2},{1,3},{2,0},{3,1},{4,6},{5,7},{6,4},{7,5},{8,10},{9,11},{10,... | collective-permute-start | bytes 860168 | tf_op jit(solution)/shard_map/ppermute | solution.py:364
  21.1 19.8 %collective-permute-start.9 = (bf16[40,3584]{1,0:T(8,128)(2,1)S(1)}, bf16[40,3584]{1,0:T(8,128)(2,1)S(1)}, u32[]{:S(2)}, u32[]{:S(2)}) collective-permute-start(bf16[40,3584]{1,0:T(8,128)(2,1)S(1)} %collective-permute-done.3.refs_3_), channel_id=1, source_target_pairs={{0,2},{1,3},{2,0},{3,1},{4,6},{5,7},{6,4},{7,5},{8,10},{9,11},{10,... | collective-permute-start | bytes 860168 | tf_op jit(solution)/shard_map/ppermute | solution.py:364
  31.4 15.4 %collective-permute-start.12 = (bf16[40,3584]{1,0:T(8,128)(2,1)S(1)}, bf16[40,3584]{1,0:T(8,128)(2,1)S(1)}, u32[]{:S(2)}, u32[]{:S(2)}) collective-permute-start(bf16[40,3584]{1,0:T(8,128)(2,1)S(1)} %collective-permute-done.4.refs_4_), channel_id=1, source_target_pairs={{0,2},{1,3},{2,0},{3,1},{4,6},{5,7},{6,4},{7,5},{8,10},{9,11},{10,... | collective-permute-start | bytes 860168 | tf_op jit(solution)/shard_map/ppermute | solution.py:364
  40.8 22.9 %collective-permute-start.10 = (bf16[40,3584]{1,0:T(8,128)(2,1)S(1)}, bf16[40,3584]{1,0:T(8,128)(2,1)S(1)}, u32[]{:S(2)}, u32[]{:S(2)}) collective-permute-start(bf16[40,3584]{1,0:T(8,128)(2,1)S(1)} %get-tuple-element.122), channel_id=1, source_target_pairs={{0,16},{1,17},{2,18},{3,19},{4,20},{5,21},{6,22},{7,23},{8,24},{9,... | collective-permute-start | bytes 860168 | tf_op jit(solution)/shard_map/ppermute | solution.py:364
  43.2 26.3 %collective-permute-start.11 = (bf16[40,3584]{1,0:T(8,128)(2,1)S(1)}, bf16[40,3584]{1,0:T(8,128)(2,1)S(1)}, u32[]{:S(2)}, u32[]{:S(2)}) collective-permute-start(bf16[40,3584]{1,0:T(8,128)(2,1)S(1)} %get-tuple-element.123), channel_id=1, source_target_pairs={{0,20},{1,21},{2,22},{3,23},{4,16},{5,17},{6,18},{7,19},{8,28},{9,... | collective-permute-start | bytes 860168 | tf_op jit(solution)/shard_map/ppermute | solution.py:364
  44.7 24.8 %collective-permute-start.13 = (bf16[40,3584]{1,0:T(8,128)(2,1)S(1)}, bf16[40,3584]{1,0:T(8,128)(2,1)S(1)}, u32[]{:S(2)}, u32[]{:S(2)}) collective-permute-start(bf16[40,3584]{1,0:T(8,128)(2,1)S(1)} %collective-permute-done.5.refs_5_), channel_id=1, source_target_pairs={{0,2},{1,3},{2,0},{3,1},{4,6},{5,7},{6,4},{7,5},{8,10},{9,11},{10,... | collective-permute-start | bytes 860168 | tf_op jit(solution)/shard_map/ppermute | solution.py:364
  46.2 23.3 %collective-permute-start.14 = (bf16[40,3584]{1,0:T(8,128)(2,1)S(1)}, bf16[40,3584]{1,0:T(8,128)(2,1)S(1)}, u32[]{:S(2)}, u32[]{:S(2)}) collective-permute-start(bf16[40,3584]{1,0:T(8,128)(2,1)S(1)} %collective-permute-done.6.refs_0_), channel_id=1, source_target_pairs={{0,2},{1,3},{2,0},{3,1},{4,6},{5,7},{6,4},{7,5},{8,10},{9,11},{10,... | collective-permute-start | bytes 860168 | tf_op jit(solution)/shard_map/ppermute | solution.py:364
  46.7 22.8 %collective-permute-start.15 = (bf16[40,3584]{1,0:T(8,128)(2,1)S(1)}, bf16[40,3584]{1,0:T(8,128)(2,1)S(1)}, u32[]{:S(2)}, u32[]{:S(2)}) collective-permute-start(bf16[40,3584]{1,0:T(8,128)(2,1)S(1)} %collective-permute-done.7.refs_1_), channel_id=1, source_target_pairs={{0,2},{1,3},{2,0},{3,1},{4,6},{5,7},{6,4},{7,5},{8,10},{9,11},{10,... | collective-permute-start | bytes 860168 | tf_op jit(solution)/shard_map/ppermute | solution.py:364
  69.5 13.9 %collective-permute-start.16 = (bf16[40,3584]{1,0:T(8,128)(2,1)S(1)}, bf16[40,3584]{1,0:T(8,128)(2,1)S(1)}, u32[]{:S(2)}, u32[]{:S(2)}) collective-permute-start(bf16[40,3584]{1,0:T(8,128)(2,1)S(1)} %collective-permute-done.10.refs_0_), channel_id=1, source_target_pairs={{0,2},{1,3},{2,0},{3,1},{4,6},{5,7},{6,4},{7,5},{8,10},{9,11},{10,... | collective-permute-start | bytes 860168 | tf_op jit(solution)/shard_map/ppermute | solution.py:364
  71.1 13.1 %collective-permute-start.17 = (bf16[40,3584]{1,0:T(8,128)(2,1)S(1)}, bf16[40,3584]{1,0:T(8,128)(2,1)S(1)}, u32[]{:S(2)}, u32[]{:S(2)}) collective-permute-start(bf16[40,3584]{1,0:T(8,128)(2,1)S(1)} %collective-permute-done.11.refs_1_), channel_id=1, source_target_pairs={{0,2},{1,3},{2,0},{3,1},{4,6},{5,7},{6,4},{7,5},{8,10},{9,11},{10,... | collective-permute-start | bytes 860168 | tf_op jit(solution)/shard_map/ppermute | solution.py:364
  82.9 14.8 %collective-permute-start.21 = (bf16[40,3712]{1,0:T(8,128)(2,1)S(1)}, bf16[40,3712]{1,0:T(8,128)(2,1)S(1)}, u32[]{:S(2)}, u32[]{:S(2)}) collective-permute-start(bf16[40,3712]{1,0:T(8,128)(2,1)S(1)} %get-tuple-element.161), channel_id=1, source_target_pairs={{0,2},{1,3},{2,0},{3,1},{4,6},{5,7},{6,4},{7,5},{8,10},{9,11},{10,... | collective-permute-start | bytes 890888 | tf_op jit(solution)/shard_map/ppermute | solution.py:364
  91.5 10.8 %collective-permute-start.22 = (bf16[40,3712]{1,0:T(8,128)(2,1)S(1)}, bf16[40,3712]{1,0:T(8,128)(2,1)S(1)}, u32[]{:S(2)}, u32[]{:S(2)}) collective-permute-start(bf16[40,3712]{1,0:T(8,128)(2,1)S(1)} %get-tuple-element.165), channel_id=1, source_target_pairs={{0,2},{1,3},{2,0},{3,1},{4,6},{5,7},{6,4},{7,5},{8,10},{9,11},{10,... | collective-permute-start | bytes 890888 | tf_op jit(solution)/shard_map/ppermute | solution.py:364
  103.2 13.2 %collective-permute-start.24 = (bf16[240,7936]{1,0:T(8,128)(2,1)S(1)}, bf16[240,7936]{1,0:T(8,128)(2,1)S(1)}, u32[]{:S(2)}, u32[]{:S(2)}) collective-permute-start(bf16[240,7936]{1,0:T(8,128)(2,1)S(1)} %get-tuple-element.172.refs_0_), channel_id=1, source_target_pairs={{0,1},{1,0},{2,3},{3,2},{4,5},{5,4},{6,7},{7,6},{8,9},{9,8},{10,11... | collective-permute-start | bytes 11427848 | tf_op jit(solution)/shard_map/ppermute | solution.py:364
  103.2 13.2 %collective-permute-start.25 = (bf16[80,7936]{1,0:T(8,128)(2,1)S(1)}, bf16[80,7936]{1,0:T(8,128)(2,1)S(1)}, u32[]{:S(2)}, u32[]{:S(2)}) collective-permute-start(bf16[80,7936]{1,0:T(8,128)(2,1)S(1)} %get-tuple-element.173.refs_1_), channel_id=1, source_target_pairs={{0,1},{1,0},{2,3},{3,2},{4,5},{5,4},{6,7},{7,6},{8,9},{9,8},{10,11... | collective-permute-start | bytes 3809288 | tf_op jit(solution)/shard_map/ppermute | solution.py:364
  104.5 11.8 %collective-permute-start.26 = (bf16[40,1920]{1,0:T(8,128)(2,1)S(1)}, bf16[40,1920]{1,0:T(8,128)(2,1)S(1)}, u32[]{:S(2)}, u32[]{:S(2)}) collective-permute-start(bf16[40,1920]{1,0:T(8,128)(2,1)S(1)} %get-tuple-element.175), channel_id=1, source_target_pairs={{0,16},{1,17},{2,18},{3,19},{4,20},{5,21},{6,22},{7,23},{8,24},{9,... | collective-permute-start | bytes 460808 | tf_op jit(solution)/shard_map/ppermute | solution.py:364
  107.7 17.7 %collective-permute-start.23 = (bf16[40,1920]{1,0:T(8,128)(2,1)S(1)}, bf16[40,1920]{1,0:T(8,128)(2,1)S(1)}, u32[]{:S(2)}, u32[]{:S(2)}) collective-permute-start(bf16[40,1920]{1,0:T(8,128)(2,1)S(1)} %get-tuple-element.171), channel_id=1, source_target_pairs={{0,4},{1,5},{2,6},{3,7},{4,0},{5,1},{6,2},{7,3},{8,12},{9,13},{10,... | collective-permute-start | bytes 460808 | tf_op jit(solution)/shard_map/ppermute | solution.py:364
  112.7 12.7 %collective-permute-start.30 = (bf16[40,1920]{1,0:T(8,128)(2,1)S(1)}, bf16[40,1920]{1,0:T(8,128)(2,1)S(1)}, u32[]{:S(2)}, u32[]{:S(2)}) collective-permute-start(bf16[40,1920]{1,0:T(8,128)(2,1)S(1)} %get-tuple-element.183), channel_id=1, source_target_pairs={{0,20},{1,21},{2,22},{3,23},{4,16},{5,17},{6,18},{7,19},{8,28},{9,... | collective-permute-start | bytes 460808 | tf_op jit(solution)/shard_map/ppermute | solution.py:364
  (17 other events, 227.3 us)

commit v6 on v5

--- a/solution.py
+++ b/solution.py
@@ -386,14 +386,19 @@
         weights += [own, swap(own, 1)]
     blocks = list(pick_rows(me, ids_t, weights_t, tokens, out_grad, expert_count, capacity))
     fetch(first, blocks)
-    weights, close = after(weights, {s: blocks[s] for s in near})
-    fetch(near, close)
+    fetch(near[:2], blocks)
+    weights, close = after(weights, {s: blocks[s] for s in near[2:-1]})
+    fetch(near[2:-1], close)
     cross(near[:-1])
-    early, waiting = {s: crossed[s] for s in near[:-2]}, {s: blocks[s] for s in second}
+    early, waiting = {s: crossed[s] for s in near[:-2]}, {s: blocks[s] for s in second + near[-1:]}
     got, early, weights, waiting = after(got, early, weights, waiting)
     crossed.update(early)
-    fetch(second, waiting)
-    cross(near[-1:] + first)
+    fetch(second + near[-1:], waiting)
+    cross(first[:1])
+    queue = first[1:] + near[-1:]
+    for before, s in zip([first[0], near[-2]] + queue, queue):
+        crossed[before], got[s] = after(crossed[before], got[s])
+        cross([s])
     got, crossed = after(got, crossed)
     cross(second)
 
@@ -406,7 +411,7 @@
             [len(group) for group in groups],
         )
 
-    left, right = near[: len(near) // 2], near[len(near) // 2 :]
+    right, left = near[: len(near) // 2], near[len(near) // 2 :]
     parcel, units, keeps, sends = work(first, left, right)
     ahead = {s: crossed[s] for s in second}
     keeps, ahead = after(keeps, ahead)

time: 128 us -> 126 us (0.984)
  starting transfers between devices: 45.5 us -> 42.7 us
    ppermute x31, starting transfers between devices: 45.5 us -> 42.7 us  [swap(): lax.ppermute(value, AXES, [(i, i ^ distance) for i in range(device_count)])]
where the time goes in v6:
time: 126 us
  waiting for transfers between devices  52.7 us (42%)
  starting transfers between devices  42.7 us (34%)
  Pallas kernels  24.7 us (20%)
  local copies, waits for them, and re-layouts  5.24 us (4%)
    ppermute x31, waiting for transfers between devices, swap(): lax.ppermute(value, AXES, [(i, i ^ distance) for i in range(device_count)])  52.7 us
    ppermute x31, starting transfers between devices, swap(): lax.ppermute(value, AXES, [(i, i ^ distance) for i in range(device_count)])  42.7 us
    pallas_call x2, Pallas kernels, run_expert(): pl.pallas_call(functools.partial(expert_kernel, capacity, count, groups),...  14.7 us
    pallas_call x1, Pallas kernels, weight_grads(): pl.pallas_call(kernel, grid=(width // tile,), out_shape=[jax.ShapeDtypeSt...  6.19 us
    unnamed x20, local copies, waits for them, and re-layouts  5.24 us
  transfers between devices with their start and end apart: 31, of which 13 were waited for; matrix products, arithmetic and copies ran while one was open for 0% of the time, Pallas kernels for 18%

profile of v6, /device:TPU:0, one launch (start us, length us, event | category | flops | bytes accessed | tf_op | source)
XLA Modules:
  0.0 126.0 jit_solution(16816055068744782028)
XLA Ops:
  6.9 2.7 %collective-permute-start = (bf16[40,3584]{1,0:T(8,128)(2,1)S(1)}, bf16[40,3584]{1,0:T(8,128)(2,1)S(1)}, u32[]{:S(2)}, u32[]{:S(2)}) collective-permute-start(bf16[40,3584]{1,0:T(8,128)(2,1)S(1)} %get-tuple-element.102), channel_id=1, source_target_pairs={{0,4},{1,5},{2,6},{3,7},{4,0},{5,1},{6,2},{7,3},{8,12},{9,13},{10,... | collective-permute-start | bytes 860168 | tf_op jit(solution)/shard_map/ppermute | solution.py:364
  9.6 3.6 %collective-permute-start.5 = (bf16[40,3584]{1,0:T(8,128)(2,1)S(1)}, bf16[40,3584]{1,0:T(8,128)(2,1)S(1)}, u32[]{:S(2)}, u32[]{:S(2)}) collective-permute-start(bf16[40,3584]{1,0:T(8,128)(2,1)S(1)} %get-tuple-element.105), channel_id=1, source_target_pairs={{0,24},{1,25},{2,26},{3,27},{4,28},{5,29},{6,30},{7,31},{8,16},{9,... | collective-permute-start | bytes 860168 | tf_op jit(solution)/shard_map/ppermute | solution.py:364
  13.2 3.8 %collective-permute-done.refs_5_ = bf16[40,3584]{1,0:T(8,128)(2,1)S(1)} collective-permute-done((bf16[40,3584]{1,0:T(8,128)(2,1)S(1)}, bf16[40,3584]{1,0:T(8,128)(2,1)S(1)}, u32[]{:S(2)}, u32[]{:S(2)}) %collective-permute-start) | collective-permute-done | bytes 286752 | tf_op jit(solution)/shard_map/ppermute | solution.py:364
  17.0 4.8 %collective-permute-start.6 = (bf16[40,3584]{1,0:T(8,128)(2,1)S(1)}, bf16[40,3584]{1,0:T(8,128)(2,1)S(1)}, u32[]{:S(2)}, u32[]{:S(2)}) collective-permute-start(bf16[40,3584]{1,0:T(8,128)(2,1)S(1)} %get-tuple-element.106), channel_id=1, source_target_pairs={{0,28},{1,29},{2,30},{3,31},{4,24},{5,25},{6,26},{7,27},{8,20},{9,... | collective-permute-start | bytes 860168 | tf_op jit(solution)/shard_map/ppermute | solution.py:364
  23.8 5.6 %collective-permute-done.6.refs_1_ = bf16[40,3584]{1,0:T(8,128)(2,1)S(1)} collective-permute-done((bf16[40,3584]{1,0:T(8,128)(2,1)S(1)}, bf16[40,3584]{1,0:T(8,128)(2,1)S(1)}, u32[]{:S(2)}, u32[]{:S(2)}) %collective-permute-start.6) | collective-permute-done | bytes 286752 | tf_op jit(solution)/shard_map/ppermute | solution.py:364
  29.5 2.1 %collective-permute-done.7.refs_10_ = bf16[40,3584]{1,0:T(8,128)(2,1)S(1)} collective-permute-done((bf16[40,3584]{1,0:T(8,128)(2,1)S(1)}, bf16[40,3584]{1,0:T(8,128)(2,1)S(1)}, u32[]{:S(2)}, u32[]{:S(2)}) %collective-permute-start.7) | collective-permute-done | bytes 286752 | tf_op jit(solution)/shard_map/ppermute | solution.py:364
  31.5 4.5 %collective-permute-done.8.refs_11_ = bf16[40,3584]{1,0:T(8,128)(2,1)S(1)} collective-permute-done((bf16[40,3584]{1,0:T(8,128)(2,1)S(1)}, bf16[40,3584]{1,0:T(8,128)(2,1)S(1)}, u32[]{:S(2)}, u32[]{:S(2)}) %collective-permute-start.8) | collective-permute-done | bytes 286752 | tf_op jit(solution)/shard_map/ppermute | solution.py:364
  37.5 3.4 %collective-permute-start.10 = (bf16[40,3584]{1,0:T(8,128)(2,1)S(1)}, bf16[40,3584]{1,0:T(8,128)(2,1)S(1)}, u32[]{:S(2)}, u32[]{:S(2)}) collective-permute-start(bf16[40,3584]{1,0:T(8,128)(2,1)S(1)} %get-tuple-element.119), channel_id=1, source_target_pairs={{0,12},{1,13},{2,14},{3,15},{4,8},{5,9},{6,10},{7,11},{8,4},{9,5},... | collective-permute-start | bytes 860168 | tf_op jit(solution)/shard_map/ppermute | solution.py:364
  41.5 2.8 %collective-permute-start.12 = (bf16[40,3584]{1,0:T(8,128)(2,1)S(1)}, bf16[40,3584]{1,0:T(8,128)(2,1)S(1)}, u32[]{:S(2)}, u32[]{:S(2)}) collective-permute-start(bf16[40,3584]{1,0:T(8,128)(2,1)S(1)} %get-tuple-element.122), channel_id=1, source_target_pairs={{0,20},{1,21},{2,22},{3,23},{4,16},{5,17},{6,18},{7,19},{8,28},{9,... | collective-permute-start | bytes 860168 | tf_op jit(solution)/shard_map/ppermute | solution.py:364
  44.4 8.4 %collective-permute-done.10.refs_3_ = bf16[40,3584]{1,0:T(8,128)(2,1)S(1)} collective-permute-done((bf16[40,3584]{1,0:T(8,128)(2,1)S(1)}, bf16[40,3584]{1,0:T(8,128)(2,1)S(1)}, u32[]{:S(2)}, u32[]{:S(2)}) %collective-permute-start.10) | collective-permute-done | bytes 286752 | tf_op jit(solution)/shard_map/ppermute | solution.py:364
  52.7 2.0 %collective-permute-start.15 = (bf16[40,3584]{1,0:T(8,128)(2,1)S(1)}, bf16[40,3584]{1,0:T(8,128)(2,1)S(1)}, u32[]{:S(2)}, u32[]{:S(2)}) collective-permute-start(bf16[40,3584]{1,0:T(8,128)(2,1)S(1)} %collective-permute-done.6.refs_1_), channel_id=1, source_target_pairs={{0,2},{1,3},{2,0},{3,1},{4,6},{5,7},{6,4},{7,5},{8,10},{9,11},{10,... | collective-permute-start | bytes 860168 | tf_op jit(solution)/shard_map/ppermute | solution.py:364
  54.8 9.7 %collective-permute-done.11.refs_0_ = bf16[40,3584]{1,0:T(8,128)(2,1)S(1)} collective-permute-done((bf16[40,3584]{1,0:T(8,128)(2,1)S(1)}, bf16[40,3584]{1,0:T(8,128)(2,1)S(1)}, u32[]{:S(2)}, u32[]{:S(2)}) %collective-permute-start.11) | collective-permute-done | bytes 286752 | tf_op jit(solution)/shard_map/ppermute | solution.py:364
  64.4 3.6 %collective-permute-done.12.refs_1_ = bf16[40,3584]{1,0:T(8,128)(2,1)S(1)} collective-permute-done((bf16[40,3584]{1,0:T(8,128)(2,1)S(1)}, bf16[40,3584]{1,0:T(8,128)(2,1)S(1)}, u32[]{:S(2)}, u32[]{:S(2)}) %collective-permute-start.12) | collective-permute-done | bytes 286752 | tf_op jit(solution)/shard_map/ppermute | solution.py:364
  71.6 8.2 %run_expert.2 = (bf16[240,7936]{1,0:T(8,128)(2,1)S(1)}, bf16[240,768]{1,0:T(8,128)(2,1)S(1)}, bf16[40,3712]{1,0:T(8,128)(2,1)S(1)}, bf16[40,3712]{1,0:T(8,128)(2...) custom-call(bf16[40,3584]{1,0:T(8,128)(2,1)S(1)} %collective-permute, ...), custom_call_target="tpu_custom_call" | custom-call | flops 4404019200 | bytes 19611648 | tf_op jit(solution)/shard_map/run_expert/pallas_call | solution.py:167
  79.8 1.6 %collective-permute-start.18 = (bf16[40,3712]{1,0:T(8,128)(2,1)S(1)}, bf16[40,3712]{1,0:T(8,128)(2,1)S(1)}, u32[]{:S(2)}, u32[]{:S(2)}) collective-permute-start(bf16[40,3712]{1,0:T(8,128)(2,1)S(1)} %get-tuple-element.154), channel_id=1, source_target_pairs={{0,2},{1,3},{2,0},{3,1},{4,6},{5,7},{6,4},{7,5},{8,10},{9,11},{10,... | collective-permute-start | bytes 890888 | tf_op jit(solution)/shard_map/ppermute | solution.py:364
  81.9 6.5 %run_expert.3 = (bf16[80,7936]{1,0:T(8,128)(2,1)S(1)}, bf16[80,768]{1,0:T(8,128)(2,1)S(1)}, bf16[40,3712]{1,0:T(8,128)(2,1)S(1)}, bf16[40,3712]{1,0:T(8,128)(2,1)S(1)}) custom-call(bf16[40,3584]{1,0:T(8,128)(2,1)S(1)} %collective-permute-done.11.refs_0_, bf16[40,3584]{1,0:T(8,128)(2,1)S(1)} %collective-permute-done.12.refs_1_, ...), custom_call_target="tpu_custom_call" | custom-call | flops 1468006400 | bytes 13877248 | tf_op jit(solution)/shard_map/run_expert/pallas_call | solution.py:167
  91.5 2.5 %collective-permute-start.19 = (bf16[40,1920]{1,0:T(8,128)(2,1)S(1)}, bf16[40,1920]{1,0:T(8,128)(2,1)S(1)}, u32[]{:S(2)}, u32[]{:S(2)}) collective-permute-start(bf16[40,1920]{1,0:T(8,128)(2,1)S(1)} %get-tuple-element.160), channel_id=1, source_target_pairs={{0,24},{1,25},{2,26},{3,27},{4,28},{5,29},{6,30},{7,31},{8,16},{9,... | collective-permute-start | bytes 460808 | tf_op jit(solution)/shard_map/ppermute | solution.py:364
  93.9 2.3 %collective-permute-start.20 = (bf16[40,1920]{1,0:T(8,128)(2,1)S(1)}, bf16[40,1920]{1,0:T(8,128)(2,1)S(1)}, u32[]{:S(2)}, u32[]{:S(2)}) collective-permute-start(bf16[40,1920]{1,0:T(8,128)(2,1)S(1)} %get-tuple-element.161), channel_id=1, source_target_pairs={{0,28},{1,29},{2,30},{3,31},{4,24},{5,25},{6,26},{7,27},{8,20},{9,... | collective-permute-start | bytes 460808 | tf_op jit(solution)/shard_map/ppermute | solution.py:364
  96.4 3.3 %collective-permute-done.22.far_ref = bf16[40,3712]{1,0:T(8,128)(2,1)S(1)} collective-permute-done((bf16[40,3712]{1,0:T(8,128)(2,1)S(1)}, bf16[40,3712]{1,0:T(8,128)(2,1)S(1)}, u32[]{:S(2)}, u32[]{:S(2)}) %collective-permute-start.22) | collective-permute-done | bytes 296992 | tf_op jit(solution)/shard_map/ppermute | solution.py:364
  99.8 2.2 %collective-permute-done.20.refs_7_ = bf16[40,1920]{1,0:T(8,128)(2,1)S(1)} collective-permute-done((bf16[40,1920]{1,0:T(8,128)(2,1)S(1)}, bf16[40,1920]{1,0:T(8,128)(2,1)S(1)}, u32[]{:S(2)}, u32[]{:S(2)}) %collective-permute-start.20) | collective-permute-done | bytes 153632 | tf_op jit(solution)/shard_map/ppermute | solution.py:364
  105.3 6.1 %collective-permute-done.26.far_ref = bf16[40,3712]{1,0:T(8,128)(2,1)S(1)} collective-permute-done((bf16[40,3712]{1,0:T(8,128)(2,1)S(1)}, bf16[40,3712]{1,0:T(8,128)(2,1)S(1)}, u32[]{:S(2)}, u32[]{:S(2)}) %collective-permute-start.26) | collective-permute-done | bytes 296992 | tf_op jit(solution)/shard_map/ppermute | solution.py:364
  111.4 1.9 %collective-permute-start.29 = (bf16[40,1920]{1,0:T(8,128)(2,1)S(1)}, bf16[40,1920]{1,0:T(8,128)(2,1)S(1)}, u32[]{:S(2)}, u32[]{:S(2)}) collective-permute-start(bf16[40,1920]{1,0:T(8,128)(2,1)S(1)} %get-tuple-element.183), channel_id=1, source_target_pairs={{0,12},{1,13},{2,14},{3,15},{4,8},{5,9},{6,10},{7,11},{8,4},{9,5},... | collective-permute-start | bytes 460808 | tf_op jit(solution)/shard_map/ppermute | solution.py:364
  116.0 6.2 %weight_grads.1 = (bf16[3584,256]{1,0:T(8,128)(2,1)}, bf16[3584,256]{1,0:T(8,128)(2,1)}, bf16[256,3584]{1,0:T(8,128)(2,1)}) custom-call(bf16[240,7936]{1,0:T(8,128)(2,1)S(1)} %get-tuple-element.172.refs_0_, bf16[80,7936]{1,0:T(8,128)(2,1)S(1)} %get-tuple-element.173.refs_1_, bf16[240,7936]{1,0:T(8,128)(2,1)S(1)} %collective-permute-done.23.refs_2_, ...), custom_call_target="tpu_custom_call" | custom-call | flops 3523215360 | bytes 14680064 | tf_op jit(solution)/shard_map/weight_grads/pallas_call | solution.py:258
  124.1 1.9 %combine.1 = (bf16[128,3584]{1,0:T(8,128)(2,1)}, bf16[8,128]{1,0:T(8,128)(2,1)}) custom-call(s32[1]{0:T(128)} %bitcast.me_ref, s32[8,128]{1,0:T(8,128)S(1)} %bitcast.20, bf16[8,128]{1,0:T(8,128)(2,1)S(1)} %bitcast.22, bf16[40,1920]{1,0:T(8,128)(2,1)S(1)} %get-tuple-element.180.refs_0_, bf16[40,1920]{1,0:T(8,128)(2,1)S(1)} %collective-permute-done.27.refs_1_, ...), custom_call_target="tpu_custom_call" | custom-call | flops 1000000000 | bytes 3000000 | tf_op jit(solution)/shard_map/combine/pallas_call | solution.py:325
  (67 shorter events, 25.7 us)
Async XLA Ops:
  0.6 21.1 %collective-permute-start.1 = (bf16[3584,256]{1,0:T(8,128)(2,1)}, bf16[3584,256]{1,0:T(8,128)(2,1)S(1)}, u32[]{:S(2)}, u32[]{:S(2)}) collective-permute-start(bf16[3584,256]{1,0:T(8,128)(2,1)} %bitcast.10), channel_id=1, source_target_pairs={{0,1},{1,0},{2,3},{3,2},{4,5},{5,4},{6,7},{7,6},{8,9},{9,8},{10,11... | collective-permute-start | bytes 5505032 | tf_op jit(solution)/shard_map/ppermute | solution.py:364
  1.1 22.1 %collective-permute-start.2 = (bf16[3584,256]{1,0:T(8,128)(2,1)}, bf16[3584,256]{1,0:T(8,128)(2,1)}, u32[]{:S(2)}, u32[]{:S(2)}) collective-permute-start(bf16[3584,256]{1,0:T(8,128)(2,1)} %bitcast.13), channel_id=1, source_target_pairs={{0,1},{1,0},{2,3},{3,2},{4,5},{5,4},{6,7},{7,6},{8,9},{9,8},{10,11... | collective-permute-start | bytes 5505032 | tf_op jit(solution)/shard_map/ppermute | solution.py:364
  1.2 22.6 %collective-permute-start.3 = (bf16[256,3584]{1,0:T(8,128)(2,1)}, bf16[256,3584]{1,0:T(8,128)(2,1)}, u32[]{:S(2)}, u32[]{:S(2)}) collective-permute-start(bf16[256,3584]{1,0:T(8,128)(2,1)} %bitcast.16), channel_id=1, source_target_pairs={{0,1},{1,0},{2,3},{3,2},{4,5},{5,4},{6,7},{7,6},{8,9},{9,8},{10,11... | collective-permute-start | bytes 5505032 | tf_op jit(solution)/shard_map/ppermute | solution.py:364
  6.9 10.1 %collective-permute-start = (bf16[40,3584]{1,0:T(8,128)(2,1)S(1)}, bf16[40,3584]{1,0:T(8,128)(2,1)S(1)}, u32[]{:S(2)}, u32[]{:S(2)}) collective-permute-start(bf16[40,3584]{1,0:T(8,128)(2,1)S(1)} %get-tuple-element.102), channel_id=1, source_target_pairs={{0,4},{1,5},{2,6},{3,7},{4,0},{5,1},{6,2},{7,3},{8,12},{9,13},{10,... | collective-permute-start | bytes 860168 | tf_op jit(solution)/shard_map/ppermute | solution.py:364
  9.6 14.3 %collective-permute-start.5 = (bf16[40,3584]{1,0:T(8,128)(2,1)S(1)}, bf16[40,3584]{1,0:T(8,128)(2,1)S(1)}, u32[]{:S(2)}, u32[]{:S(2)}) collective-permute-start(bf16[40,3584]{1,0:T(8,128)(2,1)S(1)} %get-tuple-element.105), channel_id=1, source_target_pairs={{0,24},{1,25},{2,26},{3,27},{4,28},{5,29},{6,30},{7,31},{8,16},{9,... | collective-permute-start | bytes 860168 | tf_op jit(solution)/shard_map/ppermute | solution.py:364
  17.0 12.5 %collective-permute-start.6 = (bf16[40,3584]{1,0:T(8,128)(2,1)S(1)}, bf16[40,3584]{1,0:T(8,128)(2,1)S(1)}, u32[]{:S(2)}, u32[]{:S(2)}) collective-permute-start(bf16[40,3584]{1,0:T(8,128)(2,1)S(1)} %get-tuple-element.106), channel_id=1, source_target_pairs={{0,28},{1,29},{2,30},{3,31},{4,24},{5,25},{6,26},{7,27},{8,20},{9,... | collective-permute-start | bytes 860168 | tf_op jit(solution)/shard_map/ppermute | solution.py:364
  23.3 12.8 %collective-permute-start.8 = (bf16[40,3584]{1,0:T(8,128)(2,1)S(1)}, bf16[40,3584]{1,0:T(8,128)(2,1)S(1)}, u32[]{:S(2)}, u32[]{:S(2)}) collective-permute-start(bf16[40,3584]{1,0:T(8,128)(2,1)S(1)} %collective-permute-done.refs_5_), channel_id=1, source_target_pairs={{0,2},{1,3},{2,0},{3,1},{4,6},{5,7},{6,4},{7,5},{8,10},{9,11},{10,... | collective-permute-start | bytes 860168 | tf_op jit(solution)/shard_map/ppermute | solution.py:364
  23.8 12.2 %collective-permute-start.4 = (bf16[40,3584]{1,0:T(8,128)(2,1)S(1)}, bf16[40,3584]{1,0:T(8,128)(2,1)S(1)}, u32[]{:S(2)}, u32[]{:S(2)}) collective-permute-start(bf16[40,3584]{1,0:T(8,128)(2,1)S(1)} %get-tuple-element.104), channel_id=1, source_target_pairs={{0,8},{1,9},{2,10},{3,11},{4,12},{5,13},{6,14},{7,15},{8,0},{9,1},... | collective-permute-start | bytes 860168 | tf_op jit(solution)/shard_map/ppermute | solution.py:364
  37.5 15.2 %collective-permute-start.10 = (bf16[40,3584]{1,0:T(8,128)(2,1)S(1)}, bf16[40,3584]{1,0:T(8,128)(2,1)S(1)}, u32[]{:S(2)}, u32[]{:S(2)}) collective-permute-start(bf16[40,3584]{1,0:T(8,128)(2,1)S(1)} %get-tuple-element.119), channel_id=1, source_target_pairs={{0,12},{1,13},{2,14},{3,15},{4,8},{5,9},{6,10},{7,11},{8,4},{9,5},... | collective-permute-start | bytes 860168 | tf_op jit(solution)/shard_map/ppermute | solution.py:364
  40.9 11.8 %collective-permute-start.13 = (bf16[40,3584]{1,0:T(8,128)(2,1)S(1)}, bf16[40,3584]{1,0:T(8,128)(2,1)S(1)}, u32[]{:S(2)}, u32[]{:S(2)}) collective-permute-start(bf16[40,3584]{1,0:T(8,128)(2,1)S(1)} %collective-permute-done.5.refs_0_), channel_id=1, source_target_pairs={{0,2},{1,3},{2,0},{3,1},{4,6},{5,7},{6,4},{7,5},{8,10},{9,11},{10,... | collective-permute-start | bytes 860168 | tf_op jit(solution)/shard_map/ppermute | solution.py:364
  41.5 23.0 %collective-permute-start.11 = (bf16[40,3584]{1,0:T(8,128)(2,1)S(1)}, bf16[40,3584]{1,0:T(8,128)(2,1)S(1)}, u32[]{:S(2)}, u32[]{:S(2)}) collective-permute-start(bf16[40,3584]{1,0:T(8,128)(2,1)S(1)} %get-tuple-element.121), channel_id=1, source_target_pairs={{0,16},{1,17},{2,18},{3,19},{4,20},{5,21},{6,22},{7,23},{8,24},{9,... | collective-permute-start | bytes 860168 | tf_op jit(solution)/shard_map/ppermute | solution.py:364
  41.5 26.5 %collective-permute-start.12 = (bf16[40,3584]{1,0:T(8,128)(2,1)S(1)}, bf16[40,3584]{1,0:T(8,128)(2,1)S(1)}, u32[]{:S(2)}, u32[]{:S(2)}) collective-permute-start(bf16[40,3584]{1,0:T(8,128)(2,1)S(1)} %get-tuple-element.122), channel_id=1, source_target_pairs={{0,20},{1,21},{2,22},{3,23},{4,16},{5,17},{6,18},{7,19},{8,28},{9,... | collective-permute-start | bytes 860168 | tf_op jit(solution)/shard_map/ppermute | solution.py:364
  52.7 15.3 %collective-permute-start.14 = (bf16[40,3584]{1,0:T(8,128)(2,1)S(1)}, bf16[40,3584]{1,0:T(8,128)(2,1)S(1)}, u32[]{:S(2)}, u32[]{:S(2)}) collective-permute-start(bf16[40,3584]{1,0:T(8,128)(2,1)S(1)} %collective-permute-done.10.refs_3_), channel_id=1, source_target_pairs={{0,2},{1,3},{2,0},{3,1},{4,6},{5,7},{6,4},{7,5},{8,10},{9,11},{10,... | collective-permute-start | bytes 860168 | tf_op jit(solution)/shard_map/ppermute | solution.py:364
  52.7 15.3 %collective-permute-start.15 = (bf16[40,3584]{1,0:T(8,128)(2,1)S(1)}, bf16[40,3584]{1,0:T(8,128)(2,1)S(1)}, u32[]{:S(2)}, u32[]{:S(2)}) collective-permute-start(bf16[40,3584]{1,0:T(8,128)(2,1)S(1)} %collective-permute-done.6.refs_1_), channel_id=1, source_target_pairs={{0,2},{1,3},{2,0},{3,1},{4,6},{5,7},{6,4},{7,5},{8,10},{9,11},{10,... | collective-permute-start | bytes 860168 | tf_op jit(solution)/shard_map/ppermute | solution.py:364
  68.0 13.8 %collective-permute-start.16 = (bf16[40,3584]{1,0:T(8,128)(2,1)S(1)}, bf16[40,3584]{1,0:T(8,128)(2,1)S(1)}, u32[]{:S(2)}, u32[]{:S(2)}) collective-permute-start(bf16[40,3584]{1,0:T(8,128)(2,1)S(1)} %collective-permute-done.11.refs_0_), channel_id=1, source_target_pairs={{0,2},{1,3},{2,0},{3,1},{4,6},{5,7},{6,4},{7,5},{8,10},{9,11},{10,... | collective-permute-start | bytes 860168 | tf_op jit(solution)/shard_map/ppermute | solution.py:364
  69.5 12.3 %collective-permute-start.17 = (bf16[40,3584]{1,0:T(8,128)(2,1)S(1)}, bf16[40,3584]{1,0:T(8,128)(2,1)S(1)}, u32[]{:S(2)}, u32[]{:S(2)}) collective-permute-start(bf16[40,3584]{1,0:T(8,128)(2,1)S(1)} %collective-permute-done.12.refs_1_), channel_id=1, source_target_pairs={{0,2},{1,3},{2,0},{3,1},{4,6},{5,7},{6,4},{7,5},{8,10},{9,11},{10,... | collective-permute-start | bytes 860168 | tf_op jit(solution)/shard_map/ppermute | solution.py:364
  79.8 10.1 %collective-permute-start.18 = (bf16[40,3712]{1,0:T(8,128)(2,1)S(1)}, bf16[40,3712]{1,0:T(8,128)(2,1)S(1)}, u32[]{:S(2)}, u32[]{:S(2)}) collective-permute-start(bf16[40,3712]{1,0:T(8,128)(2,1)S(1)} %get-tuple-element.154), channel_id=1, source_target_pairs={{0,2},{1,3},{2,0},{3,1},{4,6},{5,7},{6,4},{7,5},{8,10},{9,11},{10,... | collective-permute-start | bytes 890888 | tf_op jit(solution)/shard_map/ppermute | solution.py:364
  81.3 14.9 %collective-permute-start.21 = (bf16[40,3712]{1,0:T(8,128)(2,1)S(1)}, bf16[40,3712]{1,0:T(8,128)(2,1)S(1)}, u32[]{:S(2)}, u32[]{:S(2)}) collective-permute-start(bf16[40,3712]{1,0:T(8,128)(2,1)S(1)} %get-tuple-element.163), channel_id=1, source_target_pairs={{0,2},{1,3},{2,0},{3,1},{4,6},{5,7},{6,4},{7,5},{8,10},{9,11},{10,... | collective-permute-start | bytes 890888 | tf_op jit(solution)/shard_map/ppermute | solution.py:364
  101.9 12.8 %collective-permute-start.23 = (bf16[240,7936]{1,0:T(8,128)(2,1)S(1)}, bf16[240,7936]{1,0:T(8,128)(2,1)S(1)}, u32[]{:S(2)}, u32[]{:S(2)}) collective-permute-start(bf16[240,7936]{1,0:T(8,128)(2,1)S(1)} %get-tuple-element.172.refs_0_), channel_id=1, source_target_pairs={{0,1},{1,0},{2,3},{3,2},{4,5},{5,4},{6,7},{7,6},{8,9},{9,8},{10,11... | collective-permute-start | bytes 11427848 | tf_op jit(solution)/shard_map/ppermute | solution.py:364
  101.9 12.8 %collective-permute-start.24 = (bf16[80,7936]{1,0:T(8,128)(2,1)S(1)}, bf16[80,7936]{1,0:T(8,128)(2,1)S(1)}, u32[]{:S(2)}, u32[]{:S(2)}) collective-permute-start(bf16[80,7936]{1,0:T(8,128)(2,1)S(1)} %get-tuple-element.173.refs_1_), channel_id=1, source_target_pairs={{0,1},{1,0},{2,3},{3,2},{4,5},{5,4},{6,7},{7,6},{8,9},{9,8},{10,11... | collective-permute-start | bytes 3809288 | tf_op jit(solution)/shard_map/ppermute | solution.py:364
  103.0 10.4 %collective-permute-start.25 = (bf16[40,1920]{1,0:T(8,128)(2,1)S(1)}, bf16[40,1920]{1,0:T(8,128)(2,1)S(1)}, u32[]{:S(2)}, u32[]{:S(2)}) collective-permute-start(bf16[40,1920]{1,0:T(8,128)(2,1)S(1)} %get-tuple-element.175), channel_id=1, source_target_pairs={{0,16},{1,17},{2,18},{3,19},{4,20},{5,21},{6,22},{7,23},{8,24},{9,... | collective-permute-start | bytes 460808 | tf_op jit(solution)/shard_map/ppermute | solution.py:364
  104.4 17.8 %collective-permute-start.28 = (bf16[40,1920]{1,0:T(8,128)(2,1)S(1)}, bf16[40,1920]{1,0:T(8,128)(2,1)S(1)}, u32[]{:S(2)}, u32[]{:S(2)}) collective-permute-start(bf16[40,1920]{1,0:T(8,128)(2,1)S(1)} %get-tuple-element.182), channel_id=1, source_target_pairs={{0,8},{1,9},{2,10},{3,11},{4,12},{5,13},{6,14},{7,15},{8,0},{9,1},... | collective-permute-start | bytes 460808 | tf_op jit(solution)/shard_map/ppermute | solution.py:364
  111.4 10.8 %collective-permute-start.29 = (bf16[40,1920]{1,0:T(8,128)(2,1)S(1)}, bf16[40,1920]{1,0:T(8,128)(2,1)S(1)}, u32[]{:S(2)}, u32[]{:S(2)}) collective-permute-start(bf16[40,1920]{1,0:T(8,128)(2,1)S(1)} %get-tuple-element.183), channel_id=1, source_target_pairs={{0,12},{1,13},{2,14},{3,15},{4,8},{5,9},{6,10},{7,11},{8,4},{9,5},... | collective-permute-start | bytes 460808 | tf_op jit(solution)/shard_map/ppermute | solution.py:364
  113.4 10.3 %collective-permute-start.30 = (bf16[40,1920]{1,0:T(8,128)(2,1)S(1)}, bf16[40,1920]{1,0:T(8,128)(2,1)S(1)}, u32[]{:S(2)}, u32[]{:S(2)}) collective-permute-start(bf16[40,1920]{1,0:T(8,128)(2,1)S(1)} %get-tuple-element.185), channel_id=1, source_target_pairs={{0,20},{1,21},{2,22},{3,23},{4,16},{5,17},{6,18},{7,19},{8,28},{9,... | collective-permute-start | bytes 460808 | tf_op jit(solution)/shard_map/ppermute | solution.py:364
  (17 other events, 223.6 us)

commit v7 on v6

--- a/solution.py
+++ b/solution.py
@@ -245,7 +245,7 @@
     hidden_units = (parcels[0].shape[1] - 2 * width) // 3
     group_rows = [p.shape[0] for p in parcels]
     total = sum(group_rows)
-    tile = width // 4 if width % (128 * 4) == 0 else width
+    tile = width // 2 if width % (128 * 2) == 0 else width
     given = [own for own in units if own is not None]
 
     def kernel(*refs):

time: 126 us -> 126 us (level)
  no operation moved by 1% of the time
where the time goes in v7:
time: 126 us
  waiting for transfers between devices  52.9 us (42%)
  starting transfers between devices  42.6 us (34%)
  Pallas kernels  24.6 us (20%)
  local copies, waits for them, and re-layouts  5.24 us (4%)
    ppermute x31, waiting for transfers between devices, swap(): lax.ppermute(value, AXES, [(i, i ^ distance) for i in range(device_count)])  52.9 us
    ppermute x31, starting transfers between devices, swap(): lax.ppermute(value, AXES, [(i, i ^ distance) for i in range(device_count)])  42.6 us
    pallas_call x2, Pallas kernels, run_expert(): pl.pallas_call(functools.partial(expert_kernel, capacity, count, groups),...  14.7 us
    pallas_call x1, Pallas kernels, weight_grads(): pl.pallas_call(kernel, grid=(width // tile,), out_shape=[jax.ShapeDtypeSt...  6.13 us
    unnamed x20, local copies, waits for them, and re-layouts  5.24 us
  transfers between devices with their start and end apart: 31, of which 13 were waited for; matrix products, arithmetic and copies ran while one was open for 0% of the time, Pallas kernels for 18%

profile of v7, /device:TPU:0, one launch (start us, length us, event | category | flops | bytes accessed | tf_op | source)
XLA Modules:
  0.0 126.1 jit_solution(3798552671573190710)
XLA Ops:
  6.9 2.7 %collective-permute-start = (bf16[40,3584]{1,0:T(8,128)(2,1)S(1)}, bf16[40,3584]{1,0:T(8,128)(2,1)S(1)}, u32[]{:S(2)}, u32[]{:S(2)}) collective-permute-start(bf16[40,3584]{1,0:T(8,128)(2,1)S(1)} %get-tuple-element.102), channel_id=1, source_target_pairs={{0,4},{1,5},{2,6},{3,7},{4,0},{5,1},{6,2},{7,3},{8,12},{9,13},{10,... | collective-permute-start | bytes 860168 | tf_op jit(solution)/shard_map/ppermute | solution.py:364
  9.6 3.6 %collective-permute-start.5 = (bf16[40,3584]{1,0:T(8,128)(2,1)S(1)}, bf16[40,3584]{1,0:T(8,128)(2,1)S(1)}, u32[]{:S(2)}, u32[]{:S(2)}) collective-permute-start(bf16[40,3584]{1,0:T(8,128)(2,1)S(1)} %get-tuple-element.105), channel_id=1, source_target_pairs={{0,24},{1,25},{2,26},{3,27},{4,28},{5,29},{6,30},{7,31},{8,16},{9,... | collective-permute-start | bytes 860168 | tf_op jit(solution)/shard_map/ppermute | solution.py:364
  13.2 3.8 %collective-permute-done.refs_5_ = bf16[40,3584]{1,0:T(8,128)(2,1)S(1)} collective-permute-done((bf16[40,3584]{1,0:T(8,128)(2,1)S(1)}, bf16[40,3584]{1,0:T(8,128)(2,1)S(1)}, u32[]{:S(2)}, u32[]{:S(2)}) %collective-permute-start) | collective-permute-done | bytes 286752 | tf_op jit(solution)/shard_map/ppermute | solution.py:364
  17.0 4.8 %collective-permute-start.6 = (bf16[40,3584]{1,0:T(8,128)(2,1)S(1)}, bf16[40,3584]{1,0:T(8,128)(2,1)S(1)}, u32[]{:S(2)}, u32[]{:S(2)}) collective-permute-start(bf16[40,3584]{1,0:T(8,128)(2,1)S(1)} %get-tuple-element.106), channel_id=1, source_target_pairs={{0,28},{1,29},{2,30},{3,31},{4,24},{5,25},{6,26},{7,27},{8,20},{9,... | collective-permute-start | bytes 860168 | tf_op jit(solution)/shard_map/ppermute | solution.py:364
  23.8 5.6 %collective-permute-done.6.refs_1_ = bf16[40,3584]{1,0:T(8,128)(2,1)S(1)} collective-permute-done((bf16[40,3584]{1,0:T(8,128)(2,1)S(1)}, bf16[40,3584]{1,0:T(8,128)(2,1)S(1)}, u32[]{:S(2)}, u32[]{:S(2)}) %collective-permute-start.6) | collective-permute-done | bytes 286752 | tf_op jit(solution)/shard_map/ppermute | solution.py:364
  29.5 2.1 %collective-permute-done.7.refs_10_ = bf16[40,3584]{1,0:T(8,128)(2,1)S(1)} collective-permute-done((bf16[40,3584]{1,0:T(8,128)(2,1)S(1)}, bf16[40,3584]{1,0:T(8,128)(2,1)S(1)}, u32[]{:S(2)}, u32[]{:S(2)}) %collective-permute-start.7) | collective-permute-done | bytes 286752 | tf_op jit(solution)/shard_map/ppermute | solution.py:364
  31.6 4.5 %collective-permute-done.8.refs_11_ = bf16[40,3584]{1,0:T(8,128)(2,1)S(1)} collective-permute-done((bf16[40,3584]{1,0:T(8,128)(2,1)S(1)}, bf16[40,3584]{1,0:T(8,128)(2,1)S(1)}, u32[]{:S(2)}, u32[]{:S(2)}) %collective-permute-start.8) | collective-permute-done | bytes 286752 | tf_op jit(solution)/shard_map/ppermute | solution.py:364
  37.5 3.4 %collective-permute-start.10 = (bf16[40,3584]{1,0:T(8,128)(2,1)S(1)}, bf16[40,3584]{1,0:T(8,128)(2,1)S(1)}, u32[]{:S(2)}, u32[]{:S(2)}) collective-permute-start(bf16[40,3584]{1,0:T(8,128)(2,1)S(1)} %get-tuple-element.119), channel_id=1, source_target_pairs={{0,12},{1,13},{2,14},{3,15},{4,8},{5,9},{6,10},{7,11},{8,4},{9,5},... | collective-permute-start | bytes 860168 | tf_op jit(solution)/shard_map/ppermute | solution.py:364
  41.5 2.8 %collective-permute-start.12 = (bf16[40,3584]{1,0:T(8,128)(2,1)S(1)}, bf16[40,3584]{1,0:T(8,128)(2,1)S(1)}, u32[]{:S(2)}, u32[]{:S(2)}) collective-permute-start(bf16[40,3584]{1,0:T(8,128)(2,1)S(1)} %get-tuple-element.122), channel_id=1, source_target_pairs={{0,20},{1,21},{2,22},{3,23},{4,16},{5,17},{6,18},{7,19},{8,28},{9,... | collective-permute-start | bytes 860168 | tf_op jit(solution)/shard_map/ppermute | solution.py:364
  44.3 8.4 %collective-permute-done.10.refs_3_ = bf16[40,3584]{1,0:T(8,128)(2,1)S(1)} collective-permute-done((bf16[40,3584]{1,0:T(8,128)(2,1)S(1)}, bf16[40,3584]{1,0:T(8,128)(2,1)S(1)}, u32[]{:S(2)}, u32[]{:S(2)}) %collective-permute-start.10) | collective-permute-done | bytes 286752 | tf_op jit(solution)/shard_map/ppermute | solution.py:364
  52.8 2.0 %collective-permute-start.15 = (bf16[40,3584]{1,0:T(8,128)(2,1)S(1)}, bf16[40,3584]{1,0:T(8,128)(2,1)S(1)}, u32[]{:S(2)}, u32[]{:S(2)}) collective-permute-start(bf16[40,3584]{1,0:T(8,128)(2,1)S(1)} %collective-permute-done.6.refs_1_), channel_id=1, source_target_pairs={{0,2},{1,3},{2,0},{3,1},{4,6},{5,7},{6,4},{7,5},{8,10},{9,11},{10,... | collective-permute-start | bytes 860168 | tf_op jit(solution)/shard_map/ppermute | solution.py:364
  54.8 9.6 %collective-permute-done.11.refs_0_ = bf16[40,3584]{1,0:T(8,128)(2,1)S(1)} collective-permute-done((bf16[40,3584]{1,0:T(8,128)(2,1)S(1)}, bf16[40,3584]{1,0:T(8,128)(2,1)S(1)}, u32[]{:S(2)}, u32[]{:S(2)}) %collective-permute-start.11) | collective-permute-done | bytes 286752 | tf_op jit(solution)/shard_map/ppermute | solution.py:364
  64.4 3.6 %collective-permute-done.12.refs_1_ = bf16[40,3584]{1,0:T(8,128)(2,1)S(1)} collective-permute-done((bf16[40,3584]{1,0:T(8,128)(2,1)S(1)}, bf16[40,3584]{1,0:T(8,128)(2,1)S(1)}, u32[]{:S(2)}, u32[]{:S(2)}) %collective-permute-start.12) | collective-permute-done | bytes 286752 | tf_op jit(solution)/shard_map/ppermute | solution.py:364
  71.6 8.2 %run_expert.2 = (bf16[240,7936]{1,0:T(8,128)(2,1)S(1)}, bf16[240,768]{1,0:T(8,128)(2,1)S(1)}, bf16[40,3712]{1,0:T(8,128)(2,1)S(1)}, bf16[40,3712]{1,0:T(8,128)(2...) custom-call(bf16[40,3584]{1,0:T(8,128)(2,1)S(1)} %collective-permute, ...), custom_call_target="tpu_custom_call" | custom-call | flops 4404019200 | bytes 19611648 | tf_op jit(solution)/shard_map/run_expert/pallas_call | solution.py:167
  81.9 6.5 %run_expert.3 = (bf16[80,7936]{1,0:T(8,128)(2,1)S(1)}, bf16[80,768]{1,0:T(8,128)(2,1)S(1)}, bf16[40,3712]{1,0:T(8,128)(2,1)S(1)}, bf16[40,3712]{1,0:T(8,128)(2,1)S(1)}) custom-call(bf16[40,3584]{1,0:T(8,128)(2,1)S(1)} %collective-permute-done.11.refs_0_, bf16[40,3584]{1,0:T(8,128)(2,1)S(1)} %collective-permute-done.12.refs_1_, ...), custom_call_target="tpu_custom_call" | custom-call | flops 1468006400 | bytes 13877248 | tf_op jit(solution)/shard_map/run_expert/pallas_call | solution.py:167
  91.5 2.5 %collective-permute-start.19 = (bf16[40,1920]{1,0:T(8,128)(2,1)S(1)}, bf16[40,1920]{1,0:T(8,128)(2,1)S(1)}, u32[]{:S(2)}, u32[]{:S(2)}) collective-permute-start(bf16[40,1920]{1,0:T(8,128)(2,1)S(1)} %get-tuple-element.160), channel_id=1, source_target_pairs={{0,24},{1,25},{2,26},{3,27},{4,28},{5,29},{6,30},{7,31},{8,16},{9,... | collective-permute-start | bytes 460808 | tf_op jit(solution)/shard_map/ppermute | solution.py:364
  94.0 2.3 %collective-permute-start.20 = (bf16[40,1920]{1,0:T(8,128)(2,1)S(1)}, bf16[40,1920]{1,0:T(8,128)(2,1)S(1)}, u32[]{:S(2)}, u32[]{:S(2)}) collective-permute-start(bf16[40,1920]{1,0:T(8,128)(2,1)S(1)} %get-tuple-element.161), channel_id=1, source_target_pairs={{0,28},{1,29},{2,30},{3,31},{4,24},{5,25},{6,26},{7,27},{8,20},{9,... | collective-permute-start | bytes 460808 | tf_op jit(solution)/shard_map/ppermute | solution.py:364
  96.4 3.3 %collective-permute-done.22.far_ref = bf16[40,3712]{1,0:T(8,128)(2,1)S(1)} collective-permute-done((bf16[40,3712]{1,0:T(8,128)(2,1)S(1)}, bf16[40,3712]{1,0:T(8,128)(2,1)S(1)}, u32[]{:S(2)}, u32[]{:S(2)}) %collective-permute-start.22) | collective-permute-done | bytes 296992 | tf_op jit(solution)/shard_map/ppermute | solution.py:364
  99.7 2.2 %collective-permute-done.20.refs_7_ = bf16[40,1920]{1,0:T(8,128)(2,1)S(1)} collective-permute-done((bf16[40,1920]{1,0:T(8,128)(2,1)S(1)}, bf16[40,1920]{1,0:T(8,128)(2,1)S(1)}, u32[]{:S(2)}, u32[]{:S(2)}) %collective-permute-start.20) | collective-permute-done | bytes 153632 | tf_op jit(solution)/shard_map/ppermute | solution.py:364
  105.3 6.2 %collective-permute-done.26.far_ref = bf16[40,3712]{1,0:T(8,128)(2,1)S(1)} collective-permute-done((bf16[40,3712]{1,0:T(8,128)(2,1)S(1)}, bf16[40,3712]{1,0:T(8,128)(2,1)S(1)}, u32[]{:S(2)}, u32[]{:S(2)}) %collective-permute-start.26) | collective-permute-done | bytes 296992 | tf_op jit(solution)/shard_map/ppermute | solution.py:364
  111.4 1.9 %collective-permute-start.29 = (bf16[40,1920]{1,0:T(8,128)(2,1)S(1)}, bf16[40,1920]{1,0:T(8,128)(2,1)S(1)}, u32[]{:S(2)}, u32[]{:S(2)}) collective-permute-start(bf16[40,1920]{1,0:T(8,128)(2,1)S(1)} %get-tuple-element.183), channel_id=1, source_target_pairs={{0,12},{1,13},{2,14},{3,15},{4,8},{5,9},{6,10},{7,11},{8,4},{9,5},... | collective-permute-start | bytes 460808 | tf_op jit(solution)/shard_map/ppermute | solution.py:364
  116.0 6.1 %weight_grads.1 = (bf16[3584,256]{1,0:T(8,128)(2,1)}, bf16[3584,256]{1,0:T(8,128)(2,1)}, bf16[256,3584]{1,0:T(8,128)(2,1)}) custom-call(bf16[240,7936]{1,0:T(8,128)(2,1)S(1)} %get-tuple-element.172.refs_0_, bf16[80,7936]{1,0:T(8,128)(2,1)S(1)} %get-tuple-element.173.refs_1_, bf16[240,7936]{1,0:T(8,128)(2,1)S(1)} %collective-permute-done.23.refs_2_, ...), custom_call_target="tpu_custom_call" | custom-call | flops 3523215360 | bytes 14680064 | tf_op jit(solution)/shard_map/weight_grads/pallas_call | solution.py:258
  122.1 1.6 %collective-permute-done.30.refs_5_ = bf16[40,1920]{1,0:T(8,128)(2,1)S(1)} collective-permute-done((bf16[40,1920]{1,0:T(8,128)(2,1)S(1)}, bf16[40,1920]{1,0:T(8,128)(2,1)S(1)}, u32[]{:S(2)}, u32[]{:S(2)}) %collective-permute-start.30) | collective-permute-done | bytes 153632 | tf_op jit(solution)/shard_map/ppermute | solution.py:364
  124.1 1.9 %combine.1 = (bf16[128,3584]{1,0:T(8,128)(2,1)}, bf16[8,128]{1,0:T(8,128)(2,1)}) custom-call(s32[1]{0:T(128)} %bitcast.me_ref, s32[8,128]{1,0:T(8,128)S(1)} %bitcast.20, bf16[8,128]{1,0:T(8,128)(2,1)S(1)} %bitcast.22, bf16[40,1920]{1,0:T(8,128)(2,1)S(1)} %get-tuple-element.180.refs_0_, bf16[40,1920]{1,0:T(8,128)(2,1)S(1)} %collective-permute-done.27.refs_1_, ...), custom_call_target="tpu_custom_call" | custom-call | flops 1000000000 | bytes 3000000 | tf_op jit(solution)/shard_map/combine/pallas_call | solution.py:325
  (67 shorter events, 25.7 us)
Async XLA Ops:
  0.6 21.2 %collective-permute-start.1 = (bf16[3584,256]{1,0:T(8,128)(2,1)}, bf16[3584,256]{1,0:T(8,128)(2,1)S(1)}, u32[]{:S(2)}, u32[]{:S(2)}) collective-permute-start(bf16[3584,256]{1,0:T(8,128)(2,1)} %bitcast.10), channel_id=1, source_target_pairs={{0,1},{1,0},{2,3},{3,2},{4,5},{5,4},{6,7},{7,6},{8,9},{9,8},{10,11... | collective-permute-start | bytes 5505032 | tf_op jit(solution)/shard_map/ppermute | solution.py:364
  1.1 22.1 %collective-permute-start.2 = (bf16[3584,256]{1,0:T(8,128)(2,1)}, bf16[3584,256]{1,0:T(8,128)(2,1)}, u32[]{:S(2)}, u32[]{:S(2)}) collective-permute-start(bf16[3584,256]{1,0:T(8,128)(2,1)} %bitcast.13), channel_id=1, source_target_pairs={{0,1},{1,0},{2,3},{3,2},{4,5},{5,4},{6,7},{7,6},{8,9},{9,8},{10,11... | collective-permute-start | bytes 5505032 | tf_op jit(solution)/shard_map/ppermute | solution.py:364
  1.2 22.6 %collective-permute-start.3 = (bf16[256,3584]{1,0:T(8,128)(2,1)}, bf16[256,3584]{1,0:T(8,128)(2,1)}, u32[]{:S(2)}, u32[]{:S(2)}) collective-permute-start(bf16[256,3584]{1,0:T(8,128)(2,1)} %bitcast.16), channel_id=1, source_target_pairs={{0,1},{1,0},{2,3},{3,2},{4,5},{5,4},{6,7},{7,6},{8,9},{9,8},{10,11... | collective-permute-start | bytes 5505032 | tf_op jit(solution)/shard_map/ppermute | solution.py:364
  6.9 10.1 %collective-permute-start = (bf16[40,3584]{1,0:T(8,128)(2,1)S(1)}, bf16[40,3584]{1,0:T(8,128)(2,1)S(1)}, u32[]{:S(2)}, u32[]{:S(2)}) collective-permute-start(bf16[40,3584]{1,0:T(8,128)(2,1)S(1)} %get-tuple-element.102), channel_id=1, source_target_pairs={{0,4},{1,5},{2,6},{3,7},{4,0},{5,1},{6,2},{7,3},{8,12},{9,13},{10,... | collective-permute-start | bytes 860168 | tf_op jit(solution)/shard_map/ppermute | solution.py:364
  9.6 14.3 %collective-permute-start.5 = (bf16[40,3584]{1,0:T(8,128)(2,1)S(1)}, bf16[40,3584]{1,0:T(8,128)(2,1)S(1)}, u32[]{:S(2)}, u32[]{:S(2)}) collective-permute-start(bf16[40,3584]{1,0:T(8,128)(2,1)S(1)} %get-tuple-element.105), channel_id=1, source_target_pairs={{0,24},{1,25},{2,26},{3,27},{4,28},{5,29},{6,30},{7,31},{8,16},{9,... | collective-permute-start | bytes 860168 | tf_op jit(solution)/shard_map/ppermute | solution.py:364
  17.0 12.5 %collective-permute-start.6 = (bf16[40,3584]{1,0:T(8,128)(2,1)S(1)}, bf16[40,3584]{1,0:T(8,128)(2,1)S(1)}, u32[]{:S(2)}, u32[]{:S(2)}) collective-permute-start(bf16[40,3584]{1,0:T(8,128)(2,1)S(1)} %get-tuple-element.106), channel_id=1, source_target_pairs={{0,28},{1,29},{2,30},{3,31},{4,24},{5,25},{6,26},{7,27},{8,20},{9,... | collective-permute-start | bytes 860168 | tf_op jit(solution)/shard_map/ppermute | solution.py:364
  23.3 12.8 %collective-permute-start.8 = (bf16[40,3584]{1,0:T(8,128)(2,1)S(1)}, bf16[40,3584]{1,0:T(8,128)(2,1)S(1)}, u32[]{:S(2)}, u32[]{:S(2)}) collective-permute-start(bf16[40,3584]{1,0:T(8,128)(2,1)S(1)} %collective-permute-done.refs_5_), channel_id=1, source_target_pairs={{0,2},{1,3},{2,0},{3,1},{4,6},{5,7},{6,4},{7,5},{8,10},{9,11},{10,... | collective-permute-start | bytes 860168 | tf_op jit(solution)/shard_map/ppermute | solution.py:364
  23.8 12.2 %collective-permute-start.4 = (bf16[40,3584]{1,0:T(8,128)(2,1)S(1)}, bf16[40,3584]{1,0:T(8,128)(2,1)S(1)}, u32[]{:S(2)}, u32[]{:S(2)}) collective-permute-start(bf16[40,3584]{1,0:T(8,128)(2,1)S(1)} %get-tuple-element.104), channel_id=1, source_target_pairs={{0,8},{1,9},{2,10},{3,11},{4,12},{5,13},{6,14},{7,15},{8,0},{9,1},... | collective-permute-start | bytes 860168 | tf_op jit(solution)/shard_map/ppermute | solution.py:364
  37.5 15.2 %collective-permute-start.10 = (bf16[40,3584]{1,0:T(8,128)(2,1)S(1)}, bf16[40,3584]{1,0:T(8,128)(2,1)S(1)}, u32[]{:S(2)}, u32[]{:S(2)}) collective-permute-start(bf16[40,3584]{1,0:T(8,128)(2,1)S(1)} %get-tuple-element.119), channel_id=1, source_target_pairs={{0,12},{1,13},{2,14},{3,15},{4,8},{5,9},{6,10},{7,11},{8,4},{9,5},... | collective-permute-start | bytes 860168 | tf_op jit(solution)/shard_map/ppermute | solution.py:364
  40.9 11.8 %collective-permute-start.13 = (bf16[40,3584]{1,0:T(8,128)(2,1)S(1)}, bf16[40,3584]{1,0:T(8,128)(2,1)S(1)}, u32[]{:S(2)}, u32[]{:S(2)}) collective-permute-start(bf16[40,3584]{1,0:T(8,128)(2,1)S(1)} %collective-permute-done.5.refs_0_), channel_id=1, source_target_pairs={{0,2},{1,3},{2,0},{3,1},{4,6},{5,7},{6,4},{7,5},{8,10},{9,11},{10,... | collective-permute-start | bytes 860168 | tf_op jit(solution)/shard_map/ppermute | solution.py:364
  41.5 23.0 %collective-permute-start.11 = (bf16[40,3584]{1,0:T(8,128)(2,1)S(1)}, bf16[40,3584]{1,0:T(8,128)(2,1)S(1)}, u32[]{:S(2)}, u32[]{:S(2)}) collective-permute-start(bf16[40,3584]{1,0:T(8,128)(2,1)S(1)} %get-tuple-element.121), channel_id=1, source_target_pairs={{0,16},{1,17},{2,18},{3,19},{4,20},{5,21},{6,22},{7,23},{8,24},{9,... | collective-permute-start | bytes 860168 | tf_op jit(solution)/shard_map/ppermute | solution.py:364
  41.5 26.5 %collective-permute-start.12 = (bf16[40,3584]{1,0:T(8,128)(2,1)S(1)}, bf16[40,3584]{1,0:T(8,128)(2,1)S(1)}, u32[]{:S(2)}, u32[]{:S(2)}) collective-permute-start(bf16[40,3584]{1,0:T(8,128)(2,1)S(1)} %get-tuple-element.122), channel_id=1, source_target_pairs={{0,20},{1,21},{2,22},{3,23},{4,16},{5,17},{6,18},{7,19},{8,28},{9,... | collective-permute-start | bytes 860168 | tf_op jit(solution)/shard_map/ppermute | solution.py:364
  52.8 15.3 %collective-permute-start.14 = (bf16[40,3584]{1,0:T(8,128)(2,1)S(1)}, bf16[40,3584]{1,0:T(8,128)(2,1)S(1)}, u32[]{:S(2)}, u32[]{:S(2)}) collective-permute-start(bf16[40,3584]{1,0:T(8,128)(2,1)S(1)} %collective-permute-done.10.refs_3_), channel_id=1, source_target_pairs={{0,2},{1,3},{2,0},{3,1},{4,6},{5,7},{6,4},{7,5},{8,10},{9,11},{10,... | collective-permute-start | bytes 860168 | tf_op jit(solution)/shard_map/ppermute | solution.py:364
  52.8 15.3 %collective-permute-start.15 = (bf16[40,3584]{1,0:T(8,128)(2,1)S(1)}, bf16[40,3584]{1,0:T(8,128)(2,1)S(1)}, u32[]{:S(2)}, u32[]{:S(2)}) collective-permute-start(bf16[40,3584]{1,0:T(8,128)(2,1)S(1)} %collective-permute-done.6.refs_1_), channel_id=1, source_target_pairs={{0,2},{1,3},{2,0},{3,1},{4,6},{5,7},{6,4},{7,5},{8,10},{9,11},{10,... | collective-permute-start | bytes 860168 | tf_op jit(solution)/shard_map/ppermute | solution.py:364
  68.0 13.8 %collective-permute-start.16 = (bf16[40,3584]{1,0:T(8,128)(2,1)S(1)}, bf16[40,3584]{1,0:T(8,128)(2,1)S(1)}, u32[]{:S(2)}, u32[]{:S(2)}) collective-permute-start(bf16[40,3584]{1,0:T(8,128)(2,1)S(1)} %collective-permute-done.11.refs_0_), channel_id=1, source_target_pairs={{0,2},{1,3},{2,0},{3,1},{4,6},{5,7},{6,4},{7,5},{8,10},{9,11},{10,... | collective-permute-start | bytes 860168 | tf_op jit(solution)/shard_map/ppermute | solution.py:364
  69.5 12.3 %collective-permute-start.17 = (bf16[40,3584]{1,0:T(8,128)(2,1)S(1)}, bf16[40,3584]{1,0:T(8,128)(2,1)S(1)}, u32[]{:S(2)}, u32[]{:S(2)}) collective-permute-start(bf16[40,3584]{1,0:T(8,128)(2,1)S(1)} %collective-permute-done.12.refs_1_), channel_id=1, source_target_pairs={{0,2},{1,3},{2,0},{3,1},{4,6},{5,7},{6,4},{7,5},{8,10},{9,11},{10,... | collective-permute-start | bytes 860168 | tf_op jit(solution)/shard_map/ppermute | solution.py:364
  79.8 10.1 %collective-permute-start.18 = (bf16[40,3712]{1,0:T(8,128)(2,1)S(1)}, bf16[40,3712]{1,0:T(8,128)(2,1)S(1)}, u32[]{:S(2)}, u32[]{:S(2)}) collective-permute-start(bf16[40,3712]{1,0:T(8,128)(2,1)S(1)} %get-tuple-element.154), channel_id=1, source_target_pairs={{0,2},{1,3},{2,0},{3,1},{4,6},{5,7},{6,4},{7,5},{8,10},{9,11},{10,... | collective-permute-start | bytes 890888 | tf_op jit(solution)/shard_map/ppermute | solution.py:364
  81.3 14.9 %collective-permute-start.21 = (bf16[40,3712]{1,0:T(8,128)(2,1)S(1)}, bf16[40,3712]{1,0:T(8,128)(2,1)S(1)}, u32[]{:S(2)}, u32[]{:S(2)}) collective-permute-start(bf16[40,3712]{1,0:T(8,128)(2,1)S(1)} %get-tuple-element.163), channel_id=1, source_target_pairs={{0,2},{1,3},{2,0},{3,1},{4,6},{5,7},{6,4},{7,5},{8,10},{9,11},{10,... | collective-permute-start | bytes 890888 | tf_op jit(solution)/shard_map/ppermute | solution.py:364
  102.0 12.8 %collective-permute-start.23 = (bf16[240,7936]{1,0:T(8,128)(2,1)S(1)}, bf16[240,7936]{1,0:T(8,128)(2,1)S(1)}, u32[]{:S(2)}, u32[]{:S(2)}) collective-permute-start(bf16[240,7936]{1,0:T(8,128)(2,1)S(1)} %get-tuple-element.172.refs_0_), channel_id=1, source_target_pairs={{0,1},{1,0},{2,3},{3,2},{4,5},{5,4},{6,7},{7,6},{8,9},{9,8},{10,11... | collective-permute-start | bytes 11427848 | tf_op jit(solution)/shard_map/ppermute | solution.py:364
  102.0 12.7 %collective-permute-start.24 = (bf16[80,7936]{1,0:T(8,128)(2,1)S(1)}, bf16[80,7936]{1,0:T(8,128)(2,1)S(1)}, u32[]{:S(2)}, u32[]{:S(2)}) collective-permute-start(bf16[80,7936]{1,0:T(8,128)(2,1)S(1)} %get-tuple-element.173.refs_1_), channel_id=1, source_target_pairs={{0,1},{1,0},{2,3},{3,2},{4,5},{5,4},{6,7},{7,6},{8,9},{9,8},{10,11... | collective-permute-start | bytes 3809288 | tf_op jit(solution)/shard_map/ppermute | solution.py:364
  103.0 10.3 %collective-permute-start.25 = (bf16[40,1920]{1,0:T(8,128)(2,1)S(1)}, bf16[40,1920]{1,0:T(8,128)(2,1)S(1)}, u32[]{:S(2)}, u32[]{:S(2)}) collective-permute-start(bf16[40,1920]{1,0:T(8,128)(2,1)S(1)} %get-tuple-element.175), channel_id=1, source_target_pairs={{0,16},{1,17},{2,18},{3,19},{4,20},{5,21},{6,22},{7,23},{8,24},{9,... | collective-permute-start | bytes 460808 | tf_op jit(solution)/shard_map/ppermute | solution.py:364
  104.3 17.8 %collective-permute-start.28 = (bf16[40,1920]{1,0:T(8,128)(2,1)S(1)}, bf16[40,1920]{1,0:T(8,128)(2,1)S(1)}, u32[]{:S(2)}, u32[]{:S(2)}) collective-permute-start(bf16[40,1920]{1,0:T(8,128)(2,1)S(1)} %get-tuple-element.182), channel_id=1, source_target_pairs={{0,8},{1,9},{2,10},{3,11},{4,12},{5,13},{6,14},{7,15},{8,0},{9,1},... | collective-permute-start | bytes 460808 | tf_op jit(solution)/shard_map/ppermute | solution.py:364
  111.4 10.7 %collective-permute-start.29 = (bf16[40,1920]{1,0:T(8,128)(2,1)S(1)}, bf16[40,1920]{1,0:T(8,128)(2,1)S(1)}, u32[]{:S(2)}, u32[]{:S(2)}) collective-permute-start(bf16[40,1920]{1,0:T(8,128)(2,1)S(1)} %get-tuple-element.183), channel_id=1, source_target_pairs={{0,12},{1,13},{2,14},{3,15},{4,8},{5,9},{6,10},{7,11},{8,4},{9,5},... | collective-permute-start | bytes 460808 | tf_op jit(solution)/shard_map/ppermute | solution.py:364
  113.4 10.3 %collective-permute-start.30 = (bf16[40,1920]{1,0:T(8,128)(2,1)S(1)}, bf16[40,1920]{1,0:T(8,128)(2,1)S(1)}, u32[]{:S(2)}, u32[]{:S(2)}) collective-permute-start(bf16[40,1920]{1,0:T(8,128)(2,1)S(1)} %get-tuple-element.185), channel_id=1, source_target_pairs={{0,20},{1,21},{2,22},{3,23},{4,16},{5,17},{6,18},{7,19},{8,28},{9,... | collective-permute-start | bytes 460808 | tf_op jit(solution)/shard_map/ppermute | solution.py:364
  (17 other events, 223.6 us)
